TPU v7x, 128 devices: a whole 4x4x4 slice. The times are simulated.
128 devices in a mesh: lat: 8 (over x, core), lon: 16 (over y, z).
Axes of the slice: x: 4, y: 4, z: 4, core: 2. Of those that a mesh axis runs over, the one named last changes fastest.
Arguments:
- footprints: bfloat16 [65536, 1024], P(('lat', 'lon')), may hold values from 0.0019989014 to 0.099609375
- dual_weights: bfloat16 [65536, 4], P(('lat', 'lon')), may hold values from -6 to 6
- target_device: int32 [65536, 1], P(('lat', 'lon')), may hold values from 0 to 127; in each aligned block of 512 rows (0 to 511, 512 to 1023, ...) at most 8 rows name the same one
- target_block: int32 [65536], P(('lat', 'lon')), may hold values from 0 to 255
- obs_slot: int32 [65536], P(('lat', 'lon')), may hold values from 0 to 7
- diffusivity: float32 [2048, 2048], P('lat', 'lon'), may hold values from 0.02 to 0.25
Outputs:
- dual_product: float32 [65536, 4], P(('lat', 'lon'))
Inputs may be any that keep to these rules, and one draw needn't show every extreme that they name: `target_device`: among the 512 observations of one device, at most 8 name the same device, and exactly 8 do so for some device.
All inputs are finite; a program needn't handle non-finite values.
Results may differ from a plain program's by a relative error of at most 0.0006.
Values may be sent and summed in bfloat16 or wider, within the bound.
No kernel may reach another device: no remote copies, remote signals or barrier semaphores. Data moves between devices by JAX's collectives and lax.ppermute only.
A program may use at most 128 MiB of HBM per device.

v0:
```python
import jax
import jax.numpy as jnp
from jax import lax
from jax.experimental import pallas as pl
from jax.experimental.pallas import tpu as pltpu
from jax.sharding import PartitionSpec as P

SLOTS = 8
CLON = 128
PASSES = 4
RHS = 4
OBS = 512
CAP = 8
DEVICES = 128
LON = 16
ROWS = 256
CHUNKS = 8
DEPTH = ROWS // CHUNKS
TALL = DEPTH + 2 * PASSES
RUN = 9
SPAN = SLOTS * CLON
WIDE = RUN * 128
EAST = CLON + PASSES
TOTAL = DEVICES * CAP
BF = jnp.bfloat16
F32 = jnp.float32
NT = ((1,), (1,))
TN = ((0,), (0,))


def iota(shape, dim):
    return lax.broadcasted_iota(jnp.int32, shape, dim)


def pick(cond):
    return jnp.where(cond, 1.0, 0.0).astype(BF)


def mm(a, b, dims=((1,), (0,))):
    return lax.dot_general(a, b, (dims, ((), ())), preferred_element_type=F32)


def thirds(x):
    hi = x.astype(BF)
    rest = x - hi.astype(F32)
    mid = rest.astype(BF)
    return hi, mid, (rest - mid.astype(F32)).astype(BF)


def params(mib):
    return pltpu.CompilerParams(vmem_limit_bytes=mib * 1024 * 1024)


def cost(flops, size):
    return pl.CostEstimate(flops=flops, bytes_accessed=size, transcendentals=0)


def lanes(shape, dim):
    lane = iota(shape, dim)
    q, k, s = lane // 128, lane % 128 // 8, lane % 8
    return k * RUN + q, s, q, k


def rolled(x, step):
    return pltpu.roll(x, step % 128, 1)


def pack_kernel(prints_hbm, weights_hbm, target_hbm, block_hbm, slot_hbm, out, rank_out,
                prints, weights, target, block, slot, masked, meta, sems):
    pairs = ((target_hbm, target), (weights_hbm, weights), (block_hbm, block), (slot_hbm, slot), (prints_hbm, prints))
    copies = [pltpu.make_async_copy(a, b, sems.at[i]) for i, (a, b) in enumerate(pairs)]
    for copy in copies:
        copy.start()
    for copy in copies[:4]:
        copy.wait()
    t = target[...]
    hit = pick(iota((DEVICES, OBS), 0) == t)
    before = pick(iota((OBS, OBS), 0) < iota((OBS, OBS), 1))
    earlier = mm(hit, before)
    rank = jnp.sum(hit.astype(F32) * earlier, axis=0, keepdims=True)
    rank_out[...] = jnp.broadcast_to(rank, (8, OBS))
    place = t * CAP + rank.astype(jnp.int32)
    blk = block[...]
    meta[...] = jnp.zeros_like(meta)
    meta[0:RHS, :] = weights[...].astype(F32)
    meta[4:5, :] = ((blk % DEPTH) * CHUNKS + blk // DEPTH).astype(F32)
    meta[5:6, :] = slot[...].astype(F32)
    facts = meta[...].astype(BF)
    slots = mm(facts, pick(iota((8, 128), 0) == 5), TN).astype(BF)
    where = pick(iota((TOTAL, OBS), 0) == place)
    copies[4].wait()
    for s in range(SLOTS):
        live = slots >= jnp.asarray(s, BF)
        piece = prints[:, s * CLON:(s + 1) * CLON]
        masked[:, s * CLON:(s + 1) * CLON] = jnp.where(live, piece, jnp.zeros_like(piece))
    e, s, q, k = lanes((1, WIDE), 1)
    base = s * CLON + e
    source = jnp.where(e < PASSES, base + CLON - PASSES, jnp.where(e < EAST, base - PASSES, base - EAST))
    source = jnp.where(e < EAST + PASSES, source, -1)
    spread = pick(iota((SPAN, WIDE), 0) == source)
    fact = jnp.where((k == 15) & (q >= 1) & (q <= 3) & (s < 5), s, -1)
    wide = mm(masked[...], spread) + mm(facts, pick(iota((8, WIDE), 0) == fact), TN)
    moved = mm(where, wide.astype(BF)).reshape(DEVICES // LON, LON * CAP, WIDE)
    up = jnp.concatenate([moved[:, -CAP:], moved[:, :-CAP]], axis=1)
    down = jnp.concatenate([moved[:, CAP:], moved[:, :CAP]], axis=1)
    e, s, q, k = lanes((1, 1, WIDE), 2)
    from_west = (e < PASSES) | ((k == 15) & (q == 2))
    from_east = ((e >= EAST) & (e < EAST + PASSES)) | ((k == 15) & (q == 3))
    out[...] = jnp.where(from_west, up, jnp.where(from_east, down, moved)).reshape(TOTAL, WIDE).astype(BF)


def pack(prints, weights, target, block, slot):
    return pl.pallas_call(
        pack_kernel,
        in_specs=[pl.BlockSpec(memory_space=pltpu.HBM)] * 5,
        out_shape=(
            jax.ShapeDtypeStruct((TOTAL, WIDE), BF),
            jax.ShapeDtypeStruct((8, OBS), F32),
        ),
        scratch_shapes=[
            pltpu.VMEM((OBS, SPAN), BF),
            pltpu.VMEM((RHS, OBS), BF),
            pltpu.VMEM((1, OBS), jnp.int32),
            pltpu.VMEM((1, OBS), jnp.int32),
            pltpu.VMEM((1, OBS), jnp.int32),
            pltpu.VMEM((OBS, SPAN), BF),
            pltpu.VMEM((8, OBS), F32),
            pltpu.SemaphoreType.DMA((5,)),
        ],
        compiler_params=params(32),
        cost_estimate=cost(2 * TOTAL * OBS * SPAN, 3 << 20),
        name="pack",
    )(prints, weights, target, block, slot)


def faces_kernel(own, top, bottom, left, right, out, tall, wide):
    tall[0:4, :] = top[...]
    tall[4:4 + ROWS, :] = own[...]
    tall[4 + ROWS:8 + ROWS, :] = bottom[...]
    e, _, _, _ = lanes((1, WIDE), 1)

    def place(x, first, count):
        one = jnp.where((iota((count, WIDE), 0) == e - first) & (e >= first) & (e < first + count), 1.0, 0.0)
        return jnp.dot(x, one, precision=lax.Precision.HIGHEST, preferred_element_type=F32)

    flat = place(tall[...], PASSES, CLON) + (place(left[...], 0, PASSES) + place(right[...], EAST, PASSES))
    for q in range(RUN):
        wide[q] = flat[:, q * 128:(q + 1) * 128]

    def level(e):
        return [wide[q, pl.ds(e, CHUNKS, stride=DEPTH), :] for q in range(RUN)]

    none = [jnp.zeros((CHUNKS, 128), F32)] * RUN
    here, south = level(0), none
    for e in range(TALL):
        after = level(e + 1) if e + 1 < TALL else none
        north = [jnp.sqrt(x * y) for x, y in zip(here, after)]
        ahead = here[1:] + [rolled(here[0], -SLOTS)]
        east = [jnp.sqrt(x * y) for x, y in zip(here, ahead)]
        west = [rolled(east[-1], SLOTS)] + east[:-1]
        rows = slice(e * CHUNKS, (e + 1) * CHUNKS)
        for q in range(RUN):
            cols = slice(q * 128, (q + 1) * 128)
            out[0, rows, cols] = 1.0 - ((north[q] + south[q]) + (east[q] + west[q]))
            out[1, rows, cols] = north[q]
            out[2, rows, cols] = east[q]
        here, south = after, north


def faces(own, top, bottom, left, right):
    return pl.pallas_call(
        faces_kernel,
        out_shape=jax.ShapeDtypeStruct((3, TALL * CHUNKS, WIDE), F32),
        scratch_shapes=[pltpu.VMEM((ROWS + 8, CLON), F32), pltpu.VMEM((RUN, ROWS + 8, 128), F32)],
        compiler_params=params(20),
        cost_estimate=cost(1 << 30, 6 << 20),
        name="faces",
    )(own, top, bottom, left, right)


def adjoint_kernel(got, coef, field, low, high, facts_out, own, west, east):
    column, fact = iota((16, 128), 0), iota((16, 128), 1) - 120
    facts = mm(pick((fact == column) & (column < 5)), got[:, 128:256], NT)
    facts = facts + mm(pick((fact == column - 5) & (column >= 5) & (column < 10)), got[:, 256:384], NT)
    facts = facts + mm(pick((fact == column - 10) & (column >= 10) & (column < 15)), got[:, 384:512], NT)
    facts_out[...] = facts
    for q in range(RUN):
        piece = got[:, q * 128:(q + 1) * 128]
        e = (iota((1, 128), 1) // 8) * RUN + q
        ones = lambda cond: jnp.broadcast_to(pick(cond), piece.shape)
        own[:, q * 128:(q + 1) * 128] = piece * ones((e >= PASSES) & (e < EAST))
        if q < PASSES:
            west[:, q * 128:(q + 1) * 128] = piece * ones(e < PASSES)
        if q in EASTERN:
            at = EASTERN.index(q) * 128
            east[:, at:at + 128] = piece * ones((e >= EAST) & (e < EAST + PASSES))
    row = iota((ROWS, TOTAL), 0).astype(F32)

    def spread(first, r):
        return jnp.where(row == facts[first + RHS:first + RHS + 1], facts[first + r:first + r + 1], 0.0).astype(BF)

    for r in range(RHS):
        field[r] = mm(spread(0, r), own[...])
        field[r, :, :PASSES * 128] += mm(spread(5, r), west[...])
        more = mm(spread(10, r), east[...])
        for at, q in enumerate(EASTERN):
            field[r, :, q * 128:(q + 1) * 128] += more[:, at * 128:(at + 1) * 128]
        for e in range(PASSES):
            low[r, e:e + 1, :] = field[r, e * CHUNKS:e * CHUNKS + 1, :]
            last = (DEPTH - PASSES + e + 1) * CHUNKS - 1
            high[r, e:e + 1, :] = field[r, last:last + 1, :]


EASTERN = [(EAST + i) % RUN for i in range(PASSES)]


def adjoint(got, coef):
    return pl.pallas_call(
        adjoint_kernel,
        in_specs=[pl.BlockSpec(memory_space=pltpu.VMEM), pl.BlockSpec(memory_space=pl.ANY)],
        out_shape=(
            jax.ShapeDtypeStruct((RHS, ROWS, WIDE), F32),
            jax.ShapeDtypeStruct((RHS, PASSES, WIDE), F32),
            jax.ShapeDtypeStruct((RHS, PASSES, WIDE), F32),
            jax.ShapeDtypeStruct((16, TOTAL), F32),
        ),
        scratch_shapes=[
            pltpu.VMEM((TOTAL, WIDE), BF),
            pltpu.VMEM((TOTAL, PASSES * 128), BF),
            pltpu.VMEM((TOTAL, PASSES * 128), BF),
        ],
        compiler_params=params(28),
        cost_estimate=cost(5 << 30, 8 << 20),
        name="adjoint",
    )(got, coef)


def project_kernel(field, south, north, coef, got, facts, out, ends, one, two, smooth, values):
    side = 6 * CHUNKS
    sub = iota((CHUNKS, 1), 0)
    for r in range(RHS):
        for e in range(PASSES):
            rows = slice((DEPTH - PASSES + e) * CHUNKS, (DEPTH - PASSES + e + 1) * CHUNKS)
            turned = pltpu.roll(field[r, rows, :], 1, 0)
            ends[r, e * CHUNKS:(e + 1) * CHUNKS, :] = jnp.where(sub == 0, south[r, e:e + 1, :], turned)
            turned = pltpu.roll(field[r, e * CHUNKS:(e + 1) * CHUNKS, :], CHUNKS - 1, 0)
            at = side + (2 + e) * CHUNKS
            ends[r, at:at + CHUNKS, :] = jnp.where(sub == CHUNKS - 1, north[r, e:e + 1, :], turned)
        ends[r, PASSES * CHUNKS:side, :] = field[r, :2 * CHUNKS, :]
        ends[r, side:side + 2 * CHUNKS, :] = field[r, (DEPTH - 2) * CHUNKS:, :]

    def rows_of(e):
        at = e * CHUNKS
        return pl.ds(at if isinstance(at, int) else pl.multiple_of(at, CHUNKS), CHUNKS)

    def level(ref, base, e, store):
        def load(r, at, q):
            return ref[r, rows_of(at + base), q * 128:(q + 1) * 128]

        def face(kind, at, q):
            return coef[kind, rows_of(at), q * 128:(q + 1) * 128]

        for r in range(RHS):
            here = [load(r, e, q) for q in range(RUN)]
            ahead = here[1:] + [rolled(here[0], -SLOTS)]
            behind = [rolled(here[-1], SLOTS)] + here[:-1]
            east = [face(2, e, q) for q in range(RUN)]
            west = [rolled(east[-1], SLOTS)] + east[:-1]
            for q in range(RUN):
                near = face(1, e, q) * load(r, e + 1, q) + face(1, e - 1, q) * load(r, e - 1, q)
                near = near + (east[q] * ahead[q] + west[q] * behind[q])
                store(r, q, face(0, e, q) * here[q] + near)

    def sweep(ref, base, target, first, last):
        def step(e, _):
            def store(r, q, value):
                target[r, rows_of(e), q * 128:(q + 1) * 128] = value

            level(ref, base, e, store)
            return 0

        lax.fori_loop(first, last, step, 0)

    sweep(ends, 0, one, 1, 5)
    sweep(field, -PASSES, one, 5, TALL - 5)
    sweep(ends, -28, one, TALL - 5, TALL - 1)
    sweep(one, 0, two, 2, TALL - 2)
    sweep(two, 0, one, 3, TALL - 3)

    keep = []
    for q in range(RUN):
        e = (iota((1, 128), 1) // 8) * RUN + q
        keep.append((e >= PASSES) & (e < EAST))

    def final(pair, _):
        e = PASSES + 2 * pair
        first = {}
        level(one, 0, e, lambda r, q, value: first.__setitem__((r, q), value))

        def store(r, q, value):
            both = jnp.concatenate([first[r, q], value], axis=0)
            at = pl.ds(pl.multiple_of(pair * 2 * CHUNKS, 2 * CHUNKS), 2 * CHUNKS)
            smooth[r, at, q * 128:(q + 1) * 128] = jnp.where(keep[q], both, 0.0).astype(BF)

        level(one, 0, e + 1, store)
        return 0

    lax.fori_loop(0, DEPTH // 2, final, 0)
    chosen = iota((ROWS, TOTAL), 0).astype(F32) == facts[RHS:RHS + 1, :]
    for r in range(RHS):
        shares = mm(smooth[r], got[...], NT)
        values[r:r + 1, :] = jnp.sum(jnp.where(chosen, shares, 0.0), axis=0, keepdims=True)
    total = jnp.zeros((DEVICES, 128), F32)
    mine = iota((128, TOTAL), 1) % CAP == iota((128, TOTAL), 0) // RHS
    owner = pick(iota((DEVICES, TOTAL), 1) // CAP == iota((DEVICES, TOTAL), 0))
    fan = pick(iota((128, RHS), 0) % RHS == iota((128, RHS), 1))
    for part in thirds(values[0:RHS, :]):
        many = jnp.where(mine, mm(fan, part), 0.0).astype(BF)
        total = total + mm(owner, many, NT)
    out[...] = total


def project(field, south, north, coef, got, facts):
    return pl.pallas_call(
        project_kernel,
        out_shape=jax.ShapeDtypeStruct((DEVICES, 128), F32),
        scratch_shapes=[
            pltpu.VMEM((RHS, 12 * CHUNKS, WIDE), F32),
            pltpu.VMEM((RHS, TALL * CHUNKS, WIDE), F32),
            pltpu.VMEM((RHS, TALL * CHUNKS, WIDE), F32),
            pltpu.VMEM((RHS, ROWS, WIDE), BF),
            pltpu.VMEM((8, TOTAL), F32),
        ],
        compiler_params=params(32),
        cost_estimate=cost(5 << 30, 10 << 20),
        name="project",
    )(field, south, north, coef, got, facts)


def unpack_kernel(values, target, rank, out):
    hit = pick(iota((DEVICES, OBS), 0) == target[...])
    total = jnp.zeros((CAP * RHS, OBS), F32)
    for part in thirds(values[:, :CAP * RHS]):
        total = total + mm(part, hit, TN)
    total = jnp.where((iota((CAP * RHS, OBS), 0) // RHS).astype(F32) == rank[0:1, :], total, 0.0)
    pair = (total[0:8] + total[8:16]) + (total[16:24] + total[24:32])
    out[...] = pair[0:RHS] + pair[RHS:]


def unpack(values, target, rank):
    return pl.pallas_call(
        unpack_kernel,
        out_shape=jax.ShapeDtypeStruct((RHS, OBS), F32),
        compiler_params=params(16),
        name="unpack",
    )(values, target, rank)


def shift(x, axis, step, closed):
    count = lax.axis_size(axis)
    pairs = [(i, (i + step) % count) for i in range(count) if closed or 0 <= i + step < count]
    return lax.ppermute(x, axis, pairs)


def body(footprints, dual_weights, target_device, target_block, obs_slot, diffusivity):
    target = target_device.reshape(1, OBS)
    packed, rank = pack(footprints, dual_weights.T, target, target_block.reshape(1, OBS), obs_slot.reshape(1, OBS))
    top = shift(diffusivity[ROWS - PASSES:], "lat", 1, False)
    bottom = shift(diffusivity[:PASSES], "lat", -1, False)
    tall = jnp.concatenate([top, diffusivity, bottom], axis=0)
    left = shift(tall[:, CLON - PASSES:], "lon", 1, True)
    right = shift(tall[:, :PASSES], "lon", -1, True)
    coef = faces(diffusivity, top, bottom, left, right)
    got = lax.all_to_all(packed, ("lat", "lon"), split_axis=0, concat_axis=0, tiled=True)
    field, low, high, facts = adjoint(got, coef)
    south = shift(high, "lat", 1, False)
    north = shift(low, "lat", -1, False)
    values = project(field, south, north, coef, got, facts)
    returned = lax.all_to_all(values, ("lat", "lon"), split_axis=0, concat_axis=0, tiled=True)
    return unpack(returned, target, rank).T


def solution(mesh):
    placed = (
        P(("lat", "lon"), None),
        P(("lat", "lon"), None),
        P(("lat", "lon"), None),
        P(("lat", "lon")),
        P(("lat", "lon")),
        P("lat", "lon"),
    )
    return jax.shard_map(
        body, mesh=mesh, in_specs=placed, out_specs=P(("lat", "lon"), None), check_vma=False
    )
```

profile of v0, /device:TPU:1, one launch (start us, length us, event | category | flops | bytes accessed | tf_op | source)
XLA Modules:
  0.0 115.5 jit_solution(14858788985309041644)
XLA Ops:
  0.0 0.7 copy-done.5
  0.7 1.2 %copy-done.7 = bf16[512,1024]{1,0:T(8,128)(2,1)S(1)} copy-done((bf16[512,1024]{1,0:T(8,128)(2,1)S(1)}, bf16[512,1024]{1,0:T(8,128)(2,1)}, u32[]{:S(2)}) %copy-start.7) | copy-done | bytes 1048600
  1.9 0.7 copy-done.8
  2.6 0.7 copy-done.9
  3.3 0.7 copy-done.10
  4.0 3.8 %pack.1 = (bf16[1024,1152]{1,0:T(8,128)(2,1)S(1)}, f32[8,512]{1,0:T(8,128)S(1)}) custom-call(bf16[512,1024]{1,0:T(8,128)(2,1)S(1)} %copy-done.7, bf16[4,512]{1,0:T(4,128)(2,1)S(1)} %bitcast.18, s32[1,512]{1,0:T(1,128)S(1)} %bitcast.16, s32[1,512]{1,0:T(1,128)S(1)} %bitcast.19, s32[1,512]{1,0:T(1,128)S(1)} %bitcast.20), custom_call_target="tpu_custom_call" | custom-call | flops 1073741824 | bytes 3145728 | tf_op jit(solution)/shard_map/pack/pallas_call | solution.py:113
  7.9 1.4 %copy-done.3 = bf16[1024,1152]{1,0:T(8,128)(2,1)} copy-done((bf16[1024,1152]{1,0:T(8,128)(2,1)}, bf16[1024,1152]{1,0:T(8,128)(2,1)S(1)}, u32[]{:S(2)}) %copy-start.3) | copy-done | bytes 2359320
  9.3 11.5 %all-to-all-start = ((bf16[128,8,1152]{2,1,0:T(8,128)(2,1)}), bf16[128,8,1152]{2,1,0:T(8,128)(2,1)S(1)}, u32[]{:S(2)}, u32[]{:S(2)}) async-start(bf16[128,8,1152]{2,1,0:T(8,128)(2,1)} %bitcast.13), calls=%async_computation | async-start | bytes 4718592 | tf_op jit(solution)/shard_map/all_to_all | solution.py:374
  20.8 3.0 %collective-permute-start.1 = (f32[4,128]{1,0:T(4,128)S(1)}, f32[4,128]{1,0:T(4,128)S(1)}, u32[]{:S(2)}, u32[]{:S(2)}) collective-permute-start(f32[4,128]{1,0:T(4,128)S(1)} %get-tuple-element.19), channel_id=1, source_target_pairs={{16,0},{32,16},{48,32},{64,48},{80,64},{96,80},{112,96},{17,1},{33... | collective-permute-start | bytes 6152 | tf_op jit(solution)/shard_map/ppermute | solution.py:362
  23.8 2.6 %collective-permute-start = (f32[4,128]{1,0:T(4,128)S(1)}, f32[4,128]{1,0:T(4,128)S(1)}, u32[]{:S(2)}, u32[]{:S(2)}) collective-permute-start(f32[4,128]{1,0:T(4,128)S(1)} %get-tuple-element.20), channel_id=1, source_target_pairs={{0,16},{16,32},{32,48},{48,64},{64,80},{80,96},{96,112},{1,17},{17... | collective-permute-start | bytes 6152 | tf_op jit(solution)/shard_map/ppermute | solution.py:362
  26.4 21.7 %collective-permute-done.1.bottom = f32[4,128]{1,0:T(4,128)S(1)} collective-permute-done((f32[4,128]{1,0:T(4,128)S(1)}, f32[4,128]{1,0:T(4,128)S(1)}, u32[]{:S(2)}, u32[]{:S(2)}) %collective-permute-start.1) | collective-permute-done | bytes 2080 | tf_op jit(solution)/shard_map/ppermute | solution.py:362
  48.2 5.5 %collective-permute-start.3 = (f32[264,4]{1,0:T(8,128)S(1)}, f32[264,4]{1,0:T(8,128)S(1)}, u32[]{:S(2)}, u32[]{:S(2)}) collective-permute-start(f32[264,4]{1,0:T(8,128)S(1)} %get-tuple-element.17), channel_id=1, source_target_pairs={{0,15},{1,0},{2,1},{3,2},{4,3},{5,4},{6,5},{7,6},{8,7},{9,8},{10,9... | collective-permute-start | bytes 12680 | tf_op jit(solution)/shard_map/ppermute | solution.py:362
  53.6 2.0 %collective-permute-done.3.right = f32[264,4]{1,0:T(8,128)S(1)} collective-permute-done((f32[264,4]{1,0:T(8,128)S(1)}, f32[264,4]{1,0:T(8,128)S(1)}, u32[]{:S(2)}, u32[]{:S(2)}) %collective-permute-start.3) | collective-permute-done | bytes 4256 | tf_op jit(solution)/shard_map/ppermute | solution.py:362
  55.6 5.2 %collective-permute-done.2.left = f32[264,4]{1,0:T(8,128)S(1)} collective-permute-done((f32[264,4]{1,0:T(8,128)S(1)}, f32[264,4]{1,0:T(8,128)S(1)}, u32[]{:S(2)}, u32[]{:S(2)}) %collective-permute-start.2) | collective-permute-done | bytes 4256 | tf_op jit(solution)/shard_map/ppermute | solution.py:362
  60.8 4.9 %faces.1.coef = f32[3,320,1152]{2,1,0:T(8,128)S(1)} custom-call(f32[256,128]{1,0:T(8,128)S(1)} %copy-done.4, f32[4,128]{1,0:T(4,128)S(1)} %collective-permute-done.top, f32[4,128]{1,0:T(4,128)S(1)} %collective-permute-done.1.bottom, f32[264,4]{1,0:T(8,128)S(1)} %collective-permute-done.2.left, f32[264,4]{1,0:T(8,128)S(1)} %collective-permute-done.3.right), custom_call_target="tpu_custom_call" | custom-call | flops 1073741824 | bytes 6291456 | tf_op jit(solution)/shard_map/faces/pallas_call | solution.py:171
  65.7 2.0 %copy-done = f32[3,320,1152]{2,1,0:T(8,128)} copy-done((f32[3,320,1152]{2,1,0:T(8,128)}, f32[3,320,1152]{2,1,0:T(8,128)S(1)}, u32[]{:S(2)}) %copy-start) | copy-done | bytes 4423704
  67.8 2.3 %copy-done.1 = f32[3,320,1152]{2,1,0:T(8,128)S(1)} copy-done((f32[3,320,1152]{2,1,0:T(8,128)S(1)}, f32[3,320,1152]{2,1,0:T(8,128)}, u32[]{:S(2)}) %copy-start.1) | copy-done | bytes 4423704
  70.0 5.4 %adjoint.1 = (f32[4,256,1152]{2,1,0:T(8,128)S(1)}, f32[4,4,1152]{2,1,0:T(4,128)S(1)}, f32[4,4,1152]{2,1,0:T(4,128)S(1)}, f32[16,1024]{1,0:T(8,128)S(1)}) custom-call(bf16[1024,1152]{1,0:T(8,128)(2,1)S(1)} %bitcast.11, f32[3,320,1152]{2,1,0:T(8,128)S(1)} %copy-done.1), custom_call_target="tpu_custom_call" | custom-call | flops 5368709120 | bytes 8388608 | tf_op jit(solution)/shard_map/adjoint/pallas_call | solution.py:218
  75.5 4.3 %collective-permute-start.4 = (f32[4,4,1152]{2,1,0:T(4,128)S(1)}, f32[4,4,1152]{2,1,0:T(4,128)S(1)}, u32[]{:S(2)}, u32[]{:S(2)}) collective-permute-start(f32[4,4,1152]{2,1,0:T(4,128)S(1)} %get-tuple-element.13), channel_id=1, source_target_pairs={{0,16},{16,32},{32,48},{48,64},{64,80},{80,96},{96,112},{1,17},{17... | collective-permute-start | bytes 221192 | tf_op jit(solution)/shard_map/ppermute | solution.py:362
  79.8 2.1 %collective-permute-start.5 = (f32[4,4,1152]{2,1,0:T(4,128)S(1)}, f32[4,4,1152]{2,1,0:T(4,128)S(1)}, u32[]{:S(2)}, u32[]{:S(2)}) collective-permute-start(f32[4,4,1152]{2,1,0:T(4,128)S(1)} %get-tuple-element.14), channel_id=1, source_target_pairs={{16,0},{32,16},{48,32},{64,48},{80,64},{96,80},{112,96},{17,1},{33... | collective-permute-start | bytes 221192 | tf_op jit(solution)/shard_map/ppermute | solution.py:362
  82.0 3.5 %collective-permute-done.5.north = f32[4,4,1152]{2,1,0:T(4,128)S(1)} collective-permute-done((f32[4,4,1152]{2,1,0:T(4,128)S(1)}, f32[4,4,1152]{2,1,0:T(4,128)S(1)}, u32[]{:S(2)}, u32[]{:S(2)}) %collective-permute-start.5) | collective-permute-done | bytes 73760 | tf_op jit(solution)/shard_map/ppermute | solution.py:362
  85.5 16.6 %project.1 = f32[128,128]{1,0:T(8,128)S(1)} custom-call(f32[4,256,1152]{2,1,0:T(8,128)S(1)} %get-tuple-element.12.field, f32[4,4,1152]{2,1,0:T(4,128)S(1)} %collective-permute-done.4.south, f32[4,4,1152]{2,1,0:T(4,128)S(1)} %collective-permute-done.5.north, f32[3,320,1152]{2,1,0:T(8,128)S(1)} %copy-done.2, bf16[1024,1152]{1,0:T(8,128)(2,1)S(1)} %bitcast.12, ...), custom_call_target="tpu_custom_call" | custom-call | flops 5368709120 | bytes 10485760 | tf_op jit(solution)/shard_map/project/pallas_call | solution.py:324
  102.1 12.5 %all_to_all.22 = f32[128,1,128]{2,1,0:T(1,128)S(1)} all-to-all(f32[128,1,128]{2,1,0:T(1,128)S(1)} %bitcast.15), channel_id=1, replica_groups=mesh['lat'=8,'lon'=16] {'lat','lon'}, dimensions={0} | all-to-all | bytes 131072 | tf_op jit(solution)/shard_map/all_to_all | solution.py:379
  114.7 0.8 unpack.1
  (21 shorter events, 0.1 us)
Async XLA Ops:
  0.0 20.8 %copy-start.4 = (f32[256,128]{1,0:T(8,128)S(1)}, f32[256,128]{1,0:T(8,128)}, u32[]{:S(2)}) copy-start(f32[256,128]{1,0:T(8,128)} %own.1) | copy-start | bytes 393220
  0.0 0.7 copy-start.5
  0.7 1.2 %copy-start.7 = (bf16[512,1024]{1,0:T(8,128)(2,1)S(1)}, bf16[512,1024]{1,0:T(8,128)(2,1)}, u32[]{:S(2)}) copy-start(bf16[512,1024]{1,0:T(8,128)(2,1)} %prints_hbm.1) | copy-start | bytes 3145732
  1.9 0.7 copy-start.8
  2.6 0.7 copy-start.9
  3.3 0.7 copy-start.10
  7.8 1.4 %copy-start.3 = (bf16[1024,1152]{1,0:T(8,128)(2,1)}, bf16[1024,1152]{1,0:T(8,128)(2,1)S(1)}, u32[]{:S(2)}) copy-start(bf16[1024,1152]{1,0:T(8,128)(2,1)S(1)} %get-tuple-element.11) | copy-start | bytes 7077892
  9.3 58.5 %all-to-all-start = ((bf16[128,8,1152]{2,1,0:T(8,128)(2,1)}), bf16[128,8,1152]{2,1,0:T(8,128)(2,1)S(1)}, u32[]{:S(2)}, u32[]{:S(2)}) async-start(bf16[128,8,1152]{2,1,0:T(8,128)(2,1)} %bitcast.13), calls=%async_computation | async-start | bytes 4718592 | tf_op jit(solution)/shard_map/all_to_all | solution.py:374
  20.8 27.2 %collective-permute-start.1 = (f32[4,128]{1,0:T(4,128)S(1)}, f32[4,128]{1,0:T(4,128)S(1)}, u32[]{:S(2)}, u32[]{:S(2)}) collective-permute-start(f32[4,128]{1,0:T(4,128)S(1)} %get-tuple-element.19), channel_id=1, source_target_pairs={{16,0},{32,16},{48,32},{64,48},{80,64},{96,80},{112,96},{17,1},{33... | collective-permute-start | bytes 6152 | tf_op jit(solution)/shard_map/ppermute | solution.py:362
  23.8 24.3 %collective-permute-start = (f32[4,128]{1,0:T(4,128)S(1)}, f32[4,128]{1,0:T(4,128)S(1)}, u32[]{:S(2)}, u32[]{:S(2)}) collective-permute-start(f32[4,128]{1,0:T(4,128)S(1)} %get-tuple-element.20), channel_id=1, source_target_pairs={{0,16},{16,32},{32,48},{48,64},{64,80},{80,96},{96,112},{1,17},{17... | collective-permute-start | bytes 6152 | tf_op jit(solution)/shard_map/ppermute | solution.py:362
  48.2 7.4 %collective-permute-start.3 = (f32[264,4]{1,0:T(8,128)S(1)}, f32[264,4]{1,0:T(8,128)S(1)}, u32[]{:S(2)}, u32[]{:S(2)}) collective-permute-start(f32[264,4]{1,0:T(8,128)S(1)} %get-tuple-element.17), channel_id=1, source_target_pairs={{0,15},{1,0},{2,1},{3,2},{4,3},{5,4},{6,5},{7,6},{8,7},{9,8},{10,9... | collective-permute-start | bytes 12680 | tf_op jit(solution)/shard_map/ppermute | solution.py:362
  53.6 7.2 %collective-permute-start.2 = (f32[264,4]{1,0:T(8,128)S(1)}, f32[264,4]{1,0:T(8,128)S(1)}, u32[]{:S(2)}, u32[]{:S(2)}) collective-permute-start(f32[264,4]{1,0:T(8,128)S(1)} %get-tuple-element.18), channel_id=1, source_target_pairs={{0,1},{1,2},{2,3},{3,4},{4,5},{5,6},{6,7},{7,8},{8,9},{9,10},{10,1... | collective-permute-start | bytes 12680 | tf_op jit(solution)/shard_map/ppermute | solution.py:362
  65.7 2.0 %copy-start = (f32[3,320,1152]{2,1,0:T(8,128)}, f32[3,320,1152]{2,1,0:T(8,128)S(1)}, u32[]{:S(2)}) copy-start(f32[3,320,1152]{2,1,0:T(8,128)S(1)} %faces.1.coef) | copy-start | bytes 13271044
  67.8 2.3 %copy-start.1 = (f32[3,320,1152]{2,1,0:T(8,128)S(1)}, f32[3,320,1152]{2,1,0:T(8,128)}, u32[]{:S(2)}) copy-start(f32[3,320,1152]{2,1,0:T(8,128)} %copy-done) | copy-start | bytes 13271044
  70.0 15.5 %copy-start.2 = (f32[3,320,1152]{2,1,0:T(8,128)S(1)}, f32[3,320,1152]{2,1,0:T(8,128)}, u32[]{:S(2)}) copy-start(f32[3,320,1152]{2,1,0:T(8,128)} %copy-done) | copy-start | bytes 13271044
  75.5 6.5 %collective-permute-start.4 = (f32[4,4,1152]{2,1,0:T(4,128)S(1)}, f32[4,4,1152]{2,1,0:T(4,128)S(1)}, u32[]{:S(2)}, u32[]{:S(2)}) collective-permute-start(f32[4,4,1152]{2,1,0:T(4,128)S(1)} %get-tuple-element.13), channel_id=1, source_target_pairs={{0,16},{16,32},{32,48},{48,64},{64,80},{80,96},{96,112},{1,17},{17... | collective-permute-start | bytes 221192 | tf_op jit(solution)/shard_map/ppermute | solution.py:362
  79.8 5.7 %collective-permute-start.5 = (f32[4,4,1152]{2,1,0:T(4,128)S(1)}, f32[4,4,1152]{2,1,0:T(4,128)S(1)}, u32[]{:S(2)}, u32[]{:S(2)}) collective-permute-start(f32[4,4,1152]{2,1,0:T(4,128)S(1)} %get-tuple-element.14), channel_id=1, source_target_pairs={{16,0},{32,16},{48,32},{64,48},{80,64},{96,80},{112,96},{17,1},{33... | collective-permute-start | bytes 221192 | tf_op jit(solution)/shard_map/ppermute | solution.py:362
  85.5 29.2 %copy-start.6 = (s32[512,1]{0,1:T(1,128)S(1)}, s32[512,1]{0,1:T(1,128)}, u32[]{:S(2)}) copy-start(s32[512,1]{0,1:T(1,128)} %param.8) | copy-start | bytes 6148
where the time goes:
time: 116 us; the launch traced here: 115 us
  waiting for transfers between devices  32.4 us (28%)
  Pallas kernels  31.7 us (27%)
  starting transfers between devices  29 us (25%)
  blocking collectives  12.5 us (11%)
  local copies, waits for them, and re-layouts  9.81 us (8%)
    ppermute x6, waiting for transfers between devices, shift(): return lax.ppermute(x, axis, pairs)  32.4 us
    ppermute x6, starting transfers between devices, shift(): return lax.ppermute(x, axis, pairs)  17.5 us
    pallas_call x1, Pallas kernels, project(): pl.pallas_call(project_kernel, out_shape=jax.ShapeDtypeStruct((DEVICES, 1...  16.6 us
    all_to_all x1, blocking collectives, body(): lax.all_to_all(values, ('lat', 'lon'), split_axis=0, concat_axis=0, tiled...  12.5 us
    all_to_all x1, starting transfers between devices, body(): lax.all_to_all(packed, ('lat', 'lon'), split_axis=0, concat_axis=0, tiled...  11.5 us
    unnamed x22, local copies, waits for them, and re-layouts  9.71 us
    pallas_call x1, Pallas kernels, adjoint(): pl.pallas_call(adjoint_kernel, in_specs=[pl.BlockSpec(memory_space=pltpu....  5.44 us
    pallas_call x1, Pallas kernels, faces(): pl.pallas_call(faces_kernel, out_shape=jax.ShapeDtypeStruct((3, TALL * CH...  4.91 us
  transfers between devices with their start and end apart: 7, of which 4 were waited for; matrix products, arithmetic and copies ran while one was open for 0% of the time, Pallas kernels for 4%

commit v1 on v0

v1 whole, which is shorter than its diff:
```python
import jax
import jax.numpy as jnp
from jax import lax
from jax.experimental import pallas as pl
from jax.experimental.pallas import tpu as pltpu
from jax.sharding import PartitionSpec as P

SLOTS = 8
CLON = 128
PASSES = 4
RHS = 4
OBS = 512
CAP = 8
DEVICES = 128
LON = 16
ROWS = 256
CHUNKS = 8
DEPTH = ROWS // CHUNKS
TALL = DEPTH + 2 * PASSES
RUN = 9
SPAN = SLOTS * CLON
WIDE = RUN * 128
EAST = CLON + PASSES
TOTAL = DEVICES * CAP
RIM = 2 * PASSES
OUTER = 2 * PASSES * CHUNKS
MIDDLE = ROWS - OUTER
BF = jnp.bfloat16
F32 = jnp.float32
NT = ((1,), (1,))
TN = ((0,), (0,))


def iota(shape, dim):
    return lax.broadcasted_iota(jnp.int32, shape, dim)


def pick(cond):
    return jnp.where(cond, 1.0, 0.0).astype(BF)


def mm(a, b, dims=((1,), (0,))):
    return lax.dot_general(a, b, (dims, ((), ())), preferred_element_type=F32)


def thirds(x):
    hi = x.astype(BF)
    rest = x - hi.astype(F32)
    mid = rest.astype(BF)
    return hi, mid, (rest - mid.astype(F32)).astype(BF)


def params(mib):
    return pltpu.CompilerParams(vmem_limit_bytes=mib * 1024 * 1024)


def cost(flops, size):
    return pl.CostEstimate(flops=flops, bytes_accessed=size, transcendentals=0)


def lanes(shape, dim, first=0):
    lane = iota(shape, dim) + first
    q, k, s = lane // 128, lane % 128 // 8, lane % 8
    return k * RUN + q, s, q, k


def rolled(x, step):
    return pltpu.roll(x, step % 128, 1)


def beside(row):
    return row[1:] + [rolled(row[0], -SLOTS)], [rolled(row[-1], SLOTS)] + row[:-1]


PIECES = [(at, min(256, WIDE - at)) for at in range(0, WIDE, 256)]


def pack_kernel(prints_hbm, weights_hbm, target_hbm, block_hbm, slot_hbm, out_hbm, rank_out,
                prints, weights, target, block, slot, masked, meta, out, sems, out_sems):
    pairs = ((target_hbm, target), (weights_hbm, weights), (block_hbm, block), (slot_hbm, slot), (prints_hbm, prints))
    copies = [pltpu.make_async_copy(a, b, sems.at[i]) for i, (a, b) in enumerate(pairs)]
    for copy in copies:
        copy.start()
    for copy in copies[:4]:
        copy.wait()
    t = target[...]
    hit = pick(iota((DEVICES, OBS), 0) == t)
    before = pick(iota((OBS, OBS), 0) < iota((OBS, OBS), 1))
    earlier = mm(hit, before)
    rank = jnp.sum(hit.astype(F32) * earlier, axis=0, keepdims=True)
    rank_out[...] = jnp.broadcast_to(rank, (8, OBS))
    place = t * CAP + rank.astype(jnp.int32)
    blk = block[...]
    meta[...] = jnp.zeros_like(meta)
    meta[0:RHS, :] = weights[...].astype(F32)
    meta[4:5, :] = ((blk % DEPTH) * CHUNKS + blk // DEPTH).astype(F32)
    meta[5:6, :] = slot[...].astype(F32)
    facts = meta[...].astype(BF)
    slots = mm(facts, pick(iota((8, 128), 0) == 5), TN).astype(BF)
    where = pick(iota((TOTAL, OBS), 0) == place)
    copies[4].wait()
    for s in range(SLOTS):
        live = slots >= jnp.asarray(s, BF)
        piece = prints[:, s * CLON:(s + 1) * CLON]
        masked[:, s * CLON:(s + 1) * CLON] = jnp.where(live, piece, jnp.zeros_like(piece))
    sends = []
    for i, (at, size) in enumerate(PIECES):
        e, s, q, k = lanes((1, size), 1, at)
        base = s * CLON + e
        source = jnp.where(e < PASSES, base + CLON - PASSES, jnp.where(e < EAST, base - PASSES, base - EAST))
        source = jnp.where(e < EAST + PASSES, source, -1)
        spread = pick(iota((SPAN, size), 0) == source)
        fact = jnp.where((k == 15) & (q >= 1) & (q <= 3) & (s < 5), s, -1)
        wide = mm(masked[...], spread) + mm(facts, pick(iota((8, size), 0) == fact), TN)
        moved = mm(where, wide.astype(BF)).reshape(DEVICES // LON, LON * CAP, size)
        up = jnp.concatenate([moved[:, -CAP:], moved[:, :-CAP]], axis=1)
        down = jnp.concatenate([moved[:, CAP:], moved[:, :CAP]], axis=1)
        e, s, q, k = lanes((1, 1, size), 2, at)
        from_west = (e < PASSES) | ((k == 15) & (q == 2))
        from_east = ((e >= EAST) & (e < EAST + PASSES)) | ((k == 15) & (q == 3))
        result = jnp.where(from_west, up, jnp.where(from_east, down, moved))
        out[:, at:at + size] = result.reshape(TOTAL, size).astype(BF)
        sends.append(pltpu.make_async_copy(out.at[:, at:at + size], out_hbm.at[:, at:at + size], out_sems.at[i]))
        sends[-1].start()
    for send in sends:
        send.wait()


def pack(prints, weights, target, block, slot):
    hbm = pl.BlockSpec(memory_space=pltpu.HBM)
    return pl.pallas_call(
        pack_kernel,
        in_specs=[hbm] * 5,
        out_specs=(hbm, pl.BlockSpec(memory_space=pltpu.VMEM)),
        out_shape=(
            jax.ShapeDtypeStruct((TOTAL, WIDE), BF),
            jax.ShapeDtypeStruct((8, OBS), F32),
        ),
        scratch_shapes=[
            pltpu.VMEM((OBS, SPAN), BF),
            pltpu.VMEM((RHS, OBS), BF),
            pltpu.VMEM((1, OBS), jnp.int32),
            pltpu.VMEM((1, OBS), jnp.int32),
            pltpu.VMEM((1, OBS), jnp.int32),
            pltpu.VMEM((OBS, SPAN), BF),
            pltpu.VMEM((8, OBS), F32),
            pltpu.VMEM((TOTAL, WIDE), BF),
            pltpu.SemaphoreType.DMA((5,)),
            pltpu.SemaphoreType.DMA((len(PIECES),)),
        ],
        compiler_params=params(60),
        cost_estimate=cost(2 * TOTAL * OBS * SPAN, 3 << 20),
        name="pack",
    )(prints, weights, target, block, slot)


def faces_kernel(own, left, right, out, rim, wide):
    e, _, _, _ = lanes((1, WIDE), 1)

    def place(x, first, count):
        one = jnp.where((iota((count, WIDE), 0) == e - first) & (e >= first) & (e < first + count), 1.0, 0.0)
        return jnp.dot(x, one, precision=lax.Precision.HIGHEST, preferred_element_type=F32)

    flat = place(own[...], PASSES, CLON) + (place(left[...], 0, PASSES) + place(right[...], EAST, PASSES))
    beyond = jnp.zeros((PASSES, 128), F32)
    for q in range(RUN):
        wide[q, :PASSES, :] = beyond
        wide[q, PASSES:PASSES + ROWS, :] = flat[:, q * 128:(q + 1) * 128]
        wide[q, PASSES + ROWS:, :] = beyond
    for j in range(RIM):
        rim[j, :RHS, :] = jnp.broadcast_to(flat[j:j + 1], (RHS, WIDE))
        rim[j, RHS:, :] = jnp.broadcast_to(flat[ROWS - 1 - j:ROWS - j], (RHS, WIDE))

    def level(e):
        return [wide[q, pl.ds(e, CHUNKS, stride=DEPTH), :] for q in range(RUN)]

    none = [jnp.zeros((CHUNKS, 128), F32)] * RUN
    here, south = level(0), none
    for e in range(TALL):
        after = level(e + 1) if e + 1 < TALL else none
        north = [jnp.sqrt(x * y) for x, y in zip(here, after)]
        ahead, _ = beside(here)
        east = [jnp.sqrt(x * y) for x, y in zip(here, ahead)]
        _, west = beside(east)
        rows = slice(e * CHUNKS, (e + 1) * CHUNKS)
        for q in range(RUN):
            cols = slice(q * 128, (q + 1) * 128)
            out[0, rows, cols] = 1.0 - ((north[q] + south[q]) + (east[q] + west[q]))
            out[1, rows, cols] = north[q]
            out[2, rows, cols] = east[q]
        here, south = after, north


def faces(own, left, right):
    return pl.pallas_call(
        faces_kernel,
        out_shape=(
            jax.ShapeDtypeStruct((3, TALL * CHUNKS, WIDE), F32),
            jax.ShapeDtypeStruct((RIM, 2 * RHS, WIDE), F32),
        ),
        scratch_shapes=[pltpu.VMEM((RUN, ROWS + 8, 128), F32)],
        compiler_params=params(16),
        cost_estimate=cost(1 << 30, 6 << 20),
        name="faces",
    )(own, left, right)


def adjoint_kernel(got, kappa, field, rim, low, high, facts_out, own, west, east):
    column, fact = iota((16, 128), 0), iota((16, 128), 1) - 120
    facts = mm(pick((fact == column) & (column < 5)), got[:, 128:256], NT)
    facts = facts + mm(pick((fact == column - 5) & (column >= 5) & (column < 10)), got[:, 256:384], NT)
    facts = facts + mm(pick((fact == column - 10) & (column >= 10) & (column < 15)), got[:, 384:512], NT)
    facts_out[...] = facts
    for q in range(RUN):
        piece = got[:, q * 128:(q + 1) * 128]
        e = (iota((1, 128), 1) // 8) * RUN + q
        ones = lambda cond: jnp.broadcast_to(pick(cond), piece.shape)
        own[:, q * 128:(q + 1) * 128] = piece * ones((e >= PASSES) & (e < EAST))
        if q < PASSES:
            west[:, q * 128:(q + 1) * 128] = piece * ones(e < PASSES)
        if q in EASTERN:
            at = EASTERN.index(q) * 128
            east[:, at:at + 128] = piece * ones((e >= EAST) & (e < EAST + PASSES))
    row = iota((ROWS, TOTAL), 0).astype(F32)

    def spread(first, r):
        return jnp.where(row == facts[first + RHS:first + RHS + 1], facts[first + r:first + r + 1], 0.0).astype(BF)

    for r in range(RHS):
        field[r] = mm(spread(0, r), own[...])
        field[r, :, :PASSES * 128] += mm(spread(5, r), west[...])
        more = mm(spread(10, r), east[...])
        for at, q in enumerate(EASTERN):
            field[r, :, q * 128:(q + 1) * 128] += more[:, at * 128:(at + 1) * 128]
        for j in range(RIM):
            rim[j, r:r + 1, :] = field[r, j * CHUNKS:j * CHUNKS + 1, :]
            last = (DEPTH - j) * CHUNKS - 1
            rim[j, RHS + r:RHS + r + 1, :] = field[r, last:last + 1, :]
    for j in range(PASSES):
        low[j], high[j] = rim[j, :RHS, :], rim[j, RHS:, :]
        low[PASSES + j], high[PASSES + j] = kappa[j, :RHS, :], kappa[j, RHS:, :]


EASTERN = [(EAST + i) % RUN for i in range(PASSES)]


def adjoint(got, kappa):
    return pl.pallas_call(
        adjoint_kernel,
        out_shape=(
            jax.ShapeDtypeStruct((RHS, ROWS, WIDE), F32),
            jax.ShapeDtypeStruct((RIM, 2 * RHS, WIDE), F32),
            jax.ShapeDtypeStruct((2 * PASSES, RHS, WIDE), F32),
            jax.ShapeDtypeStruct((2 * PASSES, RHS, WIDE), F32),
            jax.ShapeDtypeStruct((16, TOTAL), F32),
        ),
        scratch_shapes=[
            pltpu.VMEM((TOTAL, WIDE), BF),
            pltpu.VMEM((TOTAL, PASSES * 128), BF),
            pltpu.VMEM((TOTAL, PASSES * 128), BF),
        ],
        compiler_params=params(20),
        cost_estimate=cost(5 << 30, 8 << 20),
        name="adjoint",
    )(got, kappa)


def inside(q):
    e = (iota((1, 128), 1) // 8) * RUN + q
    return (e >= PASSES) & (e < EAST)


def diffuse_kernel(field, coef, smooth, outer, ends, one, two):
    side = 6 * CHUNKS
    for r in range(RHS):
        for e in range(PASSES):
            rows = slice((DEPTH - PASSES + e) * CHUNKS, (DEPTH - PASSES + e + 1) * CHUNKS)
            ends[r, e * CHUNKS:(e + 1) * CHUNKS, :] = pltpu.roll(field[r, rows, :], 1, 0)
            at = side + (2 + e) * CHUNKS
            ends[r, at:at + CHUNKS, :] = pltpu.roll(field[r, e * CHUNKS:(e + 1) * CHUNKS, :], CHUNKS - 1, 0)
        ends[r, PASSES * CHUNKS:side, :] = field[r, :2 * CHUNKS, :]
        ends[r, side:side + 2 * CHUNKS, :] = field[r, (DEPTH - 2) * CHUNKS:, :]

    def rows_of(e):
        at = e * CHUNKS
        return pl.ds(at if isinstance(at, int) else pl.multiple_of(at, CHUNKS), CHUNKS)

    def level(ref, base, e, store):
        def load(r, at, q):
            return ref[r, rows_of(at + base), q * 128:(q + 1) * 128]

        def face(kind, at, q):
            return coef[kind, rows_of(at), q * 128:(q + 1) * 128]

        for r in range(RHS):
            here = [load(r, e, q) for q in range(RUN)]
            ahead, behind = beside(here)
            east = [face(2, e, q) for q in range(RUN)]
            _, west = beside(east)
            for q in range(RUN):
                near = face(1, e, q) * load(r, e + 1, q) + face(1, e - 1, q) * load(r, e - 1, q)
                near = near + (east[q] * ahead[q] + west[q] * behind[q])
                store(r, q, face(0, e, q) * here[q] + near)

    def sweep(ref, base, target, first, last, to=0):
        def step(e, _):
            def store(r, q, value):
                target[r, rows_of(e + to), q * 128:(q + 1) * 128] = value

            level(ref, base, e, store)
            return 0

        lax.fori_loop(first, last, step, 0, unroll=2)

    sweep(ends, 0, one, 1, 5)
    sweep(field, -PASSES, one, 5, TALL - 5)
    sweep(ends, -28, one, TALL - 5, TALL - 1)
    sweep(one, 0, two, 2, TALL - 2)
    sweep(two, 0, one, 3, TALL - 3)
    sweep(one, 0, outer, PASSES, 2 * PASSES, -PASSES)
    sweep(one, 0, outer, DEPTH, DEPTH + PASSES, -DEPTH + PASSES)

    def final(pair, _):
        e = 2 * PASSES + 2 * pair
        first = {}
        level(one, 0, e, lambda r, q, value: first.__setitem__((r, q), value))

        def store(r, q, value):
            both = jnp.concatenate([first[r, q], value], axis=0)
            at = pl.ds(pl.multiple_of(pair * 2 * CHUNKS, 2 * CHUNKS), 2 * CHUNKS)
            smooth[r, at, q * 128:(q + 1) * 128] = jnp.where(inside(q), both, 0.0).astype(BF)

        level(one, 0, e + 1, store)
        return 0

    lax.fori_loop(0, MIDDLE // (2 * CHUNKS), final, 0)


def diffuse(field, coef):
    return pl.pallas_call(
        diffuse_kernel,
        out_shape=(
            jax.ShapeDtypeStruct((RHS, MIDDLE, WIDE), BF),
            jax.ShapeDtypeStruct((RHS, OUTER, WIDE), F32),
        ),
        scratch_shapes=[
            pltpu.VMEM((RHS, 12 * CHUNKS, WIDE), F32),
            pltpu.VMEM((RHS, TALL * CHUNKS, WIDE), F32),
            pltpu.VMEM((RHS, TALL * CHUNKS, WIDE), F32),
        ],
        compiler_params=params(24),
        cost_estimate=cost(6 << 30, 8 << 20),
        name="diffuse",
    )(field, coef)


def finish_kernel(smooth, outer, rim, kappa, south, north, got, facts, out, border, values):
    def levels(base, inner):
        rows = []
        for j in range(PASSES):
            rows.append(jnp.concatenate([south[base + PASSES - 1 - j], north[base + PASSES - 1 - j]], axis=0))
        return [[x[:, q * 128:(q + 1) * 128] for q in range(RUN)] for x in rows + [inner[j] for j in range(RIM)]]

    v, k = levels(0, rim), levels(PASSES, kappa)
    count = PASSES + RIM
    across = [[jnp.sqrt(x * y) for x, y in zip(k[j], k[j + 1])] for j in range(count - 1)]
    east = [[jnp.sqrt(x * y) for x, y in zip(k[j], beside(k[j])[0])] for j in range(count - 1)]
    west = [beside(x)[1] for x in east]
    for step in range(1, PASSES + 1):
        new = list(v)
        for j in range(step, count - step):
            ahead, behind = beside(v[j])
            new[j] = []
            for q in range(RUN):
                own = 1.0 - ((across[j][q] + across[j - 1][q]) + (east[j][q] + west[j][q]))
                near = across[j][q] * v[j + 1][q] + across[j - 1][q] * v[j - 1][q]
                new[j].append(own * v[j][q] + (near + (east[j][q] * ahead[q] + west[j][q] * behind[q])))
        v = new
    sub = iota((CHUNKS, 1), 0)
    for r in range(RHS):
        for q in range(RUN):
            cols = slice(q * 128, (q + 1) * 128)
            for pair in range(PASSES):
                both = []
                for b in (2 * pair, 2 * pair + 1):
                    here = outer[r, b * CHUNKS:(b + 1) * CHUNKS, cols]
                    if b < PASSES:
                        here = jnp.where(sub == 0, v[PASSES + b][q][r:r + 1], here)
                    else:
                        j = PASSES + 2 * PASSES - 1 - b
                        here = jnp.where(sub == CHUNKS - 1, v[j][q][RHS + r:RHS + r + 1], here)
                    both.append(here)
                both = jnp.where(inside(q), jnp.concatenate(both, axis=0), 0.0).astype(BF)
                border[r, pair * 2 * CHUNKS:(pair + 1) * 2 * CHUNKS, cols] = both

    side = PASSES * CHUNKS
    for r in range(RHS):
        total = jnp.zeros((1, TOTAL), F32)
        for part, first in ((smooth[r], side), (border[r, :side], 0), (border[r, side:], ROWS - side)):
            shares = mm(part, got[...], NT)
            chosen = (iota(shares.shape, 0) + first).astype(F32) == facts[RHS:RHS + 1, :]
            total = total + jnp.sum(jnp.where(chosen, shares, 0.0), axis=0, keepdims=True)
        values[r:r + 1, :] = total
    total = jnp.zeros((DEVICES, 128), F32)
    mine = iota((128, TOTAL), 1) % CAP == iota((128, TOTAL), 0) // RHS
    owner = pick(iota((DEVICES, TOTAL), 1) // CAP == iota((DEVICES, TOTAL), 0))
    fan = pick(iota((128, RHS), 0) % RHS == iota((128, RHS), 1))
    for part in thirds(values[0:RHS, :]):
        many = jnp.where(mine, mm(fan, part), 0.0).astype(BF)
        total = total + mm(owner, many, NT)
    out[...] = total


def finish(smooth, outer, rim, kappa, south, north, got, facts):
    return pl.pallas_call(
        finish_kernel,
        out_shape=jax.ShapeDtypeStruct((DEVICES, 128), F32),
        scratch_shapes=[
            pltpu.VMEM((RHS, OUTER, WIDE), BF),
            pltpu.VMEM((8, TOTAL), F32),
        ],
        compiler_params=params(24),
        cost_estimate=cost(3 << 30, 10 << 20),
        name="finish",
    )(smooth, outer, rim, kappa, south, north, got, facts)


def unpack_kernel(values, target, rank, out):
    hit = pick(iota((DEVICES, OBS), 0) == target[...])
    total = jnp.zeros((CAP * RHS, OBS), F32)
    for part in thirds(values[:, :CAP * RHS]):
        total = total + mm(part, hit, TN)
    total = jnp.where((iota((CAP * RHS, OBS), 0) // RHS).astype(F32) == rank[0:1, :], total, 0.0)
    pair = (total[0:8] + total[8:16]) + (total[16:24] + total[24:32])
    out[...] = pair[0:RHS] + pair[RHS:]


def unpack(values, target, rank):
    return pl.pallas_call(
        unpack_kernel,
        out_shape=jax.ShapeDtypeStruct((RHS, OBS), F32),
        compiler_params=params(16),
        name="unpack",
    )(values, target, rank)


def shift(x, axis, step, closed):
    count = lax.axis_size(axis)
    pairs = [(i, (i + step) % count) for i in range(count) if closed or 0 <= i + step < count]
    return lax.ppermute(x, axis, pairs)


def body(footprints, dual_weights, target_device, target_block, obs_slot, diffusivity):
    target = target_device.reshape(1, OBS)
    packed, rank = pack(footprints, dual_weights.T, target, target_block.reshape(1, OBS), obs_slot.reshape(1, OBS))
    left = shift(diffusivity[:, CLON - PASSES:], "lon", 1, True)
    right = shift(diffusivity[:, :PASSES], "lon", -1, True)
    packed, left, right = lax.optimization_barrier((packed, left, right))
    coef, kappa = faces(diffusivity, left, right)
    got = lax.all_to_all(packed, ("lat", "lon"), split_axis=0, concat_axis=0, tiled=True)
    field, rim, low, high, facts = adjoint(got, kappa)
    south = shift(high, "lat", 1, False)
    north = shift(low, "lat", -1, False)
    smooth, outer = diffuse(field, coef)
    values = finish(smooth, outer, rim, kappa, south, north, got, facts)
    returned = lax.all_to_all(values, ("lat", "lon"), split_axis=0, concat_axis=0, tiled=True)
    return unpack(returned, target, rank).T


def solution(mesh):
    placed = (
        P(("lat", "lon"), None),
        P(("lat", "lon"), None),
        P(("lat", "lon"), None),
        P(("lat", "lon")),
        P(("lat", "lon")),
        P("lat", "lon"),
    )
    return jax.shard_map(
        body, mesh=mesh, in_specs=placed, out_specs=P(("lat", "lon"), None), check_vma=False
    )
```

time: 116 us -> 103 us (0.89)
  waiting for transfers between devices: 32.4 us -> 25.4 us
  local copies, waits for them, and re-layouts: 9.81 us -> 3.11 us
  starting transfers between devices: 29 us -> 22.6 us
  Pallas kernels: 31.7 us -> 37.5 us
  blocking collectives: 12.5 us -> 14.3 us
    ppermute x6 -> x4, waiting for transfers between devices: 32.4 us -> 0.01 us  [shift(): return lax.ppermute(x, axis, pairs)]
    all_to_all x1, waiting for transfers between devices: 0.01 us -> 25.4 us  [body(): lax.all_to_all(packed, ('lat', 'lon'), split_axis=0, concat_axis=0, tiled...]
    unnamed x22 -> x10, local copies, waits for them, and re-layouts: 9.71 us -> 2.04 us
    pallas_call x4 -> x5, Pallas kernels: 30.8 us -> 36.6 us  [the longest x1 10.2 us: diffuse(): pl.pallas_call(diffuse_kernel, out_shape=(jax.ShapeDtypeStruct((RHS, MIDD...]
    ppermute x6 -> x4, starting transfers between devices: 17.5 us -> 13 us  [shift(): return lax.ppermute(x, axis, pairs)]
    all_to_all x1, starting transfers between devices: 11.5 us -> 9.63 us  [body(): lax.all_to_all(packed, ('lat', 'lon'), split_axis=0, concat_axis=0, tiled...]
    all_to_all x1, blocking collectives: 12.5 us -> 14.3 us  [body(): lax.all_to_all(values, ('lat', 'lon'), split_axis=0, concat_axis=0, tiled...]
  transfers between devices with their start and end apart: 7 -> 5, of which waited for: 4 -> 1; matrix products, arithmetic and copies ran while one was open for 0% -> 0% of each run, Pallas kernels for 4% -> 22%
where the time goes in v1:
time: 103 us
  Pallas kernels  37.5 us (36%)
  waiting for transfers between devices  25.4 us (25%)
  starting transfers between devices  22.6 us (22%)
  blocking collectives  14.3 us (14%)
  local copies, waits for them, and re-layouts  3.11 us (3%)
    all_to_all x1, waiting for transfers between devices, body(): lax.all_to_all(packed, ('lat', 'lon'), split_axis=0, concat_axis=0, tiled...  25.4 us
    all_to_all x1, blocking collectives, body(): lax.all_to_all(values, ('lat', 'lon'), split_axis=0, concat_axis=0, tiled...  14.3 us
    ppermute x4, starting transfers between devices, shift(): return lax.ppermute(x, axis, pairs)  13 us
    pallas_call x1, Pallas kernels, diffuse(): pl.pallas_call(diffuse_kernel, out_shape=(jax.ShapeDtypeStruct((RHS, MIDD...  10.2 us
    all_to_all x1, starting transfers between devices, body(): lax.all_to_all(packed, ('lat', 'lon'), split_axis=0, concat_axis=0, tiled...  9.63 us
    pallas_call x1, Pallas kernels, finish(): pl.pallas_call(finish_kernel, out_shape=jax.ShapeDtypeStruct((DEVICES, 12...  8.89 us
    pallas_call x1, Pallas kernels, pack(): pl.pallas_call(pack_kernel, in_specs=[hbm] * 5, out_specs=(hbm, pl.BlockS...  7.38 us
    pallas_call x1, Pallas kernels, adjoint(): pl.pallas_call(adjoint_kernel, out_shape=(jax.ShapeDtypeStruct((RHS, ROWS...  5.5 us
  transfers between devices with their start and end apart: 5, of which 1 were waited for; matrix products, arithmetic and copies ran while one was open for 0% of the time, Pallas kernels for 22%

profile of v1, /device:TPU:1, one launch (start us, length us, event | category | flops | bytes accessed | tf_op | source)
XLA Modules:
  0.0 103.1 jit_solution(10860443037893766591)
XLA Ops:
  0.0 1.1 %fusion = (f32[256,4]{1,0:T(8,128)S(1)}, f32[256,4]{1,0:T(8,128)S(1)}) fusion(f32[256,128]{1,0:T(8,128)} %own.1), kind=kLoop, calls=%fused_computation | loop fusion | bytes 16384 | tf_op jit(solution)/shard_map/slice | solution.py:457
  1.1 7.1 %collective-permute-start.1 = (f32[256,4]{1,0:T(8,128)S(1)}, f32[256,4]{1,0:T(8,128)S(1)}, u32[]{:S(2)}, u32[]{:S(2)}) collective-permute-start(f32[256,4]{1,0:T(8,128)S(1)} %get-tuple-element.33), channel_id=1, source_target_pairs={{0,15},{1,0},{2,1},{3,2},{4,3},{5,4},{6,5},{7,6},{8,7},{9,8},{10,9... | collective-permute-start | bytes 12296 | tf_op jit(solution)/shard_map/ppermute | solution.py:450
  8.2 0.0 collective-permute-start
  8.2 7.4 %pack.1 = (bf16[1024,1152]{1,0:T(8,128)(2,1)}, f32[8,512]{1,0:T(8,128)}) custom-call(bf16[512,1024]{1,0:T(8,128)(2,1)} %prints_hbm.1, bf16[4,512]{1,0:T(4,128)(2,1)} %bitcast.18, s32[1,512]{1,0:T(1,128)} %bitcast.15, s32[1,512]{1,0:T(1,128)} %bitcast.19, s32[1,512]{1,0:T(1,128)} %bitcast.20), custom_call_target="tpu_custom_call" | custom-call | flops 1073741824 | bytes 3145728 | tf_op jit(solution)/shard_map/pack/pallas_call | solution.py:131
  15.6 0.0 collective-permute-done.1.right
  15.6 0.0 collective-permute-done.left
  15.6 0.0 copy-start
  15.6 9.6 %all-to-all-start = ((bf16[128,8,1152]{2,1,0:T(8,128)(2,1)}), bf16[128,8,1152]{2,1,0:T(8,128)(2,1)S(1)}, u32[]{:S(2)}, u32[]{:S(2)}) async-start(bf16[128,8,1152]{2,1,0:T(8,128)(2,1)} %bitcast.17), calls=%async_computation | async-start | bytes 4718592 | tf_op jit(solution)/shard_map/all_to_all | solution.py:460
  25.2 0.0 copy-done
  25.3 4.7 %faces.1 = (f32[3,320,1152]{2,1,0:T(8,128)S(1)}, f32[8,8,1152]{2,1,0:T(8,128)S(1)}) custom-call(f32[256,128]{1,0:T(8,128)S(1)} %copy-done, f32[256,4]{1,0:T(8,128)S(1)} %collective-permute-done.left, f32[256,4]{1,0:T(8,128)S(1)} %collective-permute-done.1.right), custom_call_target="tpu_custom_call" | custom-call | flops 1073741824 | bytes 6291456 | tf_op jit(solution)/shard_map/faces/pallas_call | solution.py:195
  29.9 0.0 copy-start.3
  29.9 2.0 %copy-done.3 = f32[3,320,1152]{2,1,0:T(8,128)} copy-done((f32[3,320,1152]{2,1,0:T(8,128)}, f32[3,320,1152]{2,1,0:T(8,128)S(1)}, u32[]{:S(2)}) %copy-start.3) | copy-done | bytes 4423704
  31.9 25.4 %all-to-all-done = bf16[128,8,1152]{2,1,0:T(8,128)(2,1)S(1)} async-done(((bf16[128,8,1152]{2,1,0:T(8,128)(2,1)}), bf16[128,8,1152]{2,1,0:T(8,128)(2,1)S(1)}, u32[]{:S(2)}, u32[]{:S(2)}) %all-to-all-start) | async-done | bytes 2359328 | tf_op jit(solution)/shard_map/all_to_all | solution.py:460
  57.4 5.5 %adjoint.1 = (f32[4,256,1152]{2,1,0:T(8,128)S(1)}, f32[8,8,1152]{2,1,0:T(8,128)S(1)}, f32[8,4,1152]{2,1,0:T(4,128)S(1)}, f32[8,4,1152]{2,1,0:T(4,128)S(1)}, f32[16,1024]{1,0:T(8,128)S(1)}) custom-call(bf16[1024,1152]{1,0:T(8,128)(2,1)S(1)} %bitcast.11, f32[8,8,1152]{2,1,0:T(8,128)S(1)} %get-tuple-element.23.kappa), custom_call_target="tpu_custom_call" | custom-call | flops 5368709120 | bytes 8388608 | tf_op jit(solution)/shard_map/adjoint/pallas_call | solution.py:248
  62.9 3.8 %collective-permute-start.2 = (f32[8,4,1152]{2,1,0:T(4,128)S(1)}, f32[8,4,1152]{2,1,0:T(4,128)S(1)}, u32[]{:S(2)}, u32[]{:S(2)}) collective-permute-start(f32[8,4,1152]{2,1,0:T(4,128)S(1)} %get-tuple-element.29), channel_id=1, source_target_pairs={{0,16},{16,32},{32,48},{48,64},{64,80},{80,96},{96,112},{1,17},{17... | collective-permute-start | bytes 442376 | tf_op jit(solution)/shard_map/ppermute | solution.py:450
  66.6 2.1 %collective-permute-start.3 = (f32[8,4,1152]{2,1,0:T(4,128)S(1)}, f32[8,4,1152]{2,1,0:T(4,128)S(1)}, u32[]{:S(2)}, u32[]{:S(2)}) collective-permute-start(f32[8,4,1152]{2,1,0:T(4,128)S(1)} %get-tuple-element.30), channel_id=1, source_target_pairs={{16,0},{32,16},{48,32},{64,48},{80,64},{96,80},{112,96},{17,1},{33... | collective-permute-start | bytes 442376 | tf_op jit(solution)/shard_map/ppermute | solution.py:450
  68.8 0.0 copy-done.4
  68.8 10.2 %diffuse.1 = (bf16[4,192,1152]{2,1,0:T(8,128)(2,1)S(1)}, f32[4,64,1152]{2,1,0:T(8,128)S(1)}) custom-call(f32[4,256,1152]{2,1,0:T(8,128)S(1)} %get-tuple-element.24.field, f32[3,320,1152]{2,1,0:T(8,128)S(1)} %copy-done.4), custom_call_target="tpu_custom_call" | custom-call | flops 6442450944 | bytes 8388608 | tf_op jit(solution)/shard_map/diffuse/pallas_call | solution.py:340
  79.0 0.0 collective-permute-done.2.south
  79.0 0.0 collective-permute-done.3.north
  79.0 0.0 copy-start.2
  79.1 8.9 %finish.1 = f32[128,128]{1,0:T(8,128)S(1)} custom-call(bf16[4,192,1152]{2,1,0:T(8,128)(2,1)S(1)} %get-tuple-element.26.smooth, f32[4,64,1152]{2,1,0:T(8,128)S(1)} %get-tuple-element.27.outer, f32[8,8,1152]{2,1,0:T(8,128)S(1)} %get-tuple-element.28.rim, f32[8,8,1152]{2,1,0:T(8,128)S(1)} %get-tuple-element.23.kappa, ...), custom_call_target="tpu_custom_call" | custom-call | flops 3221225472 | bytes 10485760 | tf_op jit(solution)/shard_map/finish/pallas_call | solution.py:415
  88.0 14.3 %all_to_all.22 = f32[128,1,128]{2,1,0:T(1,128)S(1)} all-to-all(f32[128,1,128]{2,1,0:T(1,128)S(1)} %bitcast.14), channel_id=1, replica_groups=mesh['lat'=8,'lon'=16] {'lat','lon'}, dimensions={0} | all-to-all | bytes 131072 | tf_op jit(solution)/shard_map/all_to_all | solution.py:466
  102.3 0.8 unpack.1
  (4 shorter events, 0.0 us)
Async XLA Ops:
  1.1 14.5 %collective-permute-start.1 = (f32[256,4]{1,0:T(8,128)S(1)}, f32[256,4]{1,0:T(8,128)S(1)}, u32[]{:S(2)}, u32[]{:S(2)}) collective-permute-start(f32[256,4]{1,0:T(8,128)S(1)} %get-tuple-element.33), channel_id=1, source_target_pairs={{0,15},{1,0},{2,1},{3,2},{4,3},{5,4},{6,5},{7,6},{8,7},{9,8},{10,9... | collective-permute-start | bytes 12296 | tf_op jit(solution)/shard_map/ppermute | solution.py:450
  8.2 7.4 %collective-permute-start = (f32[256,4]{1,0:T(8,128)S(1)}, f32[256,4]{1,0:T(8,128)S(1)}, u32[]{:S(2)}, u32[]{:S(2)}) collective-permute-start(f32[256,4]{1,0:T(8,128)S(1)} %get-tuple-element.34), channel_id=1, source_target_pairs={{0,1},{1,2},{2,3},{3,4},{4,5},{5,6},{6,7},{7,8},{8,9},{9,10},{10,1... | collective-permute-start | bytes 12296 | tf_op jit(solution)/shard_map/ppermute | solution.py:450
  15.6 9.7 %copy-start = (f32[256,128]{1,0:T(8,128)S(1)}, f32[256,128]{1,0:T(8,128)}, u32[]{:S(2)}) copy-start(f32[256,128]{1,0:T(8,128)} %own.1) | copy-start | bytes 393220
  15.6 41.8 %all-to-all-start = ((bf16[128,8,1152]{2,1,0:T(8,128)(2,1)}), bf16[128,8,1152]{2,1,0:T(8,128)(2,1)S(1)}, u32[]{:S(2)}, u32[]{:S(2)}) async-start(bf16[128,8,1152]{2,1,0:T(8,128)(2,1)} %bitcast.17), calls=%async_computation | async-start | bytes 4718592 | tf_op jit(solution)/shard_map/all_to_all | solution.py:460
  29.9 2.0 %copy-start.3 = (f32[3,320,1152]{2,1,0:T(8,128)}, f32[3,320,1152]{2,1,0:T(8,128)S(1)}, u32[]{:S(2)}) copy-start(f32[3,320,1152]{2,1,0:T(8,128)S(1)} %get-tuple-element.25.coef) | copy-start | bytes 13271044
  57.4 11.4 %copy-start.4 = (f32[3,320,1152]{2,1,0:T(8,128)S(1)}, f32[3,320,1152]{2,1,0:T(8,128)}, u32[]{:S(2)}) copy-start(f32[3,320,1152]{2,1,0:T(8,128)} %copy-done.3) | copy-start | bytes 13271044
  62.9 16.1 %collective-permute-start.2 = (f32[8,4,1152]{2,1,0:T(4,128)S(1)}, f32[8,4,1152]{2,1,0:T(4,128)S(1)}, u32[]{:S(2)}, u32[]{:S(2)}) collective-permute-start(f32[8,4,1152]{2,1,0:T(4,128)S(1)} %get-tuple-element.29), channel_id=1, source_target_pairs={{0,16},{16,32},{32,48},{48,64},{64,80},{80,96},{96,112},{1,17},{17... | collective-permute-start | bytes 442376 | tf_op jit(solution)/shard_map/ppermute | solution.py:450
  66.6 12.4 %collective-permute-start.3 = (f32[8,4,1152]{2,1,0:T(4,128)S(1)}, f32[8,4,1152]{2,1,0:T(4,128)S(1)}, u32[]{:S(2)}, u32[]{:S(2)}) collective-permute-start(f32[8,4,1152]{2,1,0:T(4,128)S(1)} %get-tuple-element.30), channel_id=1, source_target_pairs={{16,0},{32,16},{48,32},{64,48},{80,64},{96,80},{112,96},{17,1},{33... | collective-permute-start | bytes 442376 | tf_op jit(solution)/shard_map/ppermute | solution.py:450
  79.0 23.3 %copy-start.1 = (f32[8,512]{1,0:T(8,128)S(1)}, f32[8,512]{1,0:T(8,128)}, u32[]{:S(2)}) copy-start(f32[8,512]{1,0:T(8,128)} %get-tuple-element.32.rank) | copy-start | bytes 49156
  79.0 23.3 %copy-start.2 = (s32[512,1]{0,1:T(1,128)S(1)}, s32[512,1]{0,1:T(1,128)}, u32[]{:S(2)}) copy-start(s32[512,1]{0,1:T(1,128)} %param.8) | copy-start | bytes 6148

commit v2 on v1

v2 whole, which is shorter than its diff:
```python
import jax
import jax.numpy as jnp
from jax import lax
from jax.experimental import pallas as pl
from jax.experimental.pallas import tpu as pltpu
from jax.sharding import PartitionSpec as P

SLOTS = 8
CLON = 128
PASSES = 4
RHS = 4
OBS = 512
CAP = 8
DEVICES = 128
LON = 16
ROWS = 256
CHUNKS = 8
DEPTH = ROWS // CHUNKS
TALL = DEPTH + 2 * PASSES
RUN = 9
SPAN = SLOTS * CLON
WIDE = RUN * 128
EAST = CLON + PASSES
TOTAL = DEVICES * CAP
RIM = 2 * PASSES
OUTER = 2 * PASSES * CHUNKS
MIDDLE = ROWS - OUTER
BF = jnp.bfloat16
F32 = jnp.float32
NT = ((1,), (1,))
TN = ((0,), (0,))


def iota(shape, dim):
    return lax.broadcasted_iota(jnp.int32, shape, dim)


def pick(cond):
    return jnp.where(cond, 1.0, 0.0).astype(BF)


def mm(a, b, dims=((1,), (0,))):
    return lax.dot_general(a, b, (dims, ((), ())), preferred_element_type=F32)


def thirds(x):
    hi = x.astype(BF)
    rest = x - hi.astype(F32)
    mid = rest.astype(BF)
    return hi, mid, (rest - mid.astype(F32)).astype(BF)


def params(mib):
    return pltpu.CompilerParams(vmem_limit_bytes=mib * 1024 * 1024)


def cost(flops, size):
    return pl.CostEstimate(flops=flops, bytes_accessed=size, transcendentals=0)


def lanes(shape, dim):
    lane = iota(shape, dim)
    q, k, s = lane // 128, lane % 128 // 8, lane % 8
    return k * RUN + q, s, q, k


def rolled(x, step):
    return pltpu.roll(x, step % 128, 1)


def beside(row):
    return row[1:] + [rolled(row[0], -SLOTS)], [rolled(row[-1], SLOTS)] + row[:-1]


PIECES = 4


def pack_kernel(prints_hbm, weights_hbm, target_hbm, block_hbm, slot_hbm, out_hbm, rank_out,
                prints, weights, target, block, slot, masked, meta, spread, wide, out, sems, out_sems):
    pairs = ((target_hbm, target), (weights_hbm, weights), (block_hbm, block), (slot_hbm, slot), (prints_hbm, prints))
    copies = [pltpu.make_async_copy(a, b, sems.at[i]) for i, (a, b) in enumerate(pairs)]
    for copy in copies:
        copy.start()
    e, s, q, k = lanes((1, WIDE), 1)
    base = s * CLON + e
    source = jnp.where(e < PASSES, base + CLON - PASSES, jnp.where(e < EAST, base - PASSES, base - EAST))
    source = jnp.where(e < EAST + PASSES, source, -1)
    spread[...] = pick(iota((SPAN, WIDE), 0) == source)
    before = pick(iota((OBS, OBS), 0) < iota((OBS, OBS), 1))
    for copy in copies[:4]:
        copy.wait()
    t = target[...]
    hit = pick(iota((DEVICES, OBS), 0) == t)
    earlier = mm(hit, before)
    rank = jnp.sum(hit.astype(F32) * earlier, axis=0, keepdims=True)
    rank_out[...] = jnp.broadcast_to(rank, (8, OBS))
    place = t * CAP + rank.astype(jnp.int32)
    blk = block[...]
    meta[...] = jnp.zeros_like(meta)
    meta[0:RHS, :] = weights[...].astype(F32)
    meta[4:5, :] = ((blk % DEPTH) * CHUNKS + blk // DEPTH).astype(F32)
    meta[5:6, :] = slot[...].astype(F32)
    facts = meta[...].astype(BF)
    slots = mm(facts, pick(iota((8, 128), 0) == 5), TN).astype(BF)
    where = pick(iota((TOTAL, OBS), 0) == place)
    copies[4].wait()
    for s in range(SLOTS):
        live = slots >= jnp.asarray(s, BF)
        piece = prints[:, s * CLON:(s + 1) * CLON]
        masked[:, s * CLON:(s + 1) * CLON] = jnp.where(live, piece, jnp.zeros_like(piece))
    e, s, q, k = lanes((1, WIDE), 1)
    fact = jnp.where((k == 15) & (q >= 1) & (q <= 3) & (s < 5), s, -1)
    wide[...] = (mm(masked[...], spread[...]) + mm(facts, pick(iota((8, WIDE), 0) == fact), TN)).astype(BF)
    e, s, q, k = lanes((1, 1, WIDE), 2)
    from_west = (e < PASSES) | ((k == 15) & (q == 2))
    from_east = ((e >= EAST) & (e < EAST + PASSES)) | ((k == 15) & (q == 3))
    sends = []
    size = TOTAL // PIECES
    for i in range(PIECES):
        rows = slice(i * size, (i + 1) * size)
        moved = mm(where[rows], wide[...]).reshape(size // (LON * CAP), LON * CAP, WIDE)
        up = jnp.concatenate([moved[:, -CAP:], moved[:, :-CAP]], axis=1)
        down = jnp.concatenate([moved[:, CAP:], moved[:, :CAP]], axis=1)
        result = jnp.where(from_west, up, jnp.where(from_east, down, moved))
        out[rows, :] = result.reshape(size, WIDE).astype(BF)
        sends.append(pltpu.make_async_copy(out.at[rows, :], out_hbm.at[rows, :], out_sems.at[i]))
        sends[-1].start()
    for send in sends:
        send.wait()


def pack(prints, weights, target, block, slot):
    hbm = pl.BlockSpec(memory_space=pltpu.HBM)
    return pl.pallas_call(
        pack_kernel,
        in_specs=[hbm] * 5,
        out_specs=(hbm, pl.BlockSpec(memory_space=pltpu.VMEM)),
        out_shape=(
            jax.ShapeDtypeStruct((TOTAL, WIDE), BF),
            jax.ShapeDtypeStruct((8, OBS), F32),
        ),
        scratch_shapes=[
            pltpu.VMEM((OBS, SPAN), BF),
            pltpu.VMEM((RHS, OBS), BF),
            pltpu.VMEM((1, OBS), jnp.int32),
            pltpu.VMEM((1, OBS), jnp.int32),
            pltpu.VMEM((1, OBS), jnp.int32),
            pltpu.VMEM((OBS, SPAN), BF),
            pltpu.VMEM((8, OBS), F32),
            pltpu.VMEM((SPAN, WIDE), BF),
            pltpu.VMEM((OBS, WIDE), BF),
            pltpu.VMEM((TOTAL, WIDE), BF),
            pltpu.SemaphoreType.DMA((5,)),
            pltpu.SemaphoreType.DMA((PIECES,)),
        ],
        compiler_params=params(60),
        cost_estimate=cost(2 * TOTAL * OBS * SPAN, 3 << 20),
        name="pack",
    )(prints, weights, target, block, slot)


def faces_kernel(own, first, second, coef, last, rim, wide):
    e, _, _, _ = lanes((1, WIDE), 1)
    even = lax.axis_index("lon") % 2 == 0

    def place(x, cond, shift):
        one = jnp.where(cond & (iota((CLON, WIDE), 0) == e + shift), 1.0, 0.0)
        return jnp.dot(jnp.sqrt(x), one, precision=lax.Precision.HIGHEST, preferred_element_type=F32)

    left = jnp.where(even, second[...], first[...])
    right = jnp.where(even, first[...], second[...])
    flat = place(own[...], (e >= PASSES) & (e < EAST), -PASSES)
    flat = flat + (place(left, e < PASSES, CLON - PASSES) + place(right, (e >= EAST) & (e < EAST + PASSES), -EAST))
    beyond = jnp.zeros((PASSES, 128), F32)
    for q in range(RUN):
        wide[q, :PASSES, :] = beyond
        wide[q, PASSES:PASSES + ROWS, :] = flat[:, q * 128:(q + 1) * 128]
        wide[q, PASSES + ROWS:, :] = beyond
    for j in range(RIM):
        rim[j, :RHS, :] = jnp.broadcast_to(flat[j:j + 1], (RHS, WIDE))
        rim[j, RHS:, :] = jnp.broadcast_to(flat[ROWS - 1 - j:ROWS - j], (RHS, WIDE))

    def level(e):
        return [wide[q, pl.ds(e, CHUNKS, stride=DEPTH), :] for q in range(RUN)]

    none = [jnp.zeros((CHUNKS, 128), F32)] * RUN
    here, south = level(0), none
    for e in range(TALL):
        north = level(e + 1) if e + 1 < TALL else none
        ahead, behind = beside(here)
        rows = slice(e * CHUNKS, (e + 1) * CHUNKS)
        for q in range(RUN):
            cols = slice(q * 128, (q + 1) * 128)
            mid = 1.0 - here[q] * ((north[q] + south[q]) + (ahead[q] + behind[q]))
            coef[0, rows, cols] = mid
            coef[1, rows, cols] = here[q] * here[q]
            if PASSES <= e < TALL - PASSES:
                inner = slice((e - PASSES) * CHUNKS, (e - PASSES + 1) * CHUNKS)
                some = here[q] > 0.0
                last[0, inner, cols] = jnp.where(some, mid / jnp.where(some, here[q], 1.0), 0.0)
                last[1, inner, cols] = here[q]
        here, south = north, here


def faces(own, first, second):
    return pl.pallas_call(
        faces_kernel,
        out_shape=(
            jax.ShapeDtypeStruct((2, TALL * CHUNKS, WIDE), F32),
            jax.ShapeDtypeStruct((2, ROWS, WIDE), F32),
            jax.ShapeDtypeStruct((RIM, 2 * RHS, WIDE), F32),
        ),
        scratch_shapes=[pltpu.VMEM((RUN, ROWS + 8, 128), F32)],
        compiler_params=params(16),
        cost_estimate=cost(1 << 30, 6 << 20),
        name="faces",
    )(own, first, second)


def adjoint_kernel(got, last, roots, field, rim, inner, outer, facts_out, own, west, east):
    column, fact = iota((16, 128), 0), iota((16, 128), 1) - 120
    facts = mm(pick((fact == column) & (column < 5)), got[:, 128:256], NT)
    facts = facts + mm(pick((fact == column - 5) & (column >= 5) & (column < 10)), got[:, 256:384], NT)
    facts = facts + mm(pick((fact == column - 10) & (column >= 10) & (column < 15)), got[:, 384:512], NT)
    facts_out[...] = facts
    for q in range(RUN):
        piece = got[:, q * 128:(q + 1) * 128]
        e = (iota((1, 128), 1) // 8) * RUN + q
        ones = lambda cond: jnp.broadcast_to(pick(cond), piece.shape)
        own[:, q * 128:(q + 1) * 128] = piece * ones((e >= PASSES) & (e < EAST))
        if q < PASSES:
            west[:, q * 128:(q + 1) * 128] = piece * ones(e < PASSES)
        if q in EASTERN:
            at = EASTERN.index(q) * 128
            east[:, at:at + 128] = piece * ones((e >= EAST) & (e < EAST + PASSES))
    row = iota((ROWS, TOTAL), 0).astype(F32)

    def spread(first, r):
        return jnp.where(row == facts[first + RHS:first + RHS + 1], facts[first + r:first + r + 1], 0.0).astype(BF)

    for r in range(RHS):
        total = mm(spread(0, r), own[...])
        before, after = mm(spread(5, r), west[...]), mm(spread(10, r), east[...])
        for q in range(RUN):
            cols = slice(q * 128, (q + 1) * 128)
            part = total[:, cols]
            if q < PASSES:
                part = part + before[:, cols]
            if q in EASTERN:
                at = EASTERN.index(q) * 128
                part = part + after[:, at:at + 128]
            field[r, :, cols] = part * last[1, :, cols]
        for j in range(RIM):
            rim[j, r:r + 1, :] = field[r, j * CHUNKS:j * CHUNKS + 1, :]
            end = (DEPTH - j) * CHUNKS
            rim[j, RHS + r:RHS + r + 1, :] = field[r, end - 1:end, :]
    even = lax.axis_index("lat") % 2 == 0
    for base, ref in ((0, rim), (PASSES, roots)):
        for j in range(PASSES):
            low, high = ref[j, :RHS, :], ref[j, RHS:, :]
            inner[base + j] = jnp.where(even, high, low)
            outer[base + j] = jnp.where(even, low, high)


EASTERN = [(EAST + i) % RUN for i in range(PASSES)]


def adjoint(got, last, roots):
    return pl.pallas_call(
        adjoint_kernel,
        out_shape=(
            jax.ShapeDtypeStruct((RHS, ROWS, WIDE), F32),
            jax.ShapeDtypeStruct((RIM, 2 * RHS, WIDE), F32),
            jax.ShapeDtypeStruct((2 * PASSES, RHS, WIDE), F32),
            jax.ShapeDtypeStruct((2 * PASSES, RHS, WIDE), F32),
            jax.ShapeDtypeStruct((16, TOTAL), F32),
        ),
        scratch_shapes=[
            pltpu.VMEM((TOTAL, WIDE), BF),
            pltpu.VMEM((TOTAL, PASSES * 128), BF),
            pltpu.VMEM((TOTAL, PASSES * 128), BF),
        ],
        compiler_params=params(20),
        cost_estimate=cost(5 << 30, 8 << 20),
        name="adjoint",
    )(got, last, roots)


def inside(q):
    e = (iota((1, 128), 1) // 8) * RUN + q
    return (e >= PASSES) & (e < EAST)


def diffuse_kernel(field, coef, last, smooth, outer, ends, one, two):
    side = 6 * CHUNKS
    for r in range(RHS):
        for e in range(PASSES):
            rows = slice((DEPTH - PASSES + e) * CHUNKS, (DEPTH - PASSES + e + 1) * CHUNKS)
            ends[r, e * CHUNKS:(e + 1) * CHUNKS, :] = pltpu.roll(field[r, rows, :], 1, 0)
            at = side + (2 + e) * CHUNKS
            ends[r, at:at + CHUNKS, :] = pltpu.roll(field[r, e * CHUNKS:(e + 1) * CHUNKS, :], CHUNKS - 1, 0)
        ends[r, PASSES * CHUNKS:side, :] = field[r, :2 * CHUNKS, :]
        ends[r, side:side + 2 * CHUNKS, :] = field[r, (DEPTH - 2) * CHUNKS:, :]

    def rows_of(e):
        at = e * CHUNKS
        return pl.ds(at if isinstance(at, int) else pl.multiple_of(at, CHUNKS), CHUNKS)

    def two_levels(ref, base, e, factor, lift, store):
        def load(r, at, q):
            return ref[r, rows_of(at + base), q * 128:(q + 1) * 128]

        levels = (e, e + 1)
        turned_west = [[rolled(load(r, at, RUN - 1), SLOTS) for at in levels] for r in range(RHS)]
        turned_east = [[rolled(load(r, at, 0), -SLOTS) for at in levels] for r in range(RHS)]
        behind, here = [[[load(r, at, q) for at in levels] for r in range(RHS)] for q in (0, 1)]
        for q in [*range(1, RUN), 0]:
            mid, near = [[factor[kind, rows_of(at + lift), q * 128:(q + 1) * 128] for at in levels] for kind in (0, 1)]
            if q == 0:
                behind = turned_west
                here, ahead = [[[load(r, at, i) for at in levels] for r in range(RHS)] for i in (0, 1)]
            elif q + 1 < RUN:
                ahead = [[load(r, at, q + 1) for at in levels] for r in range(RHS)]
            else:
                ahead = turned_east
            for r in range(RHS):
                column = [load(r, e - 1, q)] + here[r] + [load(r, e + 2, q)]
                for i in range(2):
                    total = (column[i + 2] + column[i]) + (ahead[r][i] + behind[r][i])
                    store(r, q, i, mid[i] * here[r][i] + near[i] * total)
            behind, here = here, ahead

    def sweep(ref, base, target, first, end, to=0, factor=coef, lift=0):
        def step(pair, _):
            e = first + 2 * pair

            def store(r, q, i, value):
                target[r, rows_of(e + i + to), q * 128:(q + 1) * 128] = value

            two_levels(ref, base, e, factor, lift, store)
            return 0

        lax.fori_loop(0, (end - first) // 2, step, 0, unroll=2)

    sweep(ends, 0, one, 1, 5)
    sweep(field, -PASSES, one, 5, TALL - 5)
    sweep(ends, -28, one, TALL - 5, TALL - 1)
    sweep(one, 0, two, 2, TALL - 2)
    sweep(two, 0, one, 3, TALL - 3)
    sweep(one, 0, outer, PASSES, 2 * PASSES, -PASSES, last, -PASSES)
    sweep(one, 0, outer, DEPTH, DEPTH + PASSES, -DEPTH + PASSES, last, -PASSES)

    def final(pair, _):
        first = {}

        def store(r, q, i, value):
            if i == 0:
                first[r, q] = value
                return
            both = jnp.concatenate([first.pop((r, q)), value], axis=0)
            at = pl.ds(pl.multiple_of(pair * 2 * CHUNKS, 2 * CHUNKS), 2 * CHUNKS)
            smooth[r, at, q * 128:(q + 1) * 128] = jnp.where(inside(q), both, 0.0).astype(BF)

        two_levels(one, 0, 2 * PASSES + 2 * pair, last, -PASSES, store)
        return 0

    lax.fori_loop(0, MIDDLE // (2 * CHUNKS), final, 0, unroll=2)


def diffuse(field, coef, last):
    return pl.pallas_call(
        diffuse_kernel,
        out_shape=(
            jax.ShapeDtypeStruct((RHS, MIDDLE, WIDE), BF),
            jax.ShapeDtypeStruct((RHS, OUTER, WIDE), F32),
        ),
        scratch_shapes=[
            pltpu.VMEM((RHS, 12 * CHUNKS, WIDE), F32),
            pltpu.VMEM((RHS, TALL * CHUNKS, WIDE), F32),
            pltpu.VMEM((RHS, TALL * CHUNKS, WIDE), F32),
        ],
        compiler_params=params(24),
        cost_estimate=cost(6 << 30, 8 << 20),
        name="diffuse",
    )(field, coef, last)


def finish_kernel(smooth, outer, rim, roots, inner, beyond, got, facts, out, border, values):
    even = lax.axis_index("lat") % 2 == 0

    def levels(base, own):
        rows = []
        for j in range(base + PASSES - 1, base - 1, -1):
            south = jnp.where(even, beyond[j], inner[j])
            north = jnp.where(even, inner[j], beyond[j])
            rows.append(jnp.concatenate([south, north], axis=0))
        return [[x[:, q * 128:(q + 1) * 128] for q in range(RUN)] for x in rows + [own[j] for j in range(RIM)]]

    def around(x, j):
        ahead, behind = beside(x[j])
        return [(x[j + 1][q] + x[j - 1][q]) + (ahead[q] + behind[q]) for q in range(RUN)]

    v, root = levels(0, rim), levels(PASSES, roots)
    count = PASSES + RIM
    mid = [None] + [[1.0 - x * y for x, y in zip(root[j], around(root, j))] for j in range(1, count - 1)]
    for step in range(1, PASSES + 1):
        new = list(v)
        for j in range(step, count - step):
            total = around(v, j)
            new[j] = [mid[j][q] * v[j][q] + (root[j][q] * root[j][q]) * total[q] for q in range(RUN)]
        v = new
    for j in range(PASSES, 2 * PASSES):
        some = [x > 0.0 for x in root[j]]
        v[j] = [jnp.where(some[q], v[j][q] / jnp.where(some[q], root[j][q], 1.0), 0.0) for q in range(RUN)]
    sub = iota((CHUNKS, 1), 0)
    for r in range(RHS):
        for q in range(RUN):
            cols = slice(q * 128, (q + 1) * 128)
            for pair in range(PASSES):
                both = []
                for b in (2 * pair, 2 * pair + 1):
                    here = outer[r, b * CHUNKS:(b + 1) * CHUNKS, cols]
                    if b < PASSES:
                        here = jnp.where(sub == 0, v[PASSES + b][q][r:r + 1], here)
                    else:
                        j = PASSES + 2 * PASSES - 1 - b
                        here = jnp.where(sub == CHUNKS - 1, v[j][q][RHS + r:RHS + r + 1], here)
                    both.append(here)
                both = jnp.where(inside(q), jnp.concatenate(both, axis=0), 0.0).astype(BF)
                border[r, pair * 2 * CHUNKS:(pair + 1) * 2 * CHUNKS, cols] = both

    side = PASSES * CHUNKS
    chosen = iota((ROWS, TOTAL), 0).astype(F32) == facts[RHS:RHS + 1, :]
    total = [0.0] * RHS
    for ref, spans in ((smooth, ((side, MIDDLE),)), (border, ((0, side), (ROWS - side, side)))):
        shares = mm(ref[...].reshape(-1, WIDE), got[...], NT)
        at = 0
        for r in range(RHS):
            for first, size in spans:
                part = jnp.where(chosen[first:first + size], shares[at:at + size], 0.0)
                total[r] = total[r] + jnp.sum(part, axis=0, keepdims=True)
                at += size
    for r in range(RHS):
        values[r:r + 1, :] = total[r]
        values[RHS + r:RHS + r + 1, :] = total[r]
    both = values[...]
    turn = iota((2 * RHS, TOTAL), 0) // RHS
    keep = [jnp.where(iota((2 * RHS, TOTAL), 1) % CAP == turn + 2 * i, 1.0, 0.0) for i in range(CAP // 2)]
    many = [part.astype(F32) * k for part in thirds(both) for k in keep]
    owner = pick(iota((DEVICES, TOTAL), 1) // CAP == iota((DEVICES, TOTAL), 0))
    sums = mm(owner, jnp.concatenate(many, axis=0).astype(BF), NT)
    size = CAP * RHS
    out[...] = jnp.zeros_like(out)
    out[:, :size] = (sums[:, :size] + sums[:, size:2 * size]) + sums[:, 2 * size:3 * size]


def finish(smooth, outer, rim, roots, inner, beyond, got, facts):
    return pl.pallas_call(
        finish_kernel,
        out_shape=jax.ShapeDtypeStruct((DEVICES, 128), F32),
        scratch_shapes=[
            pltpu.VMEM((RHS, OUTER, WIDE), BF),
            pltpu.VMEM((8, TOTAL), F32),
        ],
        compiler_params=params(24),
        cost_estimate=cost(3 << 30, 10 << 20),
        name="finish",
    )(smooth, outer, rim, roots, inner, beyond, got, facts)


def unpack_kernel(values, target, rank, out):
    hit = pick(iota((DEVICES, OBS), 0) == target[...])
    total = jnp.zeros((CAP * RHS, OBS), F32)
    for part in thirds(values[:, :CAP * RHS]):
        total = total + mm(part, hit, TN)
    total = jnp.where((iota((CAP * RHS, OBS), 0) // RHS).astype(F32) == rank[0:1, :], total, 0.0)
    pair = (total[0:8] + total[8:16]) + (total[16:24] + total[24:32])
    out[...] = pair[0:RHS] + pair[RHS:]


def unpack(values, target, rank):
    return pl.pallas_call(
        unpack_kernel,
        out_shape=jax.ShapeDtypeStruct((RHS, OBS), F32),
        compiler_params=params(16),
        name="unpack",
    )(values, target, rank)


def swap(x, axis, second, closed):
    count = lax.axis_size(axis)
    pairs = [(i, (i + 1) % count) for i in range(int(second), count, 2) if closed or i + 1 < count]
    return lax.ppermute(x, axis, pairs + [(j, i) for i, j in pairs])


def body(footprints, dual_weights, target_device, target_block, obs_slot, diffusivity):
    target = target_device.reshape(1, OBS)
    packed, rank = pack(footprints, dual_weights.T, target, target_block.reshape(1, OBS), obs_slot.reshape(1, OBS))
    first = swap(diffusivity, "lon", False, True)
    second = swap(diffusivity, "lon", True, True)
    packed, first, second = lax.optimization_barrier((packed, first, second))
    coef, last, roots = faces(diffusivity, first, second)
    got = lax.all_to_all(packed, ("lat", "lon"), split_axis=0, concat_axis=0, tiled=True)
    field, rim, inner, beyond, facts = adjoint(got, last, roots)
    inner = swap(inner, "lat", False, False)
    beyond = swap(beyond, "lat", True, False)
    smooth, outer = diffuse(field, coef, last)
    values = finish(smooth, outer, rim, roots, inner, beyond, got, facts)
    returned = lax.all_to_all(values, ("lat", "lon"), split_axis=0, concat_axis=0, tiled=True)
    return unpack(returned, target, rank).T


def solution(mesh):
    placed = (
        P(("lat", "lon"), None),
        P(("lat", "lon"), None),
        P(("lat", "lon"), None),
        P(("lat", "lon")),
        P(("lat", "lon")),
        P("lat", "lon"),
    )
    return jax.shard_map(
        body, mesh=mesh, in_specs=placed, out_specs=P(("lat", "lon"), None), check_vma=False
    )
```

time: 103 us -> 88.5 us (0.86)
  Pallas kernels: 37.5 us -> 26.2 us
  starting transfers between devices: 22.6 us -> 18.3 us
  local copies, waits for them, and re-layouts: 3.11 us -> 4.67 us
    pallas_call x1, Pallas kernels: 8.89 us -> 3.4 us  [finish(): pl.pallas_call(finish_kernel, out_shape=jax.ShapeDtypeStruct((DEVICES, 12...]
    pallas_call x1, Pallas kernels: 10.2 us -> 6.02 us  [diffuse(): pl.pallas_call(diffuse_kernel, out_shape=(jax.ShapeDtypeStruct((RHS, MIDD...]
    unnamed x10 -> x16, local copies, waits for them, and re-layouts: 2.04 us -> 4.67 us
    all_to_all x1, starting transfers between devices: 9.63 us -> 7.08 us  [body(): lax.all_to_all(packed, ('lat', 'lon'), split_axis=0, concat_axis=0, tiled...]
    ppermute x4, starting transfers between devices: 13 us -> 11.2 us  [swap(): return lax.ppermute(x, axis, pairs + [(j, i) for i, j in pairs])]
    pallas_call x1, Pallas kernels: 7.38 us -> 5.94 us  [pack(): pl.pallas_call(pack_kernel, in_specs=[hbm] * 5, out_specs=(hbm, pl.BlockS...]
    slice x1 -> x0, local copies, waits for them, and re-layouts: 1.07 us -> none  [body(): right = shift(diffusivity[:, :PASSES], 'lon', -1, True)]
  transfers between devices with their start and end apart: 5 -> 5, of which waited for: 1 -> 1; matrix products, arithmetic and copies ran while one was open for 0% -> 0% of each run, Pallas kernels for 22% -> 19%
where the time goes in v2:
time: 88.5 us; the launch traced here: 88.3 us
  Pallas kernels  26.2 us (30%)
  waiting for transfers between devices  24.8 us (28%)
  starting transfers between devices  18.3 us (21%)
  blocking collectives  14.2 us (16%)
  local copies, waits for them, and re-layouts  4.67 us (5%)
    all_to_all x1, waiting for transfers between devices, body(): lax.all_to_all(packed, ('lat', 'lon'), split_axis=0, concat_axis=0, tiled...  24.8 us
    all_to_all x1, blocking collectives, body(): lax.all_to_all(values, ('lat', 'lon'), split_axis=0, concat_axis=0, tiled...  14.2 us
    ppermute x4, starting transfers between devices, swap(): return lax.ppermute(x, axis, pairs + [(j, i) for i, j in pairs])  11.2 us
    all_to_all x1, starting transfers between devices, body(): lax.all_to_all(packed, ('lat', 'lon'), split_axis=0, concat_axis=0, tiled...  7.08 us
    pallas_call x1, Pallas kernels, diffuse(): pl.pallas_call(diffuse_kernel, out_shape=(jax.ShapeDtypeStruct((RHS, MIDD...  6.02 us
    pallas_call x1, Pallas kernels, pack(): pl.pallas_call(pack_kernel, in_specs=[hbm] * 5, out_specs=(hbm, pl.BlockS...  5.94 us
    pallas_call x1, Pallas kernels, adjoint(): pl.pallas_call(adjoint_kernel, out_shape=(jax.ShapeDtypeStruct((RHS, ROWS...  5.63 us
    unnamed x16, local copies, waits for them, and re-layouts  4.67 us
  transfers between devices with their start and end apart: 5, of which 1 were waited for; matrix products, arithmetic and copies ran while one was open for 0% of the time, Pallas kernels for 19%

profile of v2, /device:TPU:1, one launch (start us, length us, event | category | flops | bytes accessed | tf_op | source)
XLA Modules:
  0.0 88.3 jit_solution(6918311792982711862)
XLA Ops:
  0.0 2.5 %collective-permute-start = (f32[256,128]{1,0:T(8,128)}, f32[256,128]{1,0:T(8,128)S(1)}, u32[]{:S(2)}, u32[]{:S(2)}) collective-permute-start(f32[256,128]{1,0:T(8,128)} %own.1), channel_id=1, source_target_pairs={{0,1},{2,3},{4,5},{6,7},{8,9},{10,11},{12,13},{14,15},{1,0},{3,2},... | collective-permute-start | bytes 393224 | tf_op jit(solution)/shard_map/ppermute | solution.py:493
  2.5 4.7 %collective-permute-start.1 = (f32[256,128]{1,0:T(8,128)}, f32[256,128]{1,0:T(8,128)S(1)}, u32[]{:S(2)}, u32[]{:S(2)}) collective-permute-start(f32[256,128]{1,0:T(8,128)} %own.1), channel_id=1, source_target_pairs={{1,2},{3,4},{5,6},{7,8},{9,10},{11,12},{13,14},{15,0},{2,1},{4,3},... | collective-permute-start | bytes 393224 | tf_op jit(solution)/shard_map/ppermute | solution.py:493
  7.2 5.9 %pack.1 = (bf16[1024,1152]{1,0:T(8,128)(2,1)}, f32[8,512]{1,0:T(8,128)}) custom-call(bf16[512,1024]{1,0:T(8,128)(2,1)} %prints_hbm.1, bf16[4,512]{1,0:T(4,128)(2,1)} %bitcast.18, s32[1,512]{1,0:T(1,128)} %bitcast.15, s32[1,512]{1,0:T(1,128)} %bitcast.19, s32[1,512]{1,0:T(1,128)} %bitcast.20), custom_call_target="tpu_custom_call" | custom-call | flops 1073741824 | bytes 3145728 | tf_op jit(solution)/shard_map/pack/pallas_call | solution.py:134
  13.1 0.0 collective-permute-done.first
  13.1 0.0 collective-permute-done.1.second
  13.1 0.0 copy-start.2
  13.1 7.1 %all-to-all-start = ((bf16[128,8,1152]{2,1,0:T(8,128)(2,1)}), bf16[128,8,1152]{2,1,0:T(8,128)(2,1)S(1)}, u32[]{:S(2)}, u32[]{:S(2)}) async-start(bf16[128,8,1152]{2,1,0:T(8,128)(2,1)} %bitcast.17), calls=%async_computation | async-start | bytes 4718592 | tf_op jit(solution)/shard_map/all_to_all | solution.py:503
  20.2 4.4 %faces.1 = (f32[2,320,1152]{2,1,0:T(8,128)S(1)}, f32[2,256,1152]{2,1,0:T(8,128)S(1)}, f32[8,8,1152]{2,1,0:T(8,128)S(1)}) custom-call(f32[256,128]{1,0:T(8,128)S(1)} %copy-done.2, f32[256,128]{1,0:T(8,128)S(1)} %collective-permute-done.first, f32[256,128]{1,0:T(8,128)S(1)} %collective-permute-done.1.second), custom_call_target="tpu_custom_call" | custom-call | flops 1073741824 | bytes 6291456 | tf_op jit(solution)/shard_map/faces/pallas_call | solution.py:206
  24.6 0.0 copy-start.3
  24.6 1.6 %copy-done.3 = f32[2,320,1152]{2,1,0:T(8,128)} copy-done((f32[2,320,1152]{2,1,0:T(8,128)}, f32[2,320,1152]{2,1,0:T(8,128)S(1)}, u32[]{:S(2)}) %copy-start.3) | copy-done | bytes 2949144
  26.2 1.4 %copy-done.5 = f32[2,256,1152]{2,1,0:T(8,128)} copy-done((f32[2,256,1152]{2,1,0:T(8,128)}, f32[2,256,1152]{2,1,0:T(8,128)S(1)}, u32[]{:S(2)}) %copy-start.5) | copy-done | bytes 2359320
  27.6 24.8 %all-to-all-done = bf16[128,8,1152]{2,1,0:T(8,128)(2,1)S(1)} async-done(((bf16[128,8,1152]{2,1,0:T(8,128)(2,1)}), bf16[128,8,1152]{2,1,0:T(8,128)(2,1)S(1)}, u32[]{:S(2)}, u32[]{:S(2)}) %all-to-all-start) | async-done | bytes 2359328 | tf_op jit(solution)/shard_map/all_to_all | solution.py:503
  52.4 1.7 %copy-done.6 = f32[2,256,1152]{2,1,0:T(8,128)S(1)} copy-done((f32[2,256,1152]{2,1,0:T(8,128)S(1)}, f32[2,256,1152]{2,1,0:T(8,128)}, u32[]{:S(2)}) %copy-start.6) | copy-done | bytes 2359320
  54.0 5.6 %adjoint.1 = (f32[4,256,1152]{2,1,0:T(8,128)S(1)}, f32[8,8,1152]{2,1,0:T(8,128)S(1)}, f32[8,4,1152]{2,1,0:T(4,128)S(1)}, f32[8,4,1152]{2,1,0:T(4,128)S(1)}, f32[16,1024]{1,0:T(8,128)S(1)}) custom-call(bf16[1024,1152]{1,0:T(8,128)(2,1)S(1)} %bitcast.11, f32[2,256,1152]{2,1,0:T(8,128)S(1)} %copy-done.6, f32[8,8,1152]{2,1,0:T(8,128)S(1)} %get-tuple-element.25.roots), custom_call_target="tpu_custom_call" | custom-call | flops 5368709120 | bytes 8388608 | tf_op jit(solution)/shard_map/adjoint/pallas_call | solution.py:269
  59.7 1.3 %collective-permute-start.2 = (f32[8,4,1152]{2,1,0:T(4,128)S(1)}, f32[8,4,1152]{2,1,0:T(4,128)S(1)}, u32[]{:S(2)}, u32[]{:S(2)}) collective-permute-start(f32[8,4,1152]{2,1,0:T(4,128)S(1)} %get-tuple-element.31), channel_id=1, source_target_pairs={{0,16},{32,48},{64,80},{96,112},{16,0},{48,32},{80,64},{112,96},{1... | collective-permute-start | bytes 442376 | tf_op jit(solution)/shard_map/ppermute | solution.py:493
  61.0 2.7 %collective-permute-start.3 = (f32[8,4,1152]{2,1,0:T(4,128)S(1)}, f32[8,4,1152]{2,1,0:T(4,128)S(1)}, u32[]{:S(2)}, u32[]{:S(2)}) collective-permute-start(f32[8,4,1152]{2,1,0:T(4,128)S(1)} %get-tuple-element.32), channel_id=1, source_target_pairs={{16,32},{48,64},{80,96},{32,16},{64,48},{96,80},{17,33},{49,65},{8... | collective-permute-start | bytes 442376 | tf_op jit(solution)/shard_map/ppermute | solution.py:493
  63.8 6.0 %diffuse.1 = (bf16[4,192,1152]{2,1,0:T(8,128)(2,1)S(1)}, f32[4,64,1152]{2,1,0:T(8,128)S(1)}) custom-call(f32[4,256,1152]{2,1,0:T(8,128)S(1)} %get-tuple-element.26.field, f32[2,320,1152]{2,1,0:T(8,128)S(1)} %copy-done.4, f32[2,256,1152]{2,1,0:T(8,128)S(1)} %copy-done.7), custom_call_target="tpu_custom_call" | custom-call | flops 6442450944 | bytes 8388608 | tf_op jit(solution)/shard_map/diffuse/pallas_call | solution.py:371
  69.8 0.0 collective-permute-done.2.inner
  69.8 0.0 collective-permute-done.3.beyond
  69.8 0.0 copy-start
  69.8 0.0 copy-start.1
  69.8 3.4 %finish.1 = f32[128,128]{1,0:T(8,128)S(1)} custom-call(bf16[4,192,1152]{2,1,0:T(8,128)(2,1)S(1)} %get-tuple-element.28.smooth, f32[4,64,1152]{2,1,0:T(8,128)S(1)} %get-tuple-element.29.outer, f32[8,8,1152]{2,1,0:T(8,128)S(1)} %get-tuple-element.30.rim, f32[8,8,1152]{2,1,0:T(8,128)S(1)} %get-tuple-element.25.roots, ...), custom_call_target="tpu_custom_call" | custom-call | flops 3221225472 | bytes 10485760 | tf_op jit(solution)/shard_map/finish/pallas_call | solution.py:458
  73.2 14.2 %all_to_all.22 = f32[128,1,128]{2,1,0:T(1,128)S(1)} all-to-all(f32[128,1,128]{2,1,0:T(1,128)S(1)} %bitcast.14), channel_id=1, replica_groups=mesh['lat'=8,'lon'=16] {'lat','lon'}, dimensions={0} | all-to-all | bytes 131072 | tf_op jit(solution)/shard_map/all_to_all | solution.py:509
  87.4 0.8 unpack.1
  (9 shorter events, 0.0 us)
Async XLA Ops:
  0.0 13.1 %collective-permute-start = (f32[256,128]{1,0:T(8,128)}, f32[256,128]{1,0:T(8,128)S(1)}, u32[]{:S(2)}, u32[]{:S(2)}) collective-permute-start(f32[256,128]{1,0:T(8,128)} %own.1), channel_id=1, source_target_pairs={{0,1},{2,3},{4,5},{6,7},{8,9},{10,11},{12,13},{14,15},{1,0},{3,2},... | collective-permute-start | bytes 393224 | tf_op jit(solution)/shard_map/ppermute | solution.py:493
  2.5 10.7 %collective-permute-start.1 = (f32[256,128]{1,0:T(8,128)}, f32[256,128]{1,0:T(8,128)S(1)}, u32[]{:S(2)}, u32[]{:S(2)}) collective-permute-start(f32[256,128]{1,0:T(8,128)} %own.1), channel_id=1, source_target_pairs={{1,2},{3,4},{5,6},{7,8},{9,10},{11,12},{13,14},{15,0},{2,1},{4,3},... | collective-permute-start | bytes 393224 | tf_op jit(solution)/shard_map/ppermute | solution.py:493
  13.1 7.1 %copy-start.2 = (f32[256,128]{1,0:T(8,128)S(1)}, f32[256,128]{1,0:T(8,128)}, u32[]{:S(2)}) copy-start(f32[256,128]{1,0:T(8,128)} %own.1) | copy-start | bytes 393220
  13.1 39.2 %all-to-all-start = ((bf16[128,8,1152]{2,1,0:T(8,128)(2,1)}), bf16[128,8,1152]{2,1,0:T(8,128)(2,1)S(1)}, u32[]{:S(2)}, u32[]{:S(2)}) async-start(bf16[128,8,1152]{2,1,0:T(8,128)(2,1)} %bitcast.17), calls=%async_computation | async-start | bytes 4718592 | tf_op jit(solution)/shard_map/all_to_all | solution.py:503
  24.6 1.6 %copy-start.3 = (f32[2,320,1152]{2,1,0:T(8,128)}, f32[2,320,1152]{2,1,0:T(8,128)S(1)}, u32[]{:S(2)}) copy-start(f32[2,320,1152]{2,1,0:T(8,128)S(1)} %get-tuple-element.27.coef) | copy-start | bytes 8847364
  26.2 1.4 %copy-start.5 = (f32[2,256,1152]{2,1,0:T(8,128)}, f32[2,256,1152]{2,1,0:T(8,128)S(1)}, u32[]{:S(2)}) copy-start(f32[2,256,1152]{2,1,0:T(8,128)S(1)} %get-tuple-element.24.last) | copy-start | bytes 7077892
  52.4 1.7 %copy-start.6 = (f32[2,256,1152]{2,1,0:T(8,128)S(1)}, f32[2,256,1152]{2,1,0:T(8,128)}, u32[]{:S(2)}) copy-start(f32[2,256,1152]{2,1,0:T(8,128)} %copy-done.5) | copy-start | bytes 7077892
  54.0 9.7 %copy-start.4 = (f32[2,320,1152]{2,1,0:T(8,128)S(1)}, f32[2,320,1152]{2,1,0:T(8,128)}, u32[]{:S(2)}) copy-start(f32[2,320,1152]{2,1,0:T(8,128)} %copy-done.3) | copy-start | bytes 8847364
  54.0 9.7 %copy-start.7 = (f32[2,256,1152]{2,1,0:T(8,128)S(1)}, f32[2,256,1152]{2,1,0:T(8,128)}, u32[]{:S(2)}) copy-start(f32[2,256,1152]{2,1,0:T(8,128)} %copy-done.5) | copy-start | bytes 7077892
  59.7 10.1 %collective-permute-start.2 = (f32[8,4,1152]{2,1,0:T(4,128)S(1)}, f32[8,4,1152]{2,1,0:T(4,128)S(1)}, u32[]{:S(2)}, u32[]{:S(2)}) collective-permute-start(f32[8,4,1152]{2,1,0:T(4,128)S(1)} %get-tuple-element.31), channel_id=1, source_target_pairs={{0,16},{32,48},{64,80},{96,112},{16,0},{48,32},{80,64},{112,96},{1... | collective-permute-start | bytes 442376 | tf_op jit(solution)/shard_map/ppermute | solution.py:493
  61.0 8.8 %collective-permute-start.3 = (f32[8,4,1152]{2,1,0:T(4,128)S(1)}, f32[8,4,1152]{2,1,0:T(4,128)S(1)}, u32[]{:S(2)}, u32[]{:S(2)}) collective-permute-start(f32[8,4,1152]{2,1,0:T(4,128)S(1)} %get-tuple-element.32), channel_id=1, source_target_pairs={{16,32},{48,64},{80,96},{32,16},{64,48},{96,80},{17,33},{49,65},{8... | collective-permute-start | bytes 442376 | tf_op jit(solution)/shard_map/ppermute | solution.py:493
  69.8 17.6 %copy-start = (f32[8,512]{1,0:T(8,128)S(1)}, f32[8,512]{1,0:T(8,128)}, u32[]{:S(2)}) copy-start(f32[8,512]{1,0:T(8,128)} %get-tuple-element.34.rank) | copy-start | bytes 49156
  69.8 17.6 %copy-start.1 = (s32[512,1]{0,1:T(1,128)S(1)}, s32[512,1]{0,1:T(1,128)}, u32[]{:S(2)}) copy-start(s32[512,1]{0,1:T(1,128)} %param.8) | copy-start | bytes 6148

commit v3 on v2

--- a/solution.py
+++ b/solution.py
@@ -16,7 +16,7 @@
 ROWS = 256
 CHUNKS = 8
 DEPTH = ROWS // CHUNKS
-TALL = DEPTH + 2 * PASSES
+TALL = DEPTH + 2
 RUN = 9
 SPAN = SLOTS * CLON
 WIDE = RUN * 128
@@ -159,7 +159,7 @@
     )(prints, weights, target, block, slot)
 
 
-def faces_kernel(own, first, second, coef, last, rim, wide):
+def faces_kernel(own, first, second, coef, over, root, rim, wide):
     e, _, _, _ = lanes((1, WIDE), 1)
     even = lax.axis_index("lon") % 2 == 0
 
@@ -171,53 +171,59 @@
     right = jnp.where(even, first[...], second[...])
     flat = place(own[...], (e >= PASSES) & (e < EAST), -PASSES)
     flat = flat + (place(left, e < PASSES, CLON - PASSES) + place(right, (e >= EAST) & (e < EAST + PASSES), -EAST))
-    beyond = jnp.zeros((PASSES, 128), F32)
+    beyond = jnp.zeros((CHUNKS, 128), F32)
     for q in range(RUN):
-        wide[q, :PASSES, :] = beyond
-        wide[q, PASSES:PASSES + ROWS, :] = flat[:, q * 128:(q + 1) * 128]
-        wide[q, PASSES + ROWS:, :] = beyond
+        wide[q, :CHUNKS, :] = beyond
+        wide[q, CHUNKS:CHUNKS + ROWS, :] = flat[:, q * 128:(q + 1) * 128]
+        wide[q, CHUNKS + ROWS:, :] = beyond
     for j in range(RIM):
         rim[j, :RHS, :] = jnp.broadcast_to(flat[j:j + 1], (RHS, WIDE))
         rim[j, RHS:, :] = jnp.broadcast_to(flat[ROWS - 1 - j:ROWS - j], (RHS, WIDE))
 
-    def level(e):
-        return [wide[q, pl.ds(e, CHUNKS, stride=DEPTH), :] for q in range(RUN)]
-
-    none = [jnp.zeros((CHUNKS, 128), F32)] * RUN
-    here, south = level(0), none
-    for e in range(TALL):
-        north = level(e + 1) if e + 1 < TALL else none
+    def level(b):
+        return [wide[q, pl.ds(CHUNKS + b, CHUNKS, stride=DEPTH), :] for q in range(RUN)]
+
+    south, here = level(-1), level(0)
+    for b in range(DEPTH):
+        north = level(b + 1)
         ahead, behind = beside(here)
-        rows = slice(e * CHUNKS, (e + 1) * CHUNKS)
+        rows = slice(b * CHUNKS, (b + 1) * CHUNKS)
         for q in range(RUN):
             cols = slice(q * 128, (q + 1) * 128)
             mid = 1.0 - here[q] * ((north[q] + south[q]) + (ahead[q] + behind[q]))
+            some = here[q] > 0.0
             coef[0, rows, cols] = mid
             coef[1, rows, cols] = here[q] * here[q]
-            if PASSES <= e < TALL - PASSES:
-                inner = slice((e - PASSES) * CHUNKS, (e - PASSES + 1) * CHUNKS)
-                some = here[q] > 0.0
-                last[0, inner, cols] = jnp.where(some, mid / jnp.where(some, here[q], 1.0), 0.0)
-                last[1, inner, cols] = here[q]
-        here, south = north, here
+            over[rows, cols] = jnp.where(some, mid / jnp.where(some, here[q], 1.0), 0.0)
+            root[rows, cols] = here[q]
+        south, here = here, north
 
 
 def faces(own, first, second):
     return pl.pallas_call(
         faces_kernel,
         out_shape=(
-            jax.ShapeDtypeStruct((2, TALL * CHUNKS, WIDE), F32),
             jax.ShapeDtypeStruct((2, ROWS, WIDE), F32),
+            jax.ShapeDtypeStruct((ROWS, WIDE), F32),
+            jax.ShapeDtypeStruct((ROWS, WIDE), F32),
             jax.ShapeDtypeStruct((RIM, 2 * RHS, WIDE), F32),
         ),
-        scratch_shapes=[pltpu.VMEM((RUN, ROWS + 8, 128), F32)],
-        compiler_params=params(16),
+        scratch_shapes=[pltpu.VMEM((RUN, ROWS + 2 * CHUNKS, 128), F32)],
+        compiler_params=params(12),
         cost_estimate=cost(1 << 30, 6 << 20),
         name="faces",
     )(own, first, second)
 
 
-def adjoint_kernel(got, last, roots, field, rim, inner, outer, facts_out, own, west, east):
+def surround(ref, r):
+    last = DEPTH * CHUNKS
+    ref[r, :CHUNKS, :] = pltpu.roll(ref[r, last:last + CHUNKS, :], 1, 0)
+    ref[r, last + CHUNKS:, :] = pltpu.roll(ref[r, CHUNKS:2 * CHUNKS, :], CHUNKS - 1, 0)
+
+
+def adjoint_kernel(got, root_any, roots, field, rim, inner, outer, facts_out, own, west, east, root, sem):
+    copy = pltpu.make_async_copy(root_any, root, sem)
+    copy.start()
     column, fact = iota((16, 128), 0), iota((16, 128), 1) - 120
     facts = mm(pick((fact == column) & (column < 5)), got[:, 128:256], NT)
     facts = facts + mm(pick((fact == column - 5) & (column >= 5) & (column < 10)), got[:, 256:384], NT)
@@ -241,6 +247,8 @@
     for r in range(RHS):
         total = mm(spread(0, r), own[...])
         before, after = mm(spread(5, r), west[...]), mm(spread(10, r), east[...])
+        if r == 0:
+            copy.wait()
         for q in range(RUN):
             cols = slice(q * 128, (q + 1) * 128)
             part = total[:, cols]
@@ -249,10 +257,12 @@
             if q in EASTERN:
                 at = EASTERN.index(q) * 128
                 part = part + after[:, at:at + 128]
-            field[r, :, cols] = part * last[1, :, cols]
+            field[r, CHUNKS:CHUNKS + ROWS, cols] = part * root[:, cols]
+        surround(field, r)
         for j in range(RIM):
-            rim[j, r:r + 1, :] = field[r, j * CHUNKS:j * CHUNKS + 1, :]
-            end = (DEPTH - j) * CHUNKS
+            at = (j + 1) * CHUNKS
+            rim[j, r:r + 1, :] = field[r, at:at + 1, :]
+            end = (DEPTH + 1 - j) * CHUNKS
             rim[j, RHS + r:RHS + r + 1, :] = field[r, end - 1:end, :]
     even = lax.axis_index("lat") % 2 == 0
     for base, ref in ((0, rim), (PASSES, roots)):
@@ -265,11 +275,13 @@
 EASTERN = [(EAST + i) % RUN for i in range(PASSES)]
 
 
-def adjoint(got, last, roots):
+def adjoint(got, root, roots):
+    vmem = pl.BlockSpec(memory_space=pltpu.VMEM)
     return pl.pallas_call(
         adjoint_kernel,
+        in_specs=[vmem, pl.BlockSpec(memory_space=pl.ANY), vmem],
         out_shape=(
-            jax.ShapeDtypeStruct((RHS, ROWS, WIDE), F32),
+            jax.ShapeDtypeStruct((RHS, TALL * CHUNKS, WIDE), F32),
             jax.ShapeDtypeStruct((RIM, 2 * RHS, WIDE), F32),
             jax.ShapeDtypeStruct((2 * PASSES, RHS, WIDE), F32),
             jax.ShapeDtypeStruct((2 * PASSES, RHS, WIDE), F32),
@@ -279,11 +291,13 @@
             pltpu.VMEM((TOTAL, WIDE), BF),
             pltpu.VMEM((TOTAL, PASSES * 128), BF),
             pltpu.VMEM((TOTAL, PASSES * 128), BF),
+            pltpu.VMEM((ROWS, WIDE), F32),
+            pltpu.SemaphoreType.DMA(()),
         ],
-        compiler_params=params(20),
+        compiler_params=params(16),
         cost_estimate=cost(5 << 30, 8 << 20),
         name="adjoint",
-    )(got, last, roots)
+    )(got, root, roots)
 
 
 def inside(q):
@@ -291,31 +305,23 @@
     return (e >= PASSES) & (e < EAST)
 
 
-def diffuse_kernel(field, coef, last, smooth, outer, ends, one, two):
-    side = 6 * CHUNKS
-    for r in range(RHS):
-        for e in range(PASSES):
-            rows = slice((DEPTH - PASSES + e) * CHUNKS, (DEPTH - PASSES + e + 1) * CHUNKS)
-            ends[r, e * CHUNKS:(e + 1) * CHUNKS, :] = pltpu.roll(field[r, rows, :], 1, 0)
-            at = side + (2 + e) * CHUNKS
-            ends[r, at:at + CHUNKS, :] = pltpu.roll(field[r, e * CHUNKS:(e + 1) * CHUNKS, :], CHUNKS - 1, 0)
-        ends[r, PASSES * CHUNKS:side, :] = field[r, :2 * CHUNKS, :]
-        ends[r, side:side + 2 * CHUNKS, :] = field[r, (DEPTH - 2) * CHUNKS:, :]
+def diffuse_kernel(field, coef, over, root, smooth, outer, one, two):
+    usual, final = (coef.at[0], coef.at[1]), (over, root)
 
     def rows_of(e):
         at = e * CHUNKS
         return pl.ds(at if isinstance(at, int) else pl.multiple_of(at, CHUNKS), CHUNKS)
 
-    def two_levels(ref, base, e, factor, lift, store):
+    def two_levels(ref, e, factor, store):
         def load(r, at, q):
-            return ref[r, rows_of(at + base), q * 128:(q + 1) * 128]
+            return ref[r, rows_of(at), q * 128:(q + 1) * 128]
 
         levels = (e, e + 1)
         turned_west = [[rolled(load(r, at, RUN - 1), SLOTS) for at in levels] for r in range(RHS)]
         turned_east = [[rolled(load(r, at, 0), -SLOTS) for at in levels] for r in range(RHS)]
         behind, here = [[[load(r, at, q) for at in levels] for r in range(RHS)] for q in (0, 1)]
         for q in [*range(1, RUN), 0]:
-            mid, near = [[factor[kind, rows_of(at + lift), q * 128:(q + 1) * 128] for at in levels] for kind in (0, 1)]
+            mid, near = [[kind[rows_of(at - 1), q * 128:(q + 1) * 128] for at in levels] for kind in factor]
             if q == 0:
                 behind = turned_west
                 here, ahead = [[[load(r, at, i) for at in levels] for r in range(RHS)] for i in (0, 1)]
@@ -330,27 +336,26 @@
                     store(r, q, i, mid[i] * here[r][i] + near[i] * total)
             behind, here = here, ahead
 
-    def sweep(ref, base, target, first, end, to=0, factor=coef, lift=0):
+    def sweep(ref, target, first, end, factor, to=0):
         def step(pair, _):
             e = first + 2 * pair
 
             def store(r, q, i, value):
                 target[r, rows_of(e + i + to), q * 128:(q + 1) * 128] = value
 
-            two_levels(ref, base, e, factor, lift, store)
+            two_levels(ref, e, factor, store)
             return 0
 
         lax.fori_loop(0, (end - first) // 2, step, 0, unroll=2)
 
-    sweep(ends, 0, one, 1, 5)
-    sweep(field, -PASSES, one, 5, TALL - 5)
-    sweep(ends, -28, one, TALL - 5, TALL - 1)
-    sweep(one, 0, two, 2, TALL - 2)
-    sweep(two, 0, one, 3, TALL - 3)
-    sweep(one, 0, outer, PASSES, 2 * PASSES, -PASSES, last, -PASSES)
-    sweep(one, 0, outer, DEPTH, DEPTH + PASSES, -DEPTH + PASSES, last, -PASSES)
-
-    def final(pair, _):
+    for ref, target in ((field, one), (one, two), (two, one)):
+        sweep(ref, target, 1, DEPTH + 1, usual)
+        for r in range(RHS):
+            surround(target, r)
+    sweep(one, outer, 1, PASSES + 1, final, -1)
+    sweep(one, outer, DEPTH + 1 - PASSES, DEPTH + 1, final, 2 * PASSES - 1 - DEPTH)
+
+    def rounded(pair, _):
         first = {}
 
         def store(r, q, i, value):
@@ -361,13 +366,13 @@
             at = pl.ds(pl.multiple_of(pair * 2 * CHUNKS, 2 * CHUNKS), 2 * CHUNKS)
             smooth[r, at, q * 128:(q + 1) * 128] = jnp.where(inside(q), both, 0.0).astype(BF)
 
-        two_levels(one, 0, 2 * PASSES + 2 * pair, last, -PASSES, store)
+        two_levels(one, PASSES + 1 + 2 * pair, final, store)
         return 0
 
-    lax.fori_loop(0, MIDDLE // (2 * CHUNKS), final, 0, unroll=2)
-
-
-def diffuse(field, coef, last):
+    lax.fori_loop(0, MIDDLE // (2 * CHUNKS), rounded, 0, unroll=2)
+
+
+def diffuse(field, coef, over, root):
     return pl.pallas_call(
         diffuse_kernel,
         out_shape=(
@@ -375,14 +380,13 @@
             jax.ShapeDtypeStruct((RHS, OUTER, WIDE), F32),
         ),
         scratch_shapes=[
-            pltpu.VMEM((RHS, 12 * CHUNKS, WIDE), F32),
             pltpu.VMEM((RHS, TALL * CHUNKS, WIDE), F32),
             pltpu.VMEM((RHS, TALL * CHUNKS, WIDE), F32),
         ],
-        compiler_params=params(24),
+        compiler_params=params(14),
         cost_estimate=cost(6 << 30, 8 << 20),
         name="diffuse",
-    )(field, coef, last)
+    )(field, coef, over, root)
 
 
 def finish_kernel(smooth, outer, rim, roots, inner, beyond, got, facts, out, border, values):
@@ -462,7 +466,7 @@
             pltpu.VMEM((RHS, OUTER, WIDE), BF),
             pltpu.VMEM((8, TOTAL), F32),
         ],
-        compiler_params=params(24),
+        compiler_params=params(16),
         cost_estimate=cost(3 << 30, 10 << 20),
         name="finish",
     )(smooth, outer, rim, roots, inner, beyond, got, facts)
@@ -482,7 +486,7 @@
     return pl.pallas_call(
         unpack_kernel,
         out_shape=jax.ShapeDtypeStruct((RHS, OBS), F32),
-        compiler_params=params(16),
+        compiler_params=params(8),
         name="unpack",
     )(values, target, rank)
 
@@ -499,12 +503,12 @@
     first = swap(diffusivity, "lon", False, True)
     second = swap(diffusivity, "lon", True, True)
     packed, first, second = lax.optimization_barrier((packed, first, second))
-    coef, last, roots = faces(diffusivity, first, second)
+    coef, over, root, roots = faces(diffusivity, first, second)
     got = lax.all_to_all(packed, ("lat", "lon"), split_axis=0, concat_axis=0, tiled=True)
-    field, rim, inner, beyond, facts = adjoint(got, last, roots)
+    field, rim, inner, beyond, facts = adjoint(got, root, roots)
     inner = swap(inner, "lat", False, False)
     beyond = swap(beyond, "lat", True, False)
-    smooth, outer = diffuse(field, coef, last)
+    smooth, outer = diffuse(field, coef, over, root)
     values = finish(smooth, outer, rim, roots, inner, beyond, got, facts)
     returned = lax.all_to_all(values, ("lat", "lon"), split_axis=0, concat_axis=0, tiled=True)
     return unpack(returned, target, rank).T

time: 88.5 us -> 88.3 us (level)
    unnamed x16 -> x18, local copies, waits for them, and re-layouts: 4.67 us -> 4.76 us
  transfers between devices with their start and end apart: 5 -> 5, of which waited for: 1 -> 1; matrix products, arithmetic and copies ran while one was open for 0% -> 0% of each run, Pallas kernels for 19% -> 18%
where the time goes in v3:
time: 88.3 us; the launch traced here: 88 us
  Pallas kernels  26.1 us (30%)
  waiting for transfers between devices  24.5 us (28%)
  starting transfers between devices  18.3 us (21%)
  blocking collectives  14.2 us (16%)
  local copies, waits for them, and re-layouts  4.76 us (5%)
    all_to_all x1, waiting for transfers between devices, body(): lax.all_to_all(packed, ('lat', 'lon'), split_axis=0, concat_axis=0, tiled...  24.5 us
    all_to_all x1, blocking collectives, body(): lax.all_to_all(values, ('lat', 'lon'), split_axis=0, concat_axis=0, tiled...  14.2 us
    ppermute x4, starting transfers between devices, swap(): return lax.ppermute(x, axis, pairs + [(j, i) for i, j in pairs])  11.2 us
    all_to_all x1, starting transfers between devices, body(): lax.all_to_all(packed, ('lat', 'lon'), split_axis=0, concat_axis=0, tiled...  7.08 us
    pallas_call x1, Pallas kernels, adjoint(): pl.pallas_call(adjoint_kernel, in_specs=[vmem, pl.BlockSpec(memory_space=...  6.05 us
    pallas_call x1, Pallas kernels, pack(): pl.pallas_call(pack_kernel, in_specs=[hbm] * 5, out_specs=(hbm, pl.BlockS...  5.95 us
    pallas_call x1, Pallas kernels, diffuse(): pl.pallas_call(diffuse_kernel, out_shape=(jax.ShapeDtypeStruct((RHS, MIDD...  5.7 us
    unnamed x18, local copies, waits for them, and re-layouts  4.76 us
  transfers between devices with their start and end apart: 5, of which 1 were waited for; matrix products, arithmetic and copies ran while one was open for 0% of the time, Pallas kernels for 18%

profile of v3, /device:TPU:1, one launch (start us, length us, event | category | flops | bytes accessed | tf_op | source)
XLA Modules:
  0.0 88.0 jit_solution(10329708039384114081)
XLA Ops:
  0.0 2.5 %collective-permute-start = (f32[256,128]{1,0:T(8,128)}, f32[256,128]{1,0:T(8,128)S(1)}, u32[]{:S(2)}, u32[]{:S(2)}) collective-permute-start(f32[256,128]{1,0:T(8,128)} %own.1), channel_id=1, source_target_pairs={{0,1},{2,3},{4,5},{6,7},{8,9},{10,11},{12,13},{14,15},{1,0},{3,2},... | collective-permute-start | bytes 393224 | tf_op jit(solution)/shard_map/ppermute | solution.py:497
  2.5 4.7 %collective-permute-start.1 = (f32[256,128]{1,0:T(8,128)}, f32[256,128]{1,0:T(8,128)S(1)}, u32[]{:S(2)}, u32[]{:S(2)}) collective-permute-start(f32[256,128]{1,0:T(8,128)} %own.1), channel_id=1, source_target_pairs={{1,2},{3,4},{5,6},{7,8},{9,10},{11,12},{13,14},{15,0},{2,1},{4,3},... | collective-permute-start | bytes 393224 | tf_op jit(solution)/shard_map/ppermute | solution.py:497
  7.2 5.9 %pack.1 = (bf16[1024,1152]{1,0:T(8,128)(2,1)}, f32[8,512]{1,0:T(8,128)}) custom-call(bf16[512,1024]{1,0:T(8,128)(2,1)} %prints_hbm.1, bf16[4,512]{1,0:T(4,128)(2,1)} %bitcast.18, s32[1,512]{1,0:T(1,128)} %bitcast.15, s32[1,512]{1,0:T(1,128)} %bitcast.19, s32[1,512]{1,0:T(1,128)} %bitcast.20), custom_call_target="tpu_custom_call" | custom-call | flops 1073741824 | bytes 3145728 | tf_op jit(solution)/shard_map/pack/pallas_call | solution.py:134
  13.1 0.0 collective-permute-done.first
  13.1 0.0 collective-permute-done.1.second
  13.1 0.0 copy-start.2
  13.1 7.1 %all-to-all-start = ((bf16[128,8,1152]{2,1,0:T(8,128)(2,1)}), bf16[128,8,1152]{2,1,0:T(8,128)(2,1)S(1)}, u32[]{:S(2)}, u32[]{:S(2)}) async-start(bf16[128,8,1152]{2,1,0:T(8,128)(2,1)} %bitcast.17), calls=%async_computation | async-start | bytes 4718592 | tf_op jit(solution)/shard_map/all_to_all | solution.py:507
  20.2 0.0 copy-done.2
  20.2 4.2 %faces.1 = (f32[2,256,1152]{2,1,0:T(8,128)S(1)}, f32[256,1152]{1,0:T(8,128)S(1)}, f32[256,1152]{1,0:T(8,128)S(1)}, f32[8,8,1152]{2,1,0:T(8,128)S(1)}) custom-call(f32[256,128]{1,0:T(8,128)S(1)} %copy-done.2, f32[256,128]{1,0:T(8,128)S(1)} %collective-permute-done.first, f32[256,128]{1,0:T(8,128)S(1)} %collective-permute-done.1.second), custom_call_target="tpu_custom_call" | custom-call | flops 1073741824 | bytes 6291456 | tf_op jit(solution)/shard_map/faces/pallas_call | solution.py:203
  24.4 1.4 %copy-done.3 = f32[2,256,1152]{2,1,0:T(8,128)} copy-done((f32[2,256,1152]{2,1,0:T(8,128)}, f32[2,256,1152]{2,1,0:T(8,128)S(1)}, u32[]{:S(2)}) %copy-start.3) | copy-done | bytes 2359320
  25.8 1.0 %copy-done.5 = f32[256,1152]{1,0:T(8,128)} copy-done((f32[256,1152]{1,0:T(8,128)}, f32[256,1152]{1,0:T(8,128)S(1)}, u32[]{:S(2)}) %copy-start.5) | copy-done | bytes 1179672
  26.8 1.0 %copy-done.7 = f32[256,1152]{1,0:T(8,128)} copy-done((f32[256,1152]{1,0:T(8,128)}, f32[256,1152]{1,0:T(8,128)S(1)}, u32[]{:S(2)}) %copy-start.7) | copy-done | bytes 1179672
  27.9 24.5 %all-to-all-done = bf16[128,8,1152]{2,1,0:T(8,128)(2,1)S(1)} async-done(((bf16[128,8,1152]{2,1,0:T(8,128)(2,1)}), bf16[128,8,1152]{2,1,0:T(8,128)(2,1)S(1)}, u32[]{:S(2)}, u32[]{:S(2)}) %all-to-all-start) | async-done | bytes 2359328 | tf_op jit(solution)/shard_map/all_to_all | solution.py:507
  52.4 1.3 %copy-done.8 = f32[256,1152]{1,0:T(8,128)S(1)} copy-done((f32[256,1152]{1,0:T(8,128)S(1)}, f32[256,1152]{1,0:T(8,128)}, u32[]{:S(2)}) %copy-start.8) | copy-done | bytes 1179672
  53.6 6.1 %adjoint.1 = (f32[4,272,1152]{2,1,0:T(8,128)S(1)}, f32[8,8,1152]{2,1,0:T(8,128)S(1)}, f32[8,4,1152]{2,1,0:T(4,128)S(1)}, f32[8,4,1152]{2,1,0:T(4,128)S(1)}, f32[16,1024]{1,0:T(8,128)S(1)}) custom-call(bf16[1024,1152]{1,0:T(8,128)(2,1)S(1)} %bitcast.11, f32[256,1152]{1,0:T(8,128)S(1)} %copy-done.8, f32[8,8,1152]{2,1,0:T(8,128)S(1)} %get-tuple-element.26.roots), custom_call_target="tpu_custom_call" | custom-call | flops 5368709120 | bytes 8388608 | tf_op jit(solution)/shard_map/adjoint/pallas_call | solution.py:280
  59.7 1.3 %collective-permute-start.2 = (f32[8,4,1152]{2,1,0:T(4,128)S(1)}, f32[8,4,1152]{2,1,0:T(4,128)S(1)}, u32[]{:S(2)}, u32[]{:S(2)}) collective-permute-start(f32[8,4,1152]{2,1,0:T(4,128)S(1)} %get-tuple-element.33), channel_id=1, source_target_pairs={{0,16},{32,48},{64,80},{96,112},{16,0},{48,32},{80,64},{112,96},{1... | collective-permute-start | bytes 442376 | tf_op jit(solution)/shard_map/ppermute | solution.py:497
  61.0 2.7 %collective-permute-start.3 = (f32[8,4,1152]{2,1,0:T(4,128)S(1)}, f32[8,4,1152]{2,1,0:T(4,128)S(1)}, u32[]{:S(2)}, u32[]{:S(2)}) collective-permute-start(f32[8,4,1152]{2,1,0:T(4,128)S(1)} %get-tuple-element.34), channel_id=1, source_target_pairs={{16,32},{48,64},{80,96},{32,16},{64,48},{96,80},{17,33},{49,65},{8... | collective-permute-start | bytes 442376 | tf_op jit(solution)/shard_map/ppermute | solution.py:497
  63.8 5.7 %diffuse.1 = (bf16[4,192,1152]{2,1,0:T(8,128)(2,1)S(1)}, f32[4,64,1152]{2,1,0:T(8,128)S(1)}) custom-call(f32[4,272,1152]{2,1,0:T(8,128)S(1)} %get-tuple-element.27.field, f32[2,256,1152]{2,1,0:T(8,128)S(1)} %copy-done.4, f32[256,1152]{1,0:T(8,128)S(1)} %copy-done.6, f32[256,1152]{1,0:T(8,128)S(1)} %copy-done.8), custom_call_target="tpu_custom_call" | custom-call | flops 6442450944 | bytes 8388608 | tf_op jit(solution)/shard_map/diffuse/pallas_call | solution.py:376
  69.5 0.0 collective-permute-done.2.inner
  69.5 0.0 collective-permute-done.3.beyond
  69.5 0.0 copy-start.1
  69.5 3.4 %finish.1 = f32[128,128]{1,0:T(8,128)S(1)} custom-call(bf16[4,192,1152]{2,1,0:T(8,128)(2,1)S(1)} %get-tuple-element.30.smooth, f32[4,64,1152]{2,1,0:T(8,128)S(1)} %get-tuple-element.31.outer, f32[8,8,1152]{2,1,0:T(8,128)S(1)} %get-tuple-element.32.rim, f32[8,8,1152]{2,1,0:T(8,128)S(1)} %get-tuple-element.26.roots, ...), custom_call_target="tpu_custom_call" | custom-call | flops 3221225472 | bytes 10485760 | tf_op jit(solution)/shard_map/finish/pallas_call | solution.py:462
  73.0 14.2 %all_to_all.22 = f32[128,1,128]{2,1,0:T(1,128)S(1)} all-to-all(f32[128,1,128]{2,1,0:T(1,128)S(1)} %bitcast.14), channel_id=1, replica_groups=mesh['lat'=8,'lon'=16] {'lat','lon'}, dimensions={0} | all-to-all | bytes 131072 | tf_op jit(solution)/shard_map/all_to_all | solution.py:513
  87.2 0.8 unpack.1
  (11 shorter events, 0.0 us)
Async XLA Ops:
  0.0 13.1 %collective-permute-start = (f32[256,128]{1,0:T(8,128)}, f32[256,128]{1,0:T(8,128)S(1)}, u32[]{:S(2)}, u32[]{:S(2)}) collective-permute-start(f32[256,128]{1,0:T(8,128)} %own.1), channel_id=1, source_target_pairs={{0,1},{2,3},{4,5},{6,7},{8,9},{10,11},{12,13},{14,15},{1,0},{3,2},... | collective-permute-start | bytes 393224 | tf_op jit(solution)/shard_map/ppermute | solution.py:497
  2.5 10.7 %collective-permute-start.1 = (f32[256,128]{1,0:T(8,128)}, f32[256,128]{1,0:T(8,128)S(1)}, u32[]{:S(2)}, u32[]{:S(2)}) collective-permute-start(f32[256,128]{1,0:T(8,128)} %own.1), channel_id=1, source_target_pairs={{1,2},{3,4},{5,6},{7,8},{9,10},{11,12},{13,14},{15,0},{2,1},{4,3},... | collective-permute-start | bytes 393224 | tf_op jit(solution)/shard_map/ppermute | solution.py:497
  13.1 7.1 %copy-start.2 = (f32[256,128]{1,0:T(8,128)S(1)}, f32[256,128]{1,0:T(8,128)}, u32[]{:S(2)}) copy-start(f32[256,128]{1,0:T(8,128)} %own.1) | copy-start | bytes 393220
  13.1 39.2 %all-to-all-start = ((bf16[128,8,1152]{2,1,0:T(8,128)(2,1)}), bf16[128,8,1152]{2,1,0:T(8,128)(2,1)S(1)}, u32[]{:S(2)}, u32[]{:S(2)}) async-start(bf16[128,8,1152]{2,1,0:T(8,128)(2,1)} %bitcast.17), calls=%async_computation | async-start | bytes 4718592 | tf_op jit(solution)/shard_map/all_to_all | solution.py:507
  24.4 1.4 %copy-start.3 = (f32[2,256,1152]{2,1,0:T(8,128)}, f32[2,256,1152]{2,1,0:T(8,128)S(1)}, u32[]{:S(2)}) copy-start(f32[2,256,1152]{2,1,0:T(8,128)S(1)} %get-tuple-element.28.coef) | copy-start | bytes 7077892
  25.8 1.0 %copy-start.5 = (f32[256,1152]{1,0:T(8,128)}, f32[256,1152]{1,0:T(8,128)S(1)}, u32[]{:S(2)}) copy-start(f32[256,1152]{1,0:T(8,128)S(1)} %get-tuple-element.29.over) | copy-start | bytes 3538948
  26.8 1.0 %copy-start.7 = (f32[256,1152]{1,0:T(8,128)}, f32[256,1152]{1,0:T(8,128)S(1)}, u32[]{:S(2)}) copy-start(f32[256,1152]{1,0:T(8,128)S(1)} %get-tuple-element.25.root_any.root) | copy-start | bytes 3538948
  52.4 1.3 %copy-start.8 = (f32[256,1152]{1,0:T(8,128)S(1)}, f32[256,1152]{1,0:T(8,128)}, u32[]{:S(2)}) copy-start(f32[256,1152]{1,0:T(8,128)} %copy-done.7) | copy-start | bytes 3538948
  53.6 10.1 %copy-start.4 = (f32[2,256,1152]{2,1,0:T(8,128)S(1)}, f32[2,256,1152]{2,1,0:T(8,128)}, u32[]{:S(2)}) copy-start(f32[2,256,1152]{2,1,0:T(8,128)} %copy-done.3) | copy-start | bytes 7077892
  53.6 10.2 %copy-start.6 = (f32[256,1152]{1,0:T(8,128)S(1)}, f32[256,1152]{1,0:T(8,128)}, u32[]{:S(2)}) copy-start(f32[256,1152]{1,0:T(8,128)} %copy-done.5) | copy-start | bytes 3538948
  59.7 9.8 %collective-permute-start.2 = (f32[8,4,1152]{2,1,0:T(4,128)S(1)}, f32[8,4,1152]{2,1,0:T(4,128)S(1)}, u32[]{:S(2)}, u32[]{:S(2)}) collective-permute-start(f32[8,4,1152]{2,1,0:T(4,128)S(1)} %get-tuple-element.33), channel_id=1, source_target_pairs={{0,16},{32,48},{64,80},{96,112},{16,0},{48,32},{80,64},{112,96},{1... | collective-permute-start | bytes 442376 | tf_op jit(solution)/shard_map/ppermute | solution.py:497
  61.0 8.5 %collective-permute-start.3 = (f32[8,4,1152]{2,1,0:T(4,128)S(1)}, f32[8,4,1152]{2,1,0:T(4,128)S(1)}, u32[]{:S(2)}, u32[]{:S(2)}) collective-permute-start(f32[8,4,1152]{2,1,0:T(4,128)S(1)} %get-tuple-element.34), channel_id=1, source_target_pairs={{16,32},{48,64},{80,96},{32,16},{64,48},{96,80},{17,33},{49,65},{8... | collective-permute-start | bytes 442376 | tf_op jit(solution)/shard_map/ppermute | solution.py:497
  69.5 17.6 %copy-start = (f32[8,512]{1,0:T(8,128)S(1)}, f32[8,512]{1,0:T(8,128)}, u32[]{:S(2)}) copy-start(f32[8,512]{1,0:T(8,128)} %get-tuple-element.36.rank) | copy-start | bytes 49156
  69.5 17.6 %copy-start.1 = (s32[512,1]{0,1:T(1,128)S(1)}, s32[512,1]{0,1:T(1,128)}, u32[]{:S(2)}) copy-start(s32[512,1]{0,1:T(1,128)} %param.8) | copy-start | bytes 6148

commit v4 on v3

--- a/solution.py
+++ b/solution.py
@@ -18,6 +18,7 @@
 DEPTH = ROWS // CHUNKS
 TALL = DEPTH + 2
 RUN = 9
+FRONT = 3
 SPAN = SLOTS * CLON
 WIDE = RUN * 128
 EAST = CLON + PASSES
@@ -61,7 +62,7 @@
 def lanes(shape, dim):
     lane = iota(shape, dim)
     q, k, s = lane // 128, lane % 128 // 8, lane % 8
-    return k * RUN + q, s, q, k
+    return k * RUN + q - FRONT, s, q, k
 
 
 def rolled(x, step):
@@ -84,17 +85,11 @@
     e, s, q, k = lanes((1, WIDE), 1)
     base = s * CLON + e
     source = jnp.where(e < PASSES, base + CLON - PASSES, jnp.where(e < EAST, base - PASSES, base - EAST))
-    source = jnp.where(e < EAST + PASSES, source, -1)
+    source = jnp.where((e >= 0) & (e < EAST + PASSES), source, -1)
     spread[...] = pick(iota((SPAN, WIDE), 0) == source)
     before = pick(iota((OBS, OBS), 0) < iota((OBS, OBS), 1))
     for copy in copies[:4]:
         copy.wait()
-    t = target[...]
-    hit = pick(iota((DEVICES, OBS), 0) == t)
-    earlier = mm(hit, before)
-    rank = jnp.sum(hit.astype(F32) * earlier, axis=0, keepdims=True)
-    rank_out[...] = jnp.broadcast_to(rank, (8, OBS))
-    place = t * CAP + rank.astype(jnp.int32)
     blk = block[...]
     meta[...] = jnp.zeros_like(meta)
     meta[0:RHS, :] = weights[...].astype(F32)
@@ -102,18 +97,23 @@
     meta[5:6, :] = slot[...].astype(F32)
     facts = meta[...].astype(BF)
     slots = mm(facts, pick(iota((8, 128), 0) == 5), TN).astype(BF)
-    where = pick(iota((TOTAL, OBS), 0) == place)
+    t = target[...]
+    hit = pick(iota((DEVICES, OBS), 0) == t)
+    earlier = mm(hit, before)
     copies[4].wait()
     for s in range(SLOTS):
         live = slots >= jnp.asarray(s, BF)
         piece = prints[:, s * CLON:(s + 1) * CLON]
         masked[:, s * CLON:(s + 1) * CLON] = jnp.where(live, piece, jnp.zeros_like(piece))
     e, s, q, k = lanes((1, WIDE), 1)
-    fact = jnp.where((k == 15) & (q >= 1) & (q <= 3) & (s < 5), s, -1)
+    fact = jnp.where((k == 0) & (q < FRONT) & (s < 5), s, -1)
     wide[...] = (mm(masked[...], spread[...]) + mm(facts, pick(iota((8, WIDE), 0) == fact), TN)).astype(BF)
+    rank = jnp.sum(hit.astype(F32) * earlier, axis=0, keepdims=True)
+    rank_out[...] = jnp.broadcast_to(rank, (8, OBS))
+    where = pick(iota((TOTAL, OBS), 0) == t * CAP + rank.astype(jnp.int32))
     e, s, q, k = lanes((1, 1, WIDE), 2)
-    from_west = (e < PASSES) | ((k == 15) & (q == 2))
-    from_east = ((e >= EAST) & (e < EAST + PASSES)) | ((k == 15) & (q == 3))
+    from_west = ((e >= 0) & (e < PASSES)) | ((k == 0) & (q == 1))
+    from_east = ((e >= EAST) & (e < EAST + PASSES)) | ((k == 0) & (q == 2))
     sends = []
     size = TOTAL // PIECES
     for i in range(PIECES):
@@ -170,7 +170,7 @@
     left = jnp.where(even, second[...], first[...])
     right = jnp.where(even, first[...], second[...])
     flat = place(own[...], (e >= PASSES) & (e < EAST), -PASSES)
-    flat = flat + (place(left, e < PASSES, CLON - PASSES) + place(right, (e >= EAST) & (e < EAST + PASSES), -EAST))
+    flat = flat + (place(left, (e >= 0) & (e < PASSES), CLON - PASSES) + place(right, (e >= EAST) & (e < EAST + PASSES), -EAST))
     beyond = jnp.zeros((CHUNKS, 128), F32)
     for q in range(RUN):
         wide[q, :CHUNKS, :] = beyond
@@ -215,55 +215,39 @@
     )(own, first, second)
 
 
-def surround(ref, r):
-    last = DEPTH * CHUNKS
-    ref[r, :CHUNKS, :] = pltpu.roll(ref[r, last:last + CHUNKS, :], 1, 0)
-    ref[r, last + CHUNKS:, :] = pltpu.roll(ref[r, CHUNKS:2 * CHUNKS, :], CHUNKS - 1, 0)
-
-
-def adjoint_kernel(got, root_any, roots, field, rim, inner, outer, facts_out, own, west, east, root, sem):
-    copy = pltpu.make_async_copy(root_any, root, sem)
-    copy.start()
-    column, fact = iota((16, 128), 0), iota((16, 128), 1) - 120
-    facts = mm(pick((fact == column) & (column < 5)), got[:, 128:256], NT)
-    facts = facts + mm(pick((fact == column - 5) & (column >= 5) & (column < 10)), got[:, 256:384], NT)
-    facts = facts + mm(pick((fact == column - 10) & (column >= 10) & (column < 15)), got[:, 384:512], NT)
+def adjoint_kernel(got, roots, field, rim, inner, outer, facts_out):
+    column, lane = iota((16, 128), 0), iota((16, 128), 1)
+    facts = jnp.zeros((16, TOTAL), F32)
+    for i in range(FRONT):
+        mine = (lane == column - 5 * i) & (column >= 5 * i) & (column < 5 * i + 5)
+        facts = facts + mm(pick(mine), got[:, i * 128:(i + 1) * 128], NT)
     facts_out[...] = facts
-    for q in range(RUN):
-        piece = got[:, q * 128:(q + 1) * 128]
-        e = (iota((1, 128), 1) // 8) * RUN + q
-        ones = lambda cond: jnp.broadcast_to(pick(cond), piece.shape)
-        own[:, q * 128:(q + 1) * 128] = piece * ones((e >= PASSES) & (e < EAST))
-        if q < PASSES:
-            west[:, q * 128:(q + 1) * 128] = piece * ones(e < PASSES)
-        if q in EASTERN:
-            at = EASTERN.index(q) * 128
-            east[:, at:at + 128] = piece * ones((e >= EAST) & (e < EAST + PASSES))
     row = iota((ROWS, TOTAL), 0).astype(F32)
 
     def spread(first, r):
         return jnp.where(row == facts[first + RHS:first + RHS + 1], facts[first + r:first + r + 1], 0.0).astype(BF)
 
+    lane = iota((1, 128), 1)
+    end = FRONT + PASSES
     for r in range(RHS):
-        total = mm(spread(0, r), own[...])
-        before, after = mm(spread(5, r), west[...]), mm(spread(10, r), east[...])
-        if r == 0:
-            copy.wait()
+        total = mm(spread(0, r), got[...])
+        before = mm(spread(5, r), got[:, FRONT * 128:end * 128])
+        after = mm(spread(10, r), got[:, :PASSES * 128])
         for q in range(RUN):
             cols = slice(q * 128, (q + 1) * 128)
             part = total[:, cols]
+            if FRONT <= q < end:
+                part = jnp.where(lane < SLOTS, before[:, (q - FRONT) * 128:(q - FRONT + 1) * 128], part)
             if q < PASSES:
-                part = part + before[:, cols]
-            if q in EASTERN:
-                at = EASTERN.index(q) * 128
-                part = part + after[:, at:at + 128]
-            field[r, CHUNKS:CHUNKS + ROWS, cols] = part * root[:, cols]
-        surround(field, r)
+                part = jnp.where(lane >= 128 - SLOTS, after[:, cols], part)
+            field[r, :, cols] = part
         for j in range(RIM):
-            at = (j + 1) * CHUNKS
+            at = j * CHUNKS
             rim[j, r:r + 1, :] = field[r, at:at + 1, :]
-            end = (DEPTH + 1 - j) * CHUNKS
-            rim[j, RHS + r:RHS + r + 1, :] = field[r, end - 1:end, :]
+            at = (DEPTH - j) * CHUNKS - 1
+            rim[j, RHS + r:RHS + r + 1, :] = field[r, at:at + 1, :]
+    for j in range(RIM):
+        rim[j] = rim[j] * roots[j]
     even = lax.axis_index("lat") % 2 == 0
     for base, ref in ((0, rim), (PASSES, roots)):
         for j in range(PASSES):
@@ -272,37 +256,31 @@
             outer[base + j] = jnp.where(even, low, high)
 
 
-EASTERN = [(EAST + i) % RUN for i in range(PASSES)]
-
-
-def adjoint(got, root, roots):
-    vmem = pl.BlockSpec(memory_space=pltpu.VMEM)
+def adjoint(got, roots):
     return pl.pallas_call(
         adjoint_kernel,
-        in_specs=[vmem, pl.BlockSpec(memory_space=pl.ANY), vmem],
         out_shape=(
-            jax.ShapeDtypeStruct((RHS, TALL * CHUNKS, WIDE), F32),
+            jax.ShapeDtypeStruct((RHS, ROWS, WIDE), F32),
             jax.ShapeDtypeStruct((RIM, 2 * RHS, WIDE), F32),
             jax.ShapeDtypeStruct((2 * PASSES, RHS, WIDE), F32),
             jax.ShapeDtypeStruct((2 * PASSES, RHS, WIDE), F32),
             jax.ShapeDtypeStruct((16, TOTAL), F32),
         ),
-        scratch_shapes=[
-            pltpu.VMEM((TOTAL, WIDE), BF),
-            pltpu.VMEM((TOTAL, PASSES * 128), BF),
-            pltpu.VMEM((TOTAL, PASSES * 128), BF),
-            pltpu.VMEM((ROWS, WIDE), F32),
-            pltpu.SemaphoreType.DMA(()),
-        ],
         compiler_params=params(16),
         cost_estimate=cost(5 << 30, 8 << 20),
         name="adjoint",
-    )(got, root, roots)
+    )(got, roots)
 
 
 def inside(q):
-    e = (iota((1, 128), 1) // 8) * RUN + q
+    e = (iota((1, 128), 1) // 8) * RUN + q - FRONT
     return (e >= PASSES) & (e < EAST)
+
+
+def surround(ref, r):
+    last = DEPTH * CHUNKS
+    ref[r, :CHUNKS, :] = pltpu.roll(ref[r, last:last + CHUNKS, :], 1, 0)
+    ref[r, last + CHUNKS:, :] = pltpu.roll(ref[r, CHUNKS:2 * CHUNKS, :], CHUNKS - 1, 0)
 
 
 def diffuse_kernel(field, coef, over, root, smooth, outer, one, two):
@@ -348,7 +326,18 @@
 
         lax.fori_loop(0, (end - first) // 2, step, 0, unroll=2)
 
-    for ref, target in ((field, one), (one, two), (two, one)):
+    def scale(e, _):
+        for q in range(RUN):
+            cols = slice(q * 128, (q + 1) * 128)
+            factor = root[rows_of(e), cols]
+            for r in range(RHS):
+                two[r, rows_of(e + 1), cols] = field[r, rows_of(e), cols] * factor
+        return 0
+
+    lax.fori_loop(0, DEPTH, scale, 0, unroll=2)
+    for r in range(RHS):
+        surround(two, r)
+    for ref, target in ((two, one), (one, two), (two, one)):
         sweep(ref, target, 1, DEPTH + 1, usual)
         for r in range(RHS):
             surround(target, r)
@@ -505,7 +494,7 @@
     packed, first, second = lax.optimization_barrier((packed, first, second))
     coef, over, root, roots = faces(diffusivity, first, second)
     got = lax.all_to_all(packed, ("lat", "lon"), split_axis=0, concat_axis=0, tiled=True)
-    field, rim, inner, beyond, facts = adjoint(got, root, roots)
+    field, rim, inner, beyond, facts = adjoint(got, roots)
     inner = swap(inner, "lat", False, False)
     beyond = swap(beyond, "lat", True, False)
     smooth, outer = diffuse(field, coef, over, root)

time: 88.3 us -> 86.8 us (0.983)
  local copies, waits for them, and re-layouts: 4.76 us -> 3.5 us
    unnamed x18, local copies, waits for them, and re-layouts: 4.76 us -> 3.5 us
  transfers between devices with their start and end apart: 5 -> 5, of which waited for: 1 -> 1; matrix products, arithmetic and copies ran while one was open for 0% -> 0% of each run, Pallas kernels for 18% -> 19%
where the time goes in v4:
time: 86.8 us; the launch traced here: 86.6 us
  Pallas kernels  26.1 us (30%)
  waiting for transfers between devices  24.5 us (28%)
  starting transfers between devices  18.1 us (21%)
  blocking collectives  14.2 us (16%)
  local copies, waits for them, and re-layouts  3.5 us (4%)
    all_to_all x1, waiting for transfers between devices, body(): lax.all_to_all(packed, ('lat', 'lon'), split_axis=0, concat_axis=0, tiled...  24.5 us
    all_to_all x1, blocking collectives, body(): lax.all_to_all(values, ('lat', 'lon'), split_axis=0, concat_axis=0, tiled...  14.2 us
    ppermute x4, starting transfers between devices, swap(): return lax.ppermute(x, axis, pairs + [(j, i) for i, j in pairs])  11 us
    all_to_all x1, starting transfers between devices, body(): lax.all_to_all(packed, ('lat', 'lon'), split_axis=0, concat_axis=0, tiled...  7.14 us
    pallas_call x1, Pallas kernels, diffuse(): pl.pallas_call(diffuse_kernel, out_shape=(jax.ShapeDtypeStruct((RHS, MIDD...  6.29 us
    pallas_call x1, Pallas kernels, pack(): pl.pallas_call(pack_kernel, in_specs=[hbm] * 5, out_specs=(hbm, pl.BlockS...  5.88 us
    pallas_call x1, Pallas kernels, adjoint(): pl.pallas_call(adjoint_kernel, out_shape=(jax.ShapeDtypeStruct((RHS, ROWS...  5.56 us
    pallas_call x1, Pallas kernels, faces(): pl.pallas_call(faces_kernel, out_shape=(jax.ShapeDtypeStruct((2, ROWS, WI...  4.12 us
  transfers between devices with their start and end apart: 5, of which 1 were waited for; matrix products, arithmetic and copies ran while one was open for 0% of the time, Pallas kernels for 19%

profile of v4, /device:TPU:1, one launch (start us, length us, event | category | flops | bytes accessed | tf_op | source)
XLA Modules:
  0.0 86.6 jit_solution(18213688229052238006)
XLA Ops:
  0.0 2.5 %collective-permute-start = (f32[256,128]{1,0:T(8,128)}, f32[256,128]{1,0:T(8,128)S(1)}, u32[]{:S(2)}, u32[]{:S(2)}) collective-permute-start(f32[256,128]{1,0:T(8,128)} %own.1), channel_id=1, source_target_pairs={{0,1},{2,3},{4,5},{6,7},{8,9},{10,11},{12,13},{14,15},{1,0},{3,2},... | collective-permute-start | bytes 393224 | tf_op jit(solution)/shard_map/ppermute | solution.py:486
  2.5 4.7 %collective-permute-start.1 = (f32[256,128]{1,0:T(8,128)}, f32[256,128]{1,0:T(8,128)S(1)}, u32[]{:S(2)}, u32[]{:S(2)}) collective-permute-start(f32[256,128]{1,0:T(8,128)} %own.1), channel_id=1, source_target_pairs={{1,2},{3,4},{5,6},{7,8},{9,10},{11,12},{13,14},{15,0},{2,1},{4,3},... | collective-permute-start | bytes 393224 | tf_op jit(solution)/shard_map/ppermute | solution.py:486
  7.2 5.9 %pack.1 = (bf16[1024,1152]{1,0:T(8,128)(2,1)}, f32[8,512]{1,0:T(8,128)}) custom-call(bf16[512,1024]{1,0:T(8,128)(2,1)} %prints_hbm.1, bf16[4,512]{1,0:T(4,128)(2,1)} %bitcast.18, s32[1,512]{1,0:T(1,128)} %bitcast.15, s32[1,512]{1,0:T(1,128)} %bitcast.19, s32[1,512]{1,0:T(1,128)} %bitcast.20), custom_call_target="tpu_custom_call" | custom-call | flops 1073741824 | bytes 3145728 | tf_op jit(solution)/shard_map/pack/pallas_call | solution.py:134
  13.1 0.0 collective-permute-done.first
  13.1 0.0 collective-permute-done.1.second
  13.1 0.0 copy-start.2
  13.1 7.1 %all-to-all-start = ((bf16[128,8,1152]{2,1,0:T(8,128)(2,1)}), bf16[128,8,1152]{2,1,0:T(8,128)(2,1)S(1)}, u32[]{:S(2)}, u32[]{:S(2)}) async-start(bf16[128,8,1152]{2,1,0:T(8,128)(2,1)} %bitcast.17), calls=%async_computation | async-start | bytes 4718592 | tf_op jit(solution)/shard_map/all_to_all | solution.py:496
  20.2 0.0 copy-done.2
  20.2 4.1 %faces.1 = (f32[2,256,1152]{2,1,0:T(8,128)S(1)}, f32[256,1152]{1,0:T(8,128)S(1)}, f32[256,1152]{1,0:T(8,128)S(1)}, f32[8,8,1152]{2,1,0:T(8,128)S(1)}) custom-call(f32[256,128]{1,0:T(8,128)S(1)} %copy-done.2, f32[256,128]{1,0:T(8,128)S(1)} %collective-permute-done.first, f32[256,128]{1,0:T(8,128)S(1)} %collective-permute-done.1.second), custom_call_target="tpu_custom_call" | custom-call | flops 1073741824 | bytes 6291456 | tf_op jit(solution)/shard_map/faces/pallas_call | solution.py:203
  24.4 1.4 %copy-done.3 = f32[2,256,1152]{2,1,0:T(8,128)} copy-done((f32[2,256,1152]{2,1,0:T(8,128)}, f32[2,256,1152]{2,1,0:T(8,128)S(1)}, u32[]{:S(2)}) %copy-start.3) | copy-done | bytes 2359320
  25.8 1.0 %copy-done.5 = f32[256,1152]{1,0:T(8,128)} copy-done((f32[256,1152]{1,0:T(8,128)}, f32[256,1152]{1,0:T(8,128)S(1)}, u32[]{:S(2)}) %copy-start.5) | copy-done | bytes 1179672
  26.8 1.0 %copy-done.7 = f32[256,1152]{1,0:T(8,128)} copy-done((f32[256,1152]{1,0:T(8,128)}, f32[256,1152]{1,0:T(8,128)S(1)}, u32[]{:S(2)}) %copy-start.7) | copy-done | bytes 1179672
  27.9 24.5 %all-to-all-done = bf16[128,8,1152]{2,1,0:T(8,128)(2,1)S(1)} async-done(((bf16[128,8,1152]{2,1,0:T(8,128)(2,1)}), bf16[128,8,1152]{2,1,0:T(8,128)(2,1)S(1)}, u32[]{:S(2)}, u32[]{:S(2)}) %all-to-all-start) | async-done | bytes 2359328 | tf_op jit(solution)/shard_map/all_to_all | solution.py:496
  52.4 5.6 %adjoint.1 = (f32[4,256,1152]{2,1,0:T(8,128)S(1)}, f32[8,8,1152]{2,1,0:T(8,128)S(1)}, f32[8,4,1152]{2,1,0:T(4,128)S(1)}, f32[8,4,1152]{2,1,0:T(4,128)S(1)}, f32[16,1024]{1,0:T(8,128)S(1)}) custom-call(bf16[1024,1152]{1,0:T(8,128)(2,1)S(1)} %bitcast.11, f32[8,8,1152]{2,1,0:T(8,128)S(1)} %get-tuple-element.25.roots), custom_call_target="tpu_custom_call" | custom-call | flops 5368709120 | bytes 8388608 | tf_op jit(solution)/shard_map/adjoint/pallas_call | solution.py:260
  57.9 1.4 %collective-permute-start.2 = (f32[8,4,1152]{2,1,0:T(4,128)S(1)}, f32[8,4,1152]{2,1,0:T(4,128)S(1)}, u32[]{:S(2)}, u32[]{:S(2)}) collective-permute-start(f32[8,4,1152]{2,1,0:T(4,128)S(1)} %get-tuple-element.33), channel_id=1, source_target_pairs={{0,16},{32,48},{64,80},{96,112},{16,0},{48,32},{80,64},{112,96},{1... | collective-permute-start | bytes 442376 | tf_op jit(solution)/shard_map/ppermute | solution.py:486
  59.3 2.5 %collective-permute-start.3 = (f32[8,4,1152]{2,1,0:T(4,128)S(1)}, f32[8,4,1152]{2,1,0:T(4,128)S(1)}, u32[]{:S(2)}, u32[]{:S(2)}) collective-permute-start(f32[8,4,1152]{2,1,0:T(4,128)S(1)} %get-tuple-element.34), channel_id=1, source_target_pairs={{16,32},{48,64},{80,96},{32,16},{64,48},{96,80},{17,33},{49,65},{8... | collective-permute-start | bytes 442376 | tf_op jit(solution)/shard_map/ppermute | solution.py:486
  61.8 6.3 %diffuse.1 = (bf16[4,192,1152]{2,1,0:T(8,128)(2,1)S(1)}, f32[4,64,1152]{2,1,0:T(8,128)S(1)}) custom-call(f32[4,256,1152]{2,1,0:T(8,128)S(1)} %get-tuple-element.26.field, f32[2,256,1152]{2,1,0:T(8,128)S(1)} %copy-done.4, f32[256,1152]{1,0:T(8,128)S(1)} %copy-done.6, f32[256,1152]{1,0:T(8,128)S(1)} %copy-done.8), custom_call_target="tpu_custom_call" | custom-call | flops 6442450944 | bytes 8388608 | tf_op jit(solution)/shard_map/diffuse/pallas_call | solution.py:365
  68.1 0.0 collective-permute-done.2.inner
  68.1 0.0 collective-permute-done.3.beyond
  68.1 0.0 copy-start.1
  68.1 3.4 %finish.1 = f32[128,128]{1,0:T(8,128)S(1)} custom-call(bf16[4,192,1152]{2,1,0:T(8,128)(2,1)S(1)} %get-tuple-element.30.smooth, f32[4,64,1152]{2,1,0:T(8,128)S(1)} %get-tuple-element.31.outer, f32[8,8,1152]{2,1,0:T(8,128)S(1)} %get-tuple-element.32.rim, f32[8,8,1152]{2,1,0:T(8,128)S(1)} %get-tuple-element.25.roots, ...), custom_call_target="tpu_custom_call" | custom-call | flops 3221225472 | bytes 10485760 | tf_op jit(solution)/shard_map/finish/pallas_call | solution.py:451
  71.6 14.2 %all_to_all.22 = f32[128,1,128]{2,1,0:T(1,128)S(1)} all-to-all(f32[128,1,128]{2,1,0:T(1,128)S(1)} %bitcast.14), channel_id=1, replica_groups=mesh['lat'=8,'lon'=16] {'lat','lon'}, dimensions={0} | all-to-all | bytes 131072 | tf_op jit(solution)/shard_map/all_to_all | solution.py:502
  85.8 0.0 copy-done
  85.8 0.8 unpack.1
  (11 shorter events, 0.0 us)
Async XLA Ops:
  0.0 13.1 %collective-permute-start = (f32[256,128]{1,0:T(8,128)}, f32[256,128]{1,0:T(8,128)S(1)}, u32[]{:S(2)}, u32[]{:S(2)}) collective-permute-start(f32[256,128]{1,0:T(8,128)} %own.1), channel_id=1, source_target_pairs={{0,1},{2,3},{4,5},{6,7},{8,9},{10,11},{12,13},{14,15},{1,0},{3,2},... | collective-permute-start | bytes 393224 | tf_op jit(solution)/shard_map/ppermute | solution.py:486
  2.5 10.6 %collective-permute-start.1 = (f32[256,128]{1,0:T(8,128)}, f32[256,128]{1,0:T(8,128)S(1)}, u32[]{:S(2)}, u32[]{:S(2)}) collective-permute-start(f32[256,128]{1,0:T(8,128)} %own.1), channel_id=1, source_target_pairs={{1,2},{3,4},{5,6},{7,8},{9,10},{11,12},{13,14},{15,0},{2,1},{4,3},... | collective-permute-start | bytes 393224 | tf_op jit(solution)/shard_map/ppermute | solution.py:486
  13.1 7.2 %copy-start.2 = (f32[256,128]{1,0:T(8,128)S(1)}, f32[256,128]{1,0:T(8,128)}, u32[]{:S(2)}) copy-start(f32[256,128]{1,0:T(8,128)} %own.1) | copy-start | bytes 393220
  13.1 39.3 %all-to-all-start = ((bf16[128,8,1152]{2,1,0:T(8,128)(2,1)}), bf16[128,8,1152]{2,1,0:T(8,128)(2,1)S(1)}, u32[]{:S(2)}, u32[]{:S(2)}) async-start(bf16[128,8,1152]{2,1,0:T(8,128)(2,1)} %bitcast.17), calls=%async_computation | async-start | bytes 4718592 | tf_op jit(solution)/shard_map/all_to_all | solution.py:496
  24.4 1.4 %copy-start.3 = (f32[2,256,1152]{2,1,0:T(8,128)}, f32[2,256,1152]{2,1,0:T(8,128)S(1)}, u32[]{:S(2)}) copy-start(f32[2,256,1152]{2,1,0:T(8,128)S(1)} %get-tuple-element.27.coef) | copy-start | bytes 7077892
  25.8 1.0 %copy-start.5 = (f32[256,1152]{1,0:T(8,128)}, f32[256,1152]{1,0:T(8,128)S(1)}, u32[]{:S(2)}) copy-start(f32[256,1152]{1,0:T(8,128)S(1)} %get-tuple-element.28.over) | copy-start | bytes 3538948
  26.8 1.0 %copy-start.7 = (f32[256,1152]{1,0:T(8,128)}, f32[256,1152]{1,0:T(8,128)S(1)}, u32[]{:S(2)}) copy-start(f32[256,1152]{1,0:T(8,128)S(1)} %get-tuple-element.29.root) | copy-start | bytes 3538948
  52.4 9.4 %copy-start.4 = (f32[2,256,1152]{2,1,0:T(8,128)S(1)}, f32[2,256,1152]{2,1,0:T(8,128)}, u32[]{:S(2)}) copy-start(f32[2,256,1152]{2,1,0:T(8,128)} %copy-done.3) | copy-start | bytes 7077892
  52.4 9.4 %copy-start.6 = (f32[256,1152]{1,0:T(8,128)S(1)}, f32[256,1152]{1,0:T(8,128)}, u32[]{:S(2)}) copy-start(f32[256,1152]{1,0:T(8,128)} %copy-done.5) | copy-start | bytes 3538948
  52.4 9.4 %copy-start.8 = (f32[256,1152]{1,0:T(8,128)S(1)}, f32[256,1152]{1,0:T(8,128)}, u32[]{:S(2)}) copy-start(f32[256,1152]{1,0:T(8,128)} %copy-done.7) | copy-start | bytes 3538948
  57.9 10.2 %collective-permute-start.2 = (f32[8,4,1152]{2,1,0:T(4,128)S(1)}, f32[8,4,1152]{2,1,0:T(4,128)S(1)}, u32[]{:S(2)}, u32[]{:S(2)}) collective-permute-start(f32[8,4,1152]{2,1,0:T(4,128)S(1)} %get-tuple-element.33), channel_id=1, source_target_pairs={{0,16},{32,48},{64,80},{96,112},{16,0},{48,32},{80,64},{112,96},{1... | collective-permute-start | bytes 442376 | tf_op jit(solution)/shard_map/ppermute | solution.py:486
  59.3 8.8 %collective-permute-start.3 = (f32[8,4,1152]{2,1,0:T(4,128)S(1)}, f32[8,4,1152]{2,1,0:T(4,128)S(1)}, u32[]{:S(2)}, u32[]{:S(2)}) collective-permute-start(f32[8,4,1152]{2,1,0:T(4,128)S(1)} %get-tuple-element.34), channel_id=1, source_target_pairs={{16,32},{48,64},{80,96},{32,16},{64,48},{96,80},{17,33},{49,65},{8... | collective-permute-start | bytes 442376 | tf_op jit(solution)/shard_map/ppermute | solution.py:486
  68.1 17.6 %copy-start = (f32[8,512]{1,0:T(8,128)S(1)}, f32[8,512]{1,0:T(8,128)}, u32[]{:S(2)}) copy-start(f32[8,512]{1,0:T(8,128)} %get-tuple-element.36.rank) | copy-start | bytes 49156
  68.1 17.6 %copy-start.1 = (s32[512,1]{0,1:T(1,128)S(1)}, s32[512,1]{0,1:T(1,128)}, u32[]{:S(2)}) copy-start(s32[512,1]{0,1:T(1,128)} %param.8) | copy-start | bytes 6148

commit v5 on v4

--- a/solution.py
+++ b/solution.py
@@ -224,22 +224,31 @@
     facts_out[...] = facts
     row = iota((ROWS, TOTAL), 0).astype(F32)
 
-    def spread(first, r):
-        return jnp.where(row == facts[first + RHS:first + RHS + 1], facts[first + r:first + r + 1], 0.0).astype(BF)
-
+    def border(first_tile, first_lane, tile, fact):
+        source, lane = iota((PASSES * 128, 128), 0), iota((PASSES * 128, 128), 1)
+        take = source == lane % 32 // SLOTS * 128 + first_lane + lane % SLOTS
+        cells = mm(got[:, first_tile * 128:(first_tile + PASSES) * 128], pick(take))
+        fan = pick(iota((128, 128), 0) == iota((128, 128), 1) // 32)
+        cells = cells * mm(got[:, tile * 128:(tile + 1) * 128], fan)
+        high = cells.astype(BF)
+        low = (cells - high.astype(F32)).astype(BF)
+        both = mm(pick(row == facts[fact:fact + 1]), jnp.concatenate([high, low], axis=1))
+        return both[:, :128] + both[:, 128:]
+
+    before = border(FRONT, 0, 1, 9)
+    after = border(0, 128 - SLOTS, 2, 14)
+    mine = row == facts[RHS:RHS + 1]
     lane = iota((1, 128), 1)
     end = FRONT + PASSES
     for r in range(RHS):
-        total = mm(spread(0, r), got[...])
-        before = mm(spread(5, r), got[:, FRONT * 128:end * 128])
-        after = mm(spread(10, r), got[:, :PASSES * 128])
+        total = mm(jnp.where(mine, facts[r:r + 1], 0.0).astype(BF), got[...])
         for q in range(RUN):
             cols = slice(q * 128, (q + 1) * 128)
             part = total[:, cols]
             if FRONT <= q < end:
-                part = jnp.where(lane < SLOTS, before[:, (q - FRONT) * 128:(q - FRONT + 1) * 128], part)
+                part = jnp.where(lane < SLOTS, rolled(before, -(r * 32 + (q - FRONT) * SLOTS)), part)
             if q < PASSES:
-                part = jnp.where(lane >= 128 - SLOTS, after[:, cols], part)
+                part = jnp.where(lane >= 128 - SLOTS, rolled(after, -(r * 32 + (q + 1) * SLOTS)), part)
             field[r, :, cols] = part
         for j in range(RIM):
             at = j * CHUNKS

time: 86.8 us -> 86.2 us (level)
  Pallas kernels: 26.1 us -> 25.2 us
    pallas_call x1, Pallas kernels: 5.56 us -> 4.67 us  [adjoint(): pl.pallas_call(adjoint_kernel, out_shape=(jax.ShapeDtypeStruct((RHS, ROWS...]
where the time goes in v5:
time: 86.2 us; the launch traced here: 85.9 us
  Pallas kernels  25.2 us (29%)
  waiting for transfers between devices  24.5 us (28%)
  starting transfers between devices  18.4 us (21%)
  blocking collectives  14.2 us (16%)
  local copies, waits for them, and re-layouts  3.5 us (4%)
    all_to_all x1, waiting for transfers between devices, body(): lax.all_to_all(packed, ('lat', 'lon'), split_axis=0, concat_axis=0, tiled...  24.5 us
    all_to_all x1, blocking collectives, body(): lax.all_to_all(values, ('lat', 'lon'), split_axis=0, concat_axis=0, tiled...  14.2 us
    ppermute x4, starting transfers between devices, swap(): return lax.ppermute(x, axis, pairs + [(j, i) for i, j in pairs])  11.2 us
    all_to_all x1, starting transfers between devices, body(): lax.all_to_all(packed, ('lat', 'lon'), split_axis=0, concat_axis=0, tiled...  7.14 us
    pallas_call x1, Pallas kernels, diffuse(): pl.pallas_call(diffuse_kernel, out_shape=(jax.ShapeDtypeStruct((RHS, MIDD...  6.29 us
    pallas_call x1, Pallas kernels, pack(): pl.pallas_call(pack_kernel, in_specs=[hbm] * 5, out_specs=(hbm, pl.BlockS...  5.88 us
    pallas_call x1, Pallas kernels, adjoint(): pl.pallas_call(adjoint_kernel, out_shape=(jax.ShapeDtypeStruct((RHS, ROWS...  4.67 us
    pallas_call x1, Pallas kernels, faces(): pl.pallas_call(faces_kernel, out_shape=(jax.ShapeDtypeStruct((2, ROWS, WI...  4.12 us
  transfers between devices with their start and end apart: 5, of which 1 were waited for; matrix products, arithmetic and copies ran while one was open for 0% of the time, Pallas kernels for 19%

profile of v5, /device:TPU:1, one launch (start us, length us, event | category | flops | bytes accessed | tf_op | source)
XLA Modules:
  0.0 85.9 jit_solution(7657168390780362733)
XLA Ops:
  0.0 2.5 %collective-permute-start = (f32[256,128]{1,0:T(8,128)}, f32[256,128]{1,0:T(8,128)S(1)}, u32[]{:S(2)}, u32[]{:S(2)}) collective-permute-start(f32[256,128]{1,0:T(8,128)} %own.1), channel_id=1, source_target_pairs={{0,1},{2,3},{4,5},{6,7},{8,9},{10,11},{12,13},{14,15},{1,0},{3,2},... | collective-permute-start | bytes 393224 | tf_op jit(solution)/shard_map/ppermute | solution.py:495
  2.5 4.7 %collective-permute-start.1 = (f32[256,128]{1,0:T(8,128)}, f32[256,128]{1,0:T(8,128)S(1)}, u32[]{:S(2)}, u32[]{:S(2)}) collective-permute-start(f32[256,128]{1,0:T(8,128)} %own.1), channel_id=1, source_target_pairs={{1,2},{3,4},{5,6},{7,8},{9,10},{11,12},{13,14},{15,0},{2,1},{4,3},... | collective-permute-start | bytes 393224 | tf_op jit(solution)/shard_map/ppermute | solution.py:495
  7.2 5.9 %pack.1 = (bf16[1024,1152]{1,0:T(8,128)(2,1)}, f32[8,512]{1,0:T(8,128)}) custom-call(bf16[512,1024]{1,0:T(8,128)(2,1)} %prints_hbm.1, bf16[4,512]{1,0:T(4,128)(2,1)} %bitcast.18, s32[1,512]{1,0:T(1,128)} %bitcast.15, s32[1,512]{1,0:T(1,128)} %bitcast.19, s32[1,512]{1,0:T(1,128)} %bitcast.20), custom_call_target="tpu_custom_call" | custom-call | flops 1073741824 | bytes 3145728 | tf_op jit(solution)/shard_map/pack/pallas_call | solution.py:134
  13.1 0.0 collective-permute-done.first
  13.1 0.0 collective-permute-done.1.second
  13.1 0.0 copy-start.2
  13.1 7.1 %all-to-all-start = ((bf16[128,8,1152]{2,1,0:T(8,128)(2,1)}), bf16[128,8,1152]{2,1,0:T(8,128)(2,1)S(1)}, u32[]{:S(2)}, u32[]{:S(2)}) async-start(bf16[128,8,1152]{2,1,0:T(8,128)(2,1)} %bitcast.17), calls=%async_computation | async-start | bytes 4718592 | tf_op jit(solution)/shard_map/all_to_all | solution.py:505
  20.2 0.0 copy-done.2
  20.2 4.1 %faces.1 = (f32[2,256,1152]{2,1,0:T(8,128)S(1)}, f32[256,1152]{1,0:T(8,128)S(1)}, f32[256,1152]{1,0:T(8,128)S(1)}, f32[8,8,1152]{2,1,0:T(8,128)S(1)}) custom-call(f32[256,128]{1,0:T(8,128)S(1)} %copy-done.2, f32[256,128]{1,0:T(8,128)S(1)} %collective-permute-done.first, f32[256,128]{1,0:T(8,128)S(1)} %collective-permute-done.1.second), custom_call_target="tpu_custom_call" | custom-call | flops 1073741824 | bytes 6291456 | tf_op jit(solution)/shard_map/faces/pallas_call | solution.py:203
  24.4 1.4 %copy-done.3 = f32[2,256,1152]{2,1,0:T(8,128)} copy-done((f32[2,256,1152]{2,1,0:T(8,128)}, f32[2,256,1152]{2,1,0:T(8,128)S(1)}, u32[]{:S(2)}) %copy-start.3) | copy-done | bytes 2359320
  25.8 1.0 %copy-done.5 = f32[256,1152]{1,0:T(8,128)} copy-done((f32[256,1152]{1,0:T(8,128)}, f32[256,1152]{1,0:T(8,128)S(1)}, u32[]{:S(2)}) %copy-start.5) | copy-done | bytes 1179672
  26.8 1.0 %copy-done.7 = f32[256,1152]{1,0:T(8,128)} copy-done((f32[256,1152]{1,0:T(8,128)}, f32[256,1152]{1,0:T(8,128)S(1)}, u32[]{:S(2)}) %copy-start.7) | copy-done | bytes 1179672
  27.9 24.5 %all-to-all-done = bf16[128,8,1152]{2,1,0:T(8,128)(2,1)S(1)} async-done(((bf16[128,8,1152]{2,1,0:T(8,128)(2,1)}), bf16[128,8,1152]{2,1,0:T(8,128)(2,1)S(1)}, u32[]{:S(2)}, u32[]{:S(2)}) %all-to-all-start) | async-done | bytes 2359328 | tf_op jit(solution)/shard_map/all_to_all | solution.py:505
  52.4 4.7 %adjoint.1 = (f32[4,256,1152]{2,1,0:T(8,128)S(1)}, f32[8,8,1152]{2,1,0:T(8,128)S(1)}, f32[8,4,1152]{2,1,0:T(4,128)S(1)}, f32[8,4,1152]{2,1,0:T(4,128)S(1)}, f32[16,1024]{1,0:T(8,128)S(1)}) custom-call(bf16[1024,1152]{1,0:T(8,128)(2,1)S(1)} %bitcast.11, f32[8,8,1152]{2,1,0:T(8,128)S(1)} %get-tuple-element.25.roots), custom_call_target="tpu_custom_call" | custom-call | flops 5368709120 | bytes 8388608 | tf_op jit(solution)/shard_map/adjoint/pallas_call | solution.py:269
  57.0 1.3 %collective-permute-start.2 = (f32[8,4,1152]{2,1,0:T(4,128)S(1)}, f32[8,4,1152]{2,1,0:T(4,128)S(1)}, u32[]{:S(2)}, u32[]{:S(2)}) collective-permute-start(f32[8,4,1152]{2,1,0:T(4,128)S(1)} %get-tuple-element.33), channel_id=1, source_target_pairs={{0,16},{32,48},{64,80},{96,112},{16,0},{48,32},{80,64},{112,96},{1... | collective-permute-start | bytes 442376 | tf_op jit(solution)/shard_map/ppermute | solution.py:495
  58.4 2.7 %collective-permute-start.3 = (f32[8,4,1152]{2,1,0:T(4,128)S(1)}, f32[8,4,1152]{2,1,0:T(4,128)S(1)}, u32[]{:S(2)}, u32[]{:S(2)}) collective-permute-start(f32[8,4,1152]{2,1,0:T(4,128)S(1)} %get-tuple-element.34), channel_id=1, source_target_pairs={{16,32},{48,64},{80,96},{32,16},{64,48},{96,80},{17,33},{49,65},{8... | collective-permute-start | bytes 442376 | tf_op jit(solution)/shard_map/ppermute | solution.py:495
  61.2 6.3 %diffuse.1 = (bf16[4,192,1152]{2,1,0:T(8,128)(2,1)S(1)}, f32[4,64,1152]{2,1,0:T(8,128)S(1)}) custom-call(f32[4,256,1152]{2,1,0:T(8,128)S(1)} %get-tuple-element.26.field, f32[2,256,1152]{2,1,0:T(8,128)S(1)} %copy-done.4, f32[256,1152]{1,0:T(8,128)S(1)} %copy-done.6, f32[256,1152]{1,0:T(8,128)S(1)} %copy-done.8), custom_call_target="tpu_custom_call" | custom-call | flops 6442450944 | bytes 8388608 | tf_op jit(solution)/shard_map/diffuse/pallas_call | solution.py:374
  67.4 0.0 collective-permute-done.2.inner
  67.5 0.0 collective-permute-done.3.beyond
  67.5 0.0 copy-start.1
  67.5 3.4 %finish.1 = f32[128,128]{1,0:T(8,128)S(1)} custom-call(bf16[4,192,1152]{2,1,0:T(8,128)(2,1)S(1)} %get-tuple-element.30.smooth, f32[4,64,1152]{2,1,0:T(8,128)S(1)} %get-tuple-element.31.outer, f32[8,8,1152]{2,1,0:T(8,128)S(1)} %get-tuple-element.32.rim, f32[8,8,1152]{2,1,0:T(8,128)S(1)} %get-tuple-element.25.roots, ...), custom_call_target="tpu_custom_call" | custom-call | flops 3221225472 | bytes 10485760 | tf_op jit(solution)/shard_map/finish/pallas_call | solution.py:460
  70.9 14.2 %all_to_all.22 = f32[128,1,128]{2,1,0:T(1,128)S(1)} all-to-all(f32[128,1,128]{2,1,0:T(1,128)S(1)} %bitcast.14), channel_id=1, replica_groups=mesh['lat'=8,'lon'=16] {'lat','lon'}, dimensions={0} | all-to-all | bytes 131072 | tf_op jit(solution)/shard_map/all_to_all | solution.py:511
  85.1 0.0 copy-done
  85.1 0.8 unpack.1
  (11 shorter events, 0.0 us)
Async XLA Ops:
  0.0 13.1 %collective-permute-start = (f32[256,128]{1,0:T(8,128)}, f32[256,128]{1,0:T(8,128)S(1)}, u32[]{:S(2)}, u32[]{:S(2)}) collective-permute-start(f32[256,128]{1,0:T(8,128)} %own.1), channel_id=1, source_target_pairs={{0,1},{2,3},{4,5},{6,7},{8,9},{10,11},{12,13},{14,15},{1,0},{3,2},... | collective-permute-start | bytes 393224 | tf_op jit(solution)/shard_map/ppermute | solution.py:495
  2.5 10.6 %collective-permute-start.1 = (f32[256,128]{1,0:T(8,128)}, f32[256,128]{1,0:T(8,128)S(1)}, u32[]{:S(2)}, u32[]{:S(2)}) collective-permute-start(f32[256,128]{1,0:T(8,128)} %own.1), channel_id=1, source_target_pairs={{1,2},{3,4},{5,6},{7,8},{9,10},{11,12},{13,14},{15,0},{2,1},{4,3},... | collective-permute-start | bytes 393224 | tf_op jit(solution)/shard_map/ppermute | solution.py:495
  13.1 7.2 %copy-start.2 = (f32[256,128]{1,0:T(8,128)S(1)}, f32[256,128]{1,0:T(8,128)}, u32[]{:S(2)}) copy-start(f32[256,128]{1,0:T(8,128)} %own.1) | copy-start | bytes 393220
  13.1 39.3 %all-to-all-start = ((bf16[128,8,1152]{2,1,0:T(8,128)(2,1)}), bf16[128,8,1152]{2,1,0:T(8,128)(2,1)S(1)}, u32[]{:S(2)}, u32[]{:S(2)}) async-start(bf16[128,8,1152]{2,1,0:T(8,128)(2,1)} %bitcast.17), calls=%async_computation | async-start | bytes 4718592 | tf_op jit(solution)/shard_map/all_to_all | solution.py:505
  24.4 1.4 %copy-start.3 = (f32[2,256,1152]{2,1,0:T(8,128)}, f32[2,256,1152]{2,1,0:T(8,128)S(1)}, u32[]{:S(2)}) copy-start(f32[2,256,1152]{2,1,0:T(8,128)S(1)} %get-tuple-element.27.coef) | copy-start | bytes 7077892
  25.8 1.0 %copy-start.5 = (f32[256,1152]{1,0:T(8,128)}, f32[256,1152]{1,0:T(8,128)S(1)}, u32[]{:S(2)}) copy-start(f32[256,1152]{1,0:T(8,128)S(1)} %get-tuple-element.28.over) | copy-start | bytes 3538948
  26.8 1.0 %copy-start.7 = (f32[256,1152]{1,0:T(8,128)}, f32[256,1152]{1,0:T(8,128)S(1)}, u32[]{:S(2)}) copy-start(f32[256,1152]{1,0:T(8,128)S(1)} %get-tuple-element.29.root) | copy-start | bytes 3538948
  52.4 8.8 %copy-start.4 = (f32[2,256,1152]{2,1,0:T(8,128)S(1)}, f32[2,256,1152]{2,1,0:T(8,128)}, u32[]{:S(2)}) copy-start(f32[2,256,1152]{2,1,0:T(8,128)} %copy-done.3) | copy-start | bytes 7077892
  52.4 8.8 %copy-start.6 = (f32[256,1152]{1,0:T(8,128)S(1)}, f32[256,1152]{1,0:T(8,128)}, u32[]{:S(2)}) copy-start(f32[256,1152]{1,0:T(8,128)} %copy-done.5) | copy-start | bytes 3538948
  52.4 8.8 %copy-start.8 = (f32[256,1152]{1,0:T(8,128)S(1)}, f32[256,1152]{1,0:T(8,128)}, u32[]{:S(2)}) copy-start(f32[256,1152]{1,0:T(8,128)} %copy-done.7) | copy-start | bytes 3538948
  57.0 10.4 %collective-permute-start.2 = (f32[8,4,1152]{2,1,0:T(4,128)S(1)}, f32[8,4,1152]{2,1,0:T(4,128)S(1)}, u32[]{:S(2)}, u32[]{:S(2)}) collective-permute-start(f32[8,4,1152]{2,1,0:T(4,128)S(1)} %get-tuple-element.33), channel_id=1, source_target_pairs={{0,16},{32,48},{64,80},{96,112},{16,0},{48,32},{80,64},{112,96},{1... | collective-permute-start | bytes 442376 | tf_op jit(solution)/shard_map/ppermute | solution.py:495
  58.4 9.1 %collective-permute-start.3 = (f32[8,4,1152]{2,1,0:T(4,128)S(1)}, f32[8,4,1152]{2,1,0:T(4,128)S(1)}, u32[]{:S(2)}, u32[]{:S(2)}) collective-permute-start(f32[8,4,1152]{2,1,0:T(4,128)S(1)} %get-tuple-element.34), channel_id=1, source_target_pairs={{16,32},{48,64},{80,96},{32,16},{64,48},{96,80},{17,33},{49,65},{8... | collective-permute-start | bytes 442376 | tf_op jit(solution)/shard_map/ppermute | solution.py:495
  67.5 17.6 %copy-start = (f32[8,512]{1,0:T(8,128)S(1)}, f32[8,512]{1,0:T(8,128)}, u32[]{:S(2)}) copy-start(f32[8,512]{1,0:T(8,128)} %get-tuple-element.36.rank) | copy-start | bytes 49156
  67.5 17.6 %copy-start.1 = (s32[512,1]{0,1:T(1,128)S(1)}, s32[512,1]{0,1:T(1,128)}, u32[]{:S(2)}) copy-start(s32[512,1]{0,1:T(1,128)} %param.8) | copy-start | bytes 6148

commit v6 on v5

--- a/solution.py
+++ b/solution.py
@@ -175,7 +175,7 @@
     for q in range(RUN):
         wide[q, :CHUNKS, :] = beyond
         wide[q, CHUNKS:CHUNKS + ROWS, :] = flat[:, q * 128:(q + 1) * 128]
-        wide[q, CHUNKS + ROWS:, :] = beyond
+        wide[q, CHUNKS + ROWS:2 * CHUNKS + ROWS, :] = beyond
     for j in range(RIM):
         rim[j, :RHS, :] = jnp.broadcast_to(flat[j:j + 1], (RHS, WIDE))
         rim[j, RHS:, :] = jnp.broadcast_to(flat[ROWS - 1 - j:ROWS - j], (RHS, WIDE))
@@ -208,7 +208,7 @@
             jax.ShapeDtypeStruct((ROWS, WIDE), F32),
             jax.ShapeDtypeStruct((RIM, 2 * RHS, WIDE), F32),
         ),
-        scratch_shapes=[pltpu.VMEM((RUN, ROWS + 2 * CHUNKS, 128), F32)],
+        scratch_shapes=[pltpu.VMEM((RUN, ROWS + 2 * CHUNKS + DEPTH, 128), F32)],
         compiler_params=params(12),
         cost_estimate=cost(1 << 30, 6 << 20),
         name="faces",
@@ -299,41 +299,42 @@
         at = e * CHUNKS
         return pl.ds(at if isinstance(at, int) else pl.multiple_of(at, CHUNKS), CHUNKS)
 
-    def two_levels(ref, e, factor, store):
+    def some_levels(ref, e, factor, store, count):
         def load(r, at, q):
             return ref[r, rows_of(at), q * 128:(q + 1) * 128]
 
-        levels = (e, e + 1)
-        turned_west = [[rolled(load(r, at, RUN - 1), SLOTS) for at in levels] for r in range(RHS)]
-        turned_east = [[rolled(load(r, at, 0), -SLOTS) for at in levels] for r in range(RHS)]
-        behind, here = [[[load(r, at, q) for at in levels] for r in range(RHS)] for q in (0, 1)]
-        for q in [*range(1, RUN), 0]:
-            mid, near = [[kind[rows_of(at - 1), q * 128:(q + 1) * 128] for at in levels] for kind in factor]
-            if q == 0:
-                behind = turned_west
-                here, ahead = [[[load(r, at, i) for at in levels] for r in range(RHS)] for i in (0, 1)]
-            elif q + 1 < RUN:
-                ahead = [[load(r, at, q + 1) for at in levels] for r in range(RHS)]
-            else:
-                ahead = turned_east
-            for r in range(RHS):
-                column = [load(r, e - 1, q)] + here[r] + [load(r, e + 2, q)]
-                for i in range(2):
-                    total = (column[i + 2] + column[i]) + (ahead[r][i] + behind[r][i])
-                    store(r, q, i, mid[i] * here[r][i] + near[i] * total)
-            behind, here = here, ahead
+        levels = tuple(e + i for i in range(count))
+        for group in ((0, 1), (2, 3)):
+            turned_west = {r: [rolled(load(r, at, RUN - 1), SLOTS) for at in levels] for r in group}
+            turned_east = {r: [rolled(load(r, at, 0), -SLOTS) for at in levels] for r in group}
+            behind, here = [{r: [load(r, at, q) for at in levels] for r in group} for q in (0, 1)]
+            for q in [*range(1, RUN), 0]:
+                mid, near = [[kind[rows_of(at - 1), q * 128:(q + 1) * 128] for at in levels] for kind in factor]
+                if q == 0:
+                    behind = turned_west
+                    here, ahead = [{r: [load(r, at, i) for at in levels] for r in group} for i in (0, 1)]
+                elif q + 1 < RUN:
+                    ahead = {r: [load(r, at, q + 1) for at in levels] for r in group}
+                else:
+                    ahead = turned_east
+                for r in group:
+                    column = [load(r, e - 1, q)] + here[r] + [load(r, e + count, q)]
+                    for i in range(count):
+                        total = (column[i + 2] + column[i]) + (ahead[r][i] + behind[r][i])
+                        store(r, q, i, mid[i] * here[r][i] + near[i] * total)
+                behind, here = here, ahead
 
     def sweep(ref, target, first, end, factor, to=0):
         def step(pair, _):
-            e = first + 2 * pair
+            e = first + 4 * pair
 
             def store(r, q, i, value):
                 target[r, rows_of(e + i + to), q * 128:(q + 1) * 128] = value
 
-            two_levels(ref, e, factor, store)
+            some_levels(ref, e, factor, store, 4)
             return 0
 
-        lax.fori_loop(0, (end - first) // 2, step, 0, unroll=2)
+        lax.fori_loop(0, (end - first) // 4, step, 0)
 
     def scale(e, _):
         for q in range(RUN):
@@ -364,7 +365,7 @@
             at = pl.ds(pl.multiple_of(pair * 2 * CHUNKS, 2 * CHUNKS), 2 * CHUNKS)
             smooth[r, at, q * 128:(q + 1) * 128] = jnp.where(inside(q), both, 0.0).astype(BF)
 
-        two_levels(one, PASSES + 1 + 2 * pair, final, store)
+        some_levels(one, PASSES + 1 + 2 * pair, final, store, 2)
         return 0
 
     lax.fori_loop(0, MIDDLE // (2 * CHUNKS), rounded, 0, unroll=2)

time: 86.2 us -> 86 us (level)
  no operation moved by 1% of the time
where the time goes in v6:
time: 86 us; the launch traced here: 85.8 us
  Pallas kernels  25 us (29%)
  waiting for transfers between devices  24.5 us (28%)
  starting transfers between devices  18.4 us (21%)
  blocking collectives  14.2 us (17%)
  local copies, waits for them, and re-layouts  3.5 us (4%)
    all_to_all x1, waiting for transfers between devices, body(): lax.all_to_all(packed, ('lat', 'lon'), split_axis=0, concat_axis=0, tiled...  24.5 us
    all_to_all x1, blocking collectives, body(): lax.all_to_all(values, ('lat', 'lon'), split_axis=0, concat_axis=0, tiled...  14.2 us
    ppermute x4, starting transfers between devices, swap(): return lax.ppermute(x, axis, pairs + [(j, i) for i, j in pairs])  11.2 us
    all_to_all x1, starting transfers between devices, body(): lax.all_to_all(packed, ('lat', 'lon'), split_axis=0, concat_axis=0, tiled...  7.14 us
    pallas_call x1, Pallas kernels, diffuse(): pl.pallas_call(diffuse_kernel, out_shape=(jax.ShapeDtypeStruct((RHS, MIDD...  6.13 us
    pallas_call x1, Pallas kernels, pack(): pl.pallas_call(pack_kernel, in_specs=[hbm] * 5, out_specs=(hbm, pl.BlockS...  5.88 us
    pallas_call x1, Pallas kernels, adjoint(): pl.pallas_call(adjoint_kernel, out_shape=(jax.ShapeDtypeStruct((RHS, ROWS...  4.67 us
    pallas_call x1, Pallas kernels, faces(): pl.pallas_call(faces_kernel, out_shape=(jax.ShapeDtypeStruct((2, ROWS, WI...  4.12 us
  transfers between devices with their start and end apart: 5, of which 1 were waited for; matrix products, arithmetic and copies ran while one was open for 0% of the time, Pallas kernels for 19%

profile of v6, /device:TPU:1, one launch (start us, length us, event | category | flops | bytes accessed | tf_op | source)
XLA Modules:
  0.0 85.8 jit_solution(3375420150751822130)
XLA Ops:
  0.0 2.5 %collective-permute-start = (f32[256,128]{1,0:T(8,128)}, f32[256,128]{1,0:T(8,128)S(1)}, u32[]{:S(2)}, u32[]{:S(2)}) collective-permute-start(f32[256,128]{1,0:T(8,128)} %own.1), channel_id=1, source_target_pairs={{0,1},{2,3},{4,5},{6,7},{8,9},{10,11},{12,13},{14,15},{1,0},{3,2},... | collective-permute-start | bytes 393224 | tf_op jit(solution)/shard_map/ppermute | solution.py:496
  2.5 4.7 %collective-permute-start.1 = (f32[256,128]{1,0:T(8,128)}, f32[256,128]{1,0:T(8,128)S(1)}, u32[]{:S(2)}, u32[]{:S(2)}) collective-permute-start(f32[256,128]{1,0:T(8,128)} %own.1), channel_id=1, source_target_pairs={{1,2},{3,4},{5,6},{7,8},{9,10},{11,12},{13,14},{15,0},{2,1},{4,3},... | collective-permute-start | bytes 393224 | tf_op jit(solution)/shard_map/ppermute | solution.py:496
  7.2 5.9 %pack.1 = (bf16[1024,1152]{1,0:T(8,128)(2,1)}, f32[8,512]{1,0:T(8,128)}) custom-call(bf16[512,1024]{1,0:T(8,128)(2,1)} %prints_hbm.1, bf16[4,512]{1,0:T(4,128)(2,1)} %bitcast.18, s32[1,512]{1,0:T(1,128)} %bitcast.15, s32[1,512]{1,0:T(1,128)} %bitcast.19, s32[1,512]{1,0:T(1,128)} %bitcast.20), custom_call_target="tpu_custom_call" | custom-call | flops 1073741824 | bytes 3145728 | tf_op jit(solution)/shard_map/pack/pallas_call | solution.py:134
  13.1 0.0 collective-permute-done.first
  13.1 0.0 collective-permute-done.1.second
  13.1 0.0 copy-start.2
  13.1 7.1 %all-to-all-start = ((bf16[128,8,1152]{2,1,0:T(8,128)(2,1)}), bf16[128,8,1152]{2,1,0:T(8,128)(2,1)S(1)}, u32[]{:S(2)}, u32[]{:S(2)}) async-start(bf16[128,8,1152]{2,1,0:T(8,128)(2,1)} %bitcast.17), calls=%async_computation | async-start | bytes 4718592 | tf_op jit(solution)/shard_map/all_to_all | solution.py:506
  20.2 0.0 copy-done.2
  20.2 4.1 %faces.1 = (f32[2,256,1152]{2,1,0:T(8,128)S(1)}, f32[256,1152]{1,0:T(8,128)S(1)}, f32[256,1152]{1,0:T(8,128)S(1)}, f32[8,8,1152]{2,1,0:T(8,128)S(1)}) custom-call(f32[256,128]{1,0:T(8,128)S(1)} %copy-done.2, f32[256,128]{1,0:T(8,128)S(1)} %collective-permute-done.first, f32[256,128]{1,0:T(8,128)S(1)} %collective-permute-done.1.second), custom_call_target="tpu_custom_call" | custom-call | flops 1073741824 | bytes 6291456 | tf_op jit(solution)/shard_map/faces/pallas_call | solution.py:203
  24.4 1.4 %copy-done.3 = f32[2,256,1152]{2,1,0:T(8,128)} copy-done((f32[2,256,1152]{2,1,0:T(8,128)}, f32[2,256,1152]{2,1,0:T(8,128)S(1)}, u32[]{:S(2)}) %copy-start.3) | copy-done | bytes 2359320
  25.8 1.0 %copy-done.5 = f32[256,1152]{1,0:T(8,128)} copy-done((f32[256,1152]{1,0:T(8,128)}, f32[256,1152]{1,0:T(8,128)S(1)}, u32[]{:S(2)}) %copy-start.5) | copy-done | bytes 1179672
  26.8 1.0 %copy-done.7 = f32[256,1152]{1,0:T(8,128)} copy-done((f32[256,1152]{1,0:T(8,128)}, f32[256,1152]{1,0:T(8,128)S(1)}, u32[]{:S(2)}) %copy-start.7) | copy-done | bytes 1179672
  27.9 24.5 %all-to-all-done = bf16[128,8,1152]{2,1,0:T(8,128)(2,1)S(1)} async-done(((bf16[128,8,1152]{2,1,0:T(8,128)(2,1)}), bf16[128,8,1152]{2,1,0:T(8,128)(2,1)S(1)}, u32[]{:S(2)}, u32[]{:S(2)}) %all-to-all-start) | async-done | bytes 2359328 | tf_op jit(solution)/shard_map/all_to_all | solution.py:506
  52.4 4.7 %adjoint.1 = (f32[4,256,1152]{2,1,0:T(8,128)S(1)}, f32[8,8,1152]{2,1,0:T(8,128)S(1)}, f32[8,4,1152]{2,1,0:T(4,128)S(1)}, f32[8,4,1152]{2,1,0:T(4,128)S(1)}, f32[16,1024]{1,0:T(8,128)S(1)}) custom-call(bf16[1024,1152]{1,0:T(8,128)(2,1)S(1)} %bitcast.11, f32[8,8,1152]{2,1,0:T(8,128)S(1)} %get-tuple-element.25.roots), custom_call_target="tpu_custom_call" | custom-call | flops 5368709120 | bytes 8388608 | tf_op jit(solution)/shard_map/adjoint/pallas_call | solution.py:269
  57.0 1.3 %collective-permute-start.2 = (f32[8,4,1152]{2,1,0:T(4,128)S(1)}, f32[8,4,1152]{2,1,0:T(4,128)S(1)}, u32[]{:S(2)}, u32[]{:S(2)}) collective-permute-start(f32[8,4,1152]{2,1,0:T(4,128)S(1)} %get-tuple-element.33), channel_id=1, source_target_pairs={{0,16},{32,48},{64,80},{96,112},{16,0},{48,32},{80,64},{112,96},{1... | collective-permute-start | bytes 442376 | tf_op jit(solution)/shard_map/ppermute | solution.py:496
  58.4 2.7 %collective-permute-start.3 = (f32[8,4,1152]{2,1,0:T(4,128)S(1)}, f32[8,4,1152]{2,1,0:T(4,128)S(1)}, u32[]{:S(2)}, u32[]{:S(2)}) collective-permute-start(f32[8,4,1152]{2,1,0:T(4,128)S(1)} %get-tuple-element.34), channel_id=1, source_target_pairs={{16,32},{48,64},{80,96},{32,16},{64,48},{96,80},{17,33},{49,65},{8... | collective-permute-start | bytes 442376 | tf_op jit(solution)/shard_map/ppermute | solution.py:496
  61.2 6.1 %diffuse.1 = (bf16[4,192,1152]{2,1,0:T(8,128)(2,1)S(1)}, f32[4,64,1152]{2,1,0:T(8,128)S(1)}) custom-call(f32[4,256,1152]{2,1,0:T(8,128)S(1)} %get-tuple-element.26.field, f32[2,256,1152]{2,1,0:T(8,128)S(1)} %copy-done.4, f32[256,1152]{1,0:T(8,128)S(1)} %copy-done.6, f32[256,1152]{1,0:T(8,128)S(1)} %copy-done.8), custom_call_target="tpu_custom_call" | custom-call | flops 6442450944 | bytes 8388608 | tf_op jit(solution)/shard_map/diffuse/pallas_call | solution.py:375
  67.3 0.0 collective-permute-done.2.inner
  67.3 0.0 collective-permute-done.3.beyond
  67.3 0.0 copy-start.1
  67.3 3.4 %finish.1 = f32[128,128]{1,0:T(8,128)S(1)} custom-call(bf16[4,192,1152]{2,1,0:T(8,128)(2,1)S(1)} %get-tuple-element.30.smooth, f32[4,64,1152]{2,1,0:T(8,128)S(1)} %get-tuple-element.31.outer, f32[8,8,1152]{2,1,0:T(8,128)S(1)} %get-tuple-element.32.rim, f32[8,8,1152]{2,1,0:T(8,128)S(1)} %get-tuple-element.25.roots, ...), custom_call_target="tpu_custom_call" | custom-call | flops 3221225472 | bytes 10485760 | tf_op jit(solution)/shard_map/finish/pallas_call | solution.py:461
  70.7 14.2 %all_to_all.22 = f32[128,1,128]{2,1,0:T(1,128)S(1)} all-to-all(f32[128,1,128]{2,1,0:T(1,128)S(1)} %bitcast.14), channel_id=1, replica_groups=mesh['lat'=8,'lon'=16] {'lat','lon'}, dimensions={0} | all-to-all | bytes 131072 | tf_op jit(solution)/shard_map/all_to_all | solution.py:512
  84.9 0.0 copy-done
  84.9 0.8 unpack.1
  (11 shorter events, 0.0 us)
Async XLA Ops:
  0.0 13.1 %collective-permute-start = (f32[256,128]{1,0:T(8,128)}, f32[256,128]{1,0:T(8,128)S(1)}, u32[]{:S(2)}, u32[]{:S(2)}) collective-permute-start(f32[256,128]{1,0:T(8,128)} %own.1), channel_id=1, source_target_pairs={{0,1},{2,3},{4,5},{6,7},{8,9},{10,11},{12,13},{14,15},{1,0},{3,2},... | collective-permute-start | bytes 393224 | tf_op jit(solution)/shard_map/ppermute | solution.py:496
  2.5 10.6 %collective-permute-start.1 = (f32[256,128]{1,0:T(8,128)}, f32[256,128]{1,0:T(8,128)S(1)}, u32[]{:S(2)}, u32[]{:S(2)}) collective-permute-start(f32[256,128]{1,0:T(8,128)} %own.1), channel_id=1, source_target_pairs={{1,2},{3,4},{5,6},{7,8},{9,10},{11,12},{13,14},{15,0},{2,1},{4,3},... | collective-permute-start | bytes 393224 | tf_op jit(solution)/shard_map/ppermute | solution.py:496
  13.1 7.2 %copy-start.2 = (f32[256,128]{1,0:T(8,128)S(1)}, f32[256,128]{1,0:T(8,128)}, u32[]{:S(2)}) copy-start(f32[256,128]{1,0:T(8,128)} %own.1) | copy-start | bytes 393220
  13.1 39.3 %all-to-all-start = ((bf16[128,8,1152]{2,1,0:T(8,128)(2,1)}), bf16[128,8,1152]{2,1,0:T(8,128)(2,1)S(1)}, u32[]{:S(2)}, u32[]{:S(2)}) async-start(bf16[128,8,1152]{2,1,0:T(8,128)(2,1)} %bitcast.17), calls=%async_computation | async-start | bytes 4718592 | tf_op jit(solution)/shard_map/all_to_all | solution.py:506
  24.4 1.4 %copy-start.3 = (f32[2,256,1152]{2,1,0:T(8,128)}, f32[2,256,1152]{2,1,0:T(8,128)S(1)}, u32[]{:S(2)}) copy-start(f32[2,256,1152]{2,1,0:T(8,128)S(1)} %get-tuple-element.27.coef) | copy-start | bytes 7077892
  25.8 1.0 %copy-start.5 = (f32[256,1152]{1,0:T(8,128)}, f32[256,1152]{1,0:T(8,128)S(1)}, u32[]{:S(2)}) copy-start(f32[256,1152]{1,0:T(8,128)S(1)} %get-tuple-element.28.over) | copy-start | bytes 3538948
  26.8 1.0 %copy-start.7 = (f32[256,1152]{1,0:T(8,128)}, f32[256,1152]{1,0:T(8,128)S(1)}, u32[]{:S(2)}) copy-start(f32[256,1152]{1,0:T(8,128)S(1)} %get-tuple-element.29.root) | copy-start | bytes 3538948
  52.4 8.8 %copy-start.4 = (f32[2,256,1152]{2,1,0:T(8,128)S(1)}, f32[2,256,1152]{2,1,0:T(8,128)}, u32[]{:S(2)}) copy-start(f32[2,256,1152]{2,1,0:T(8,128)} %copy-done.3) | copy-start | bytes 7077892
  52.4 8.8 %copy-start.6 = (f32[256,1152]{1,0:T(8,128)S(1)}, f32[256,1152]{1,0:T(8,128)}, u32[]{:S(2)}) copy-start(f32[256,1152]{1,0:T(8,128)} %copy-done.5) | copy-start | bytes 3538948
  52.4 8.8 %copy-start.8 = (f32[256,1152]{1,0:T(8,128)S(1)}, f32[256,1152]{1,0:T(8,128)}, u32[]{:S(2)}) copy-start(f32[256,1152]{1,0:T(8,128)} %copy-done.7) | copy-start | bytes 3538948
  57.0 10.2 %collective-permute-start.2 = (f32[8,4,1152]{2,1,0:T(4,128)S(1)}, f32[8,4,1152]{2,1,0:T(4,128)S(1)}, u32[]{:S(2)}, u32[]{:S(2)}) collective-permute-start(f32[8,4,1152]{2,1,0:T(4,128)S(1)} %get-tuple-element.33), channel_id=1, source_target_pairs={{0,16},{32,48},{64,80},{96,112},{16,0},{48,32},{80,64},{112,96},{1... | collective-permute-start | bytes 442376 | tf_op jit(solution)/shard_map/ppermute | solution.py:496
  58.4 8.9 %collective-permute-start.3 = (f32[8,4,1152]{2,1,0:T(4,128)S(1)}, f32[8,4,1152]{2,1,0:T(4,128)S(1)}, u32[]{:S(2)}, u32[]{:S(2)}) collective-permute-start(f32[8,4,1152]{2,1,0:T(4,128)S(1)} %get-tuple-element.34), channel_id=1, source_target_pairs={{16,32},{48,64},{80,96},{32,16},{64,48},{96,80},{17,33},{49,65},{8... | collective-permute-start | bytes 442376 | tf_op jit(solution)/shard_map/ppermute | solution.py:496
  67.3 17.6 %copy-start = (f32[8,512]{1,0:T(8,128)S(1)}, f32[8,512]{1,0:T(8,128)}, u32[]{:S(2)}) copy-start(f32[8,512]{1,0:T(8,128)} %get-tuple-element.36.rank) | copy-start | bytes 49156
  67.3 17.6 %copy-start.1 = (s32[512,1]{0,1:T(1,128)S(1)}, s32[512,1]{0,1:T(1,128)}, u32[]{:S(2)}) copy-start(s32[512,1]{0,1:T(1,128)} %param.8) | copy-start | bytes 6148

commit v7 on v6

--- a/solution.py
+++ b/solution.py
@@ -73,13 +73,16 @@
     return row[1:] + [rolled(row[0], -SLOTS)], [rolled(row[-1], SLOTS)] + row[:-1]
 
 
-PIECES = 4
+PIECES = 8
 
 
 def pack_kernel(prints_hbm, weights_hbm, target_hbm, block_hbm, slot_hbm, out_hbm, rank_out,
                 prints, weights, target, block, slot, masked, meta, spread, wide, out, sems, out_sems):
     pairs = ((target_hbm, target), (weights_hbm, weights), (block_hbm, block), (slot_hbm, slot), (prints_hbm, prints))
-    copies = [pltpu.make_async_copy(a, b, sems.at[i]) for i, (a, b) in enumerate(pairs)]
+    copies = [pltpu.make_async_copy(a, b, sems.at[i]) for i, (a, b) in enumerate(pairs[:4])]
+    parts = [slice(i * OBS // 2, (i + 1) * OBS // 2) for i in range(2)]
+    for i, part in enumerate(parts):
+        copies.append(pltpu.make_async_copy(prints_hbm.at[part, :], prints.at[part, :], sems.at[4 + i]))
     for copy in copies:
         copy.start()
     e, s, q, k = lanes((1, WIDE), 1)
@@ -100,14 +103,16 @@
     t = target[...]
     hit = pick(iota((DEVICES, OBS), 0) == t)
     earlier = mm(hit, before)
-    copies[4].wait()
-    for s in range(SLOTS):
-        live = slots >= jnp.asarray(s, BF)
-        piece = prints[:, s * CLON:(s + 1) * CLON]
-        masked[:, s * CLON:(s + 1) * CLON] = jnp.where(live, piece, jnp.zeros_like(piece))
     e, s, q, k = lanes((1, WIDE), 1)
     fact = jnp.where((k == 0) & (q < FRONT) & (s < 5), s, -1)
-    wide[...] = (mm(masked[...], spread[...]) + mm(facts, pick(iota((8, WIDE), 0) == fact), TN)).astype(BF)
+    extra = mm(facts, pick(iota((8, WIDE), 0) == fact), TN)
+    for copy, part in zip(copies[4:], parts):
+        copy.wait()
+        for s in range(SLOTS):
+            live = slots[part] >= jnp.asarray(s, BF)
+            piece = prints[part, s * CLON:(s + 1) * CLON]
+            masked[part, s * CLON:(s + 1) * CLON] = jnp.where(live, piece, jnp.zeros_like(piece))
+        wide[part, :] = (mm(masked[part, :], spread[...]) + extra[part]).astype(BF)
     rank = jnp.sum(hit.astype(F32) * earlier, axis=0, keepdims=True)
     rank_out[...] = jnp.broadcast_to(rank, (8, OBS))
     where = pick(iota((TOTAL, OBS), 0) == t * CAP + rank.astype(jnp.int32))
@@ -150,7 +155,7 @@
             pltpu.VMEM((SPAN, WIDE), BF),
             pltpu.VMEM((OBS, WIDE), BF),
             pltpu.VMEM((TOTAL, WIDE), BF),
-            pltpu.SemaphoreType.DMA((5,)),
+            pltpu.SemaphoreType.DMA((6,)),
             pltpu.SemaphoreType.DMA((PIECES,)),
         ],
         compiler_params=params(60),

time: 86 us -> 86 us (level)
  no operation moved by 1% of the time
where the time goes in v7:
time: 86 us; the launch traced here: 85.8 us
  Pallas kernels  25 us (29%)
  waiting for transfers between devices  24.5 us (28%)
  starting transfers between devices  18.4 us (21%)
  blocking collectives  14.2 us (17%)
  local copies, waits for them, and re-layouts  3.5 us (4%)
    all_to_all x1, waiting for transfers between devices, body(): lax.all_to_all(packed, ('lat', 'lon'), split_axis=0, concat_axis=0, tiled...  24.5 us
    all_to_all x1, blocking collectives, body(): lax.all_to_all(values, ('lat', 'lon'), split_axis=0, concat_axis=0, tiled...  14.2 us
    ppermute x4, starting transfers between devices, swap(): return lax.ppermute(x, axis, pairs + [(j, i) for i, j in pairs])  11.2 us
    all_to_all x1, starting transfers between devices, body(): lax.all_to_all(packed, ('lat', 'lon'), split_axis=0, concat_axis=0, tiled...  7.15 us
    pallas_call x1, Pallas kernels, diffuse(): pl.pallas_call(diffuse_kernel, out_shape=(jax.ShapeDtypeStruct((RHS, MIDD...  6.13 us
    pallas_call x1, Pallas kernels, pack(): pl.pallas_call(pack_kernel, in_specs=[hbm] * 5, out_specs=(hbm, pl.BlockS...  5.88 us
    pallas_call x1, Pallas kernels, adjoint(): pl.pallas_call(adjoint_kernel, out_shape=(jax.ShapeDtypeStruct((RHS, ROWS...  4.67 us
    pallas_call x1, Pallas kernels, faces(): pl.pallas_call(faces_kernel, out_shape=(jax.ShapeDtypeStruct((2, ROWS, WI...  4.12 us
  transfers between devices with their start and end apart: 5, of which 1 were waited for; matrix products, arithmetic and copies ran while one was open for 0% of the time, Pallas kernels for 19%

profile of v7, /device:TPU:1, one launch (start us, length us, event | category | flops | bytes accessed | tf_op | source)
XLA Modules:
  0.0 85.8 jit_solution(2032301203616194891)
XLA Ops:
  0.0 2.5 %collective-permute-start = (f32[256,128]{1,0:T(8,128)}, f32[256,128]{1,0:T(8,128)S(1)}, u32[]{:S(2)}, u32[]{:S(2)}) collective-permute-start(f32[256,128]{1,0:T(8,128)} %own.1), channel_id=1, source_target_pairs={{0,1},{2,3},{4,5},{6,7},{8,9},{10,11},{12,13},{14,15},{1,0},{3,2},... | collective-permute-start | bytes 393224 | tf_op jit(solution)/shard_map/ppermute | solution.py:501
  2.5 4.7 %collective-permute-start.1 = (f32[256,128]{1,0:T(8,128)}, f32[256,128]{1,0:T(8,128)S(1)}, u32[]{:S(2)}, u32[]{:S(2)}) collective-permute-start(f32[256,128]{1,0:T(8,128)} %own.1), channel_id=1, source_target_pairs={{1,2},{3,4},{5,6},{7,8},{9,10},{11,12},{13,14},{15,0},{2,1},{4,3},... | collective-permute-start | bytes 393224 | tf_op jit(solution)/shard_map/ppermute | solution.py:501
  7.2 5.9 %pack.1 = (bf16[1024,1152]{1,0:T(8,128)(2,1)}, f32[8,512]{1,0:T(8,128)}) custom-call(bf16[512,1024]{1,0:T(8,128)(2,1)} %prints_hbm.1, bf16[4,512]{1,0:T(4,128)(2,1)} %bitcast.18, s32[1,512]{1,0:T(1,128)} %bitcast.15, s32[1,512]{1,0:T(1,128)} %bitcast.19, s32[1,512]{1,0:T(1,128)} %bitcast.20), custom_call_target="tpu_custom_call" | custom-call | flops 1073741824 | bytes 3145728 | tf_op jit(solution)/shard_map/pack/pallas_call | solution.py:139
  13.0 0.0 collective-permute-done.first
  13.1 0.0 collective-permute-done.1.second
  13.1 0.0 copy-start.2
  13.1 7.1 %all-to-all-start = ((bf16[128,8,1152]{2,1,0:T(8,128)(2,1)}), bf16[128,8,1152]{2,1,0:T(8,128)(2,1)S(1)}, u32[]{:S(2)}, u32[]{:S(2)}) async-start(bf16[128,8,1152]{2,1,0:T(8,128)(2,1)} %bitcast.17), calls=%async_computation | async-start | bytes 4718592 | tf_op jit(solution)/shard_map/all_to_all | solution.py:511
  20.2 0.0 copy-done.2
  20.2 4.1 %faces.1 = (f32[2,256,1152]{2,1,0:T(8,128)S(1)}, f32[256,1152]{1,0:T(8,128)S(1)}, f32[256,1152]{1,0:T(8,128)S(1)}, f32[8,8,1152]{2,1,0:T(8,128)S(1)}) custom-call(f32[256,128]{1,0:T(8,128)S(1)} %copy-done.2, f32[256,128]{1,0:T(8,128)S(1)} %collective-permute-done.first, f32[256,128]{1,0:T(8,128)S(1)} %collective-permute-done.1.second), custom_call_target="tpu_custom_call" | custom-call | flops 1073741824 | bytes 6291456 | tf_op jit(solution)/shard_map/faces/pallas_call | solution.py:208
  24.4 1.4 %copy-done.3 = f32[2,256,1152]{2,1,0:T(8,128)} copy-done((f32[2,256,1152]{2,1,0:T(8,128)}, f32[2,256,1152]{2,1,0:T(8,128)S(1)}, u32[]{:S(2)}) %copy-start.3) | copy-done | bytes 2359320
  25.8 1.0 %copy-done.5 = f32[256,1152]{1,0:T(8,128)} copy-done((f32[256,1152]{1,0:T(8,128)}, f32[256,1152]{1,0:T(8,128)S(1)}, u32[]{:S(2)}) %copy-start.5) | copy-done | bytes 1179672
  26.8 1.0 %copy-done.7 = f32[256,1152]{1,0:T(8,128)} copy-done((f32[256,1152]{1,0:T(8,128)}, f32[256,1152]{1,0:T(8,128)S(1)}, u32[]{:S(2)}) %copy-start.7) | copy-done | bytes 1179672
  27.9 24.5 %all-to-all-done = bf16[128,8,1152]{2,1,0:T(8,128)(2,1)S(1)} async-done(((bf16[128,8,1152]{2,1,0:T(8,128)(2,1)}), bf16[128,8,1152]{2,1,0:T(8,128)(2,1)S(1)}, u32[]{:S(2)}, u32[]{:S(2)}) %all-to-all-start) | async-done | bytes 2359328 | tf_op jit(solution)/shard_map/all_to_all | solution.py:511
  52.4 4.7 %adjoint.1 = (f32[4,256,1152]{2,1,0:T(8,128)S(1)}, f32[8,8,1152]{2,1,0:T(8,128)S(1)}, f32[8,4,1152]{2,1,0:T(4,128)S(1)}, f32[8,4,1152]{2,1,0:T(4,128)S(1)}, f32[16,1024]{1,0:T(8,128)S(1)}) custom-call(bf16[1024,1152]{1,0:T(8,128)(2,1)S(1)} %bitcast.11, f32[8,8,1152]{2,1,0:T(8,128)S(1)} %get-tuple-element.25.roots), custom_call_target="tpu_custom_call" | custom-call | flops 5368709120 | bytes 8388608 | tf_op jit(solution)/shard_map/adjoint/pallas_call | solution.py:274
  57.0 1.3 %collective-permute-start.2 = (f32[8,4,1152]{2,1,0:T(4,128)S(1)}, f32[8,4,1152]{2,1,0:T(4,128)S(1)}, u32[]{:S(2)}, u32[]{:S(2)}) collective-permute-start(f32[8,4,1152]{2,1,0:T(4,128)S(1)} %get-tuple-element.33), channel_id=1, source_target_pairs={{0,16},{32,48},{64,80},{96,112},{16,0},{48,32},{80,64},{112,96},{1... | collective-permute-start | bytes 442376 | tf_op jit(solution)/shard_map/ppermute | solution.py:501
  58.4 2.7 %collective-permute-start.3 = (f32[8,4,1152]{2,1,0:T(4,128)S(1)}, f32[8,4,1152]{2,1,0:T(4,128)S(1)}, u32[]{:S(2)}, u32[]{:S(2)}) collective-permute-start(f32[8,4,1152]{2,1,0:T(4,128)S(1)} %get-tuple-element.34), channel_id=1, source_target_pairs={{16,32},{48,64},{80,96},{32,16},{64,48},{96,80},{17,33},{49,65},{8... | collective-permute-start | bytes 442376 | tf_op jit(solution)/shard_map/ppermute | solution.py:501
  61.2 6.1 %diffuse.1 = (bf16[4,192,1152]{2,1,0:T(8,128)(2,1)S(1)}, f32[4,64,1152]{2,1,0:T(8,128)S(1)}) custom-call(f32[4,256,1152]{2,1,0:T(8,128)S(1)} %get-tuple-element.26.field, f32[2,256,1152]{2,1,0:T(8,128)S(1)} %copy-done.4, f32[256,1152]{1,0:T(8,128)S(1)} %copy-done.6, f32[256,1152]{1,0:T(8,128)S(1)} %copy-done.8), custom_call_target="tpu_custom_call" | custom-call | flops 6442450944 | bytes 8388608 | tf_op jit(solution)/shard_map/diffuse/pallas_call | solution.py:380
  67.3 0.0 collective-permute-done.2.inner
  67.3 0.0 collective-permute-done.3.beyond
  67.3 0.0 copy-start.1
  67.3 3.4 %finish.1 = f32[128,128]{1,0:T(8,128)S(1)} custom-call(bf16[4,192,1152]{2,1,0:T(8,128)(2,1)S(1)} %get-tuple-element.30.smooth, f32[4,64,1152]{2,1,0:T(8,128)S(1)} %get-tuple-element.31.outer, f32[8,8,1152]{2,1,0:T(8,128)S(1)} %get-tuple-element.32.rim, f32[8,8,1152]{2,1,0:T(8,128)S(1)} %get-tuple-element.25.roots, ...), custom_call_target="tpu_custom_call" | custom-call | flops 3221225472 | bytes 10485760 | tf_op jit(solution)/shard_map/finish/pallas_call | solution.py:466
  70.7 14.2 %all_to_all.22 = f32[128,1,128]{2,1,0:T(1,128)S(1)} all-to-all(f32[128,1,128]{2,1,0:T(1,128)S(1)} %bitcast.14), channel_id=1, replica_groups=mesh['lat'=8,'lon'=16] {'lat','lon'}, dimensions={0} | all-to-all | bytes 131072 | tf_op jit(solution)/shard_map/all_to_all | solution.py:517
  84.9 0.0 copy-done
  84.9 0.8 unpack.1
  (11 shorter events, 0.0 us)
Async XLA Ops:
  0.0 13.1 %collective-permute-start = (f32[256,128]{1,0:T(8,128)}, f32[256,128]{1,0:T(8,128)S(1)}, u32[]{:S(2)}, u32[]{:S(2)}) collective-permute-start(f32[256,128]{1,0:T(8,128)} %own.1), channel_id=1, source_target_pairs={{0,1},{2,3},{4,5},{6,7},{8,9},{10,11},{12,13},{14,15},{1,0},{3,2},... | collective-permute-start | bytes 393224 | tf_op jit(solution)/shard_map/ppermute | solution.py:501
  2.5 10.6 %collective-permute-start.1 = (f32[256,128]{1,0:T(8,128)}, f32[256,128]{1,0:T(8,128)S(1)}, u32[]{:S(2)}, u32[]{:S(2)}) collective-permute-start(f32[256,128]{1,0:T(8,128)} %own.1), channel_id=1, source_target_pairs={{1,2},{3,4},{5,6},{7,8},{9,10},{11,12},{13,14},{15,0},{2,1},{4,3},... | collective-permute-start | bytes 393224 | tf_op jit(solution)/shard_map/ppermute | solution.py:501
  13.1 7.2 %copy-start.2 = (f32[256,128]{1,0:T(8,128)S(1)}, f32[256,128]{1,0:T(8,128)}, u32[]{:S(2)}) copy-start(f32[256,128]{1,0:T(8,128)} %own.1) | copy-start | bytes 393220
  13.1 39.3 %all-to-all-start = ((bf16[128,8,1152]{2,1,0:T(8,128)(2,1)}), bf16[128,8,1152]{2,1,0:T(8,128)(2,1)S(1)}, u32[]{:S(2)}, u32[]{:S(2)}) async-start(bf16[128,8,1152]{2,1,0:T(8,128)(2,1)} %bitcast.17), calls=%async_computation | async-start | bytes 4718592 | tf_op jit(solution)/shard_map/all_to_all | solution.py:511
  24.4 1.4 %copy-start.3 = (f32[2,256,1152]{2,1,0:T(8,128)}, f32[2,256,1152]{2,1,0:T(8,128)S(1)}, u32[]{:S(2)}) copy-start(f32[2,256,1152]{2,1,0:T(8,128)S(1)} %get-tuple-element.27.coef) | copy-start | bytes 7077892
  25.8 1.0 %copy-start.5 = (f32[256,1152]{1,0:T(8,128)}, f32[256,1152]{1,0:T(8,128)S(1)}, u32[]{:S(2)}) copy-start(f32[256,1152]{1,0:T(8,128)S(1)} %get-tuple-element.28.over) | copy-start | bytes 3538948
  26.8 1.0 %copy-start.7 = (f32[256,1152]{1,0:T(8,128)}, f32[256,1152]{1,0:T(8,128)S(1)}, u32[]{:S(2)}) copy-start(f32[256,1152]{1,0:T(8,128)S(1)} %get-tuple-element.29.root) | copy-start | bytes 3538948
  52.4 8.8 %copy-start.4 = (f32[2,256,1152]{2,1,0:T(8,128)S(1)}, f32[2,256,1152]{2,1,0:T(8,128)}, u32[]{:S(2)}) copy-start(f32[2,256,1152]{2,1,0:T(8,128)} %copy-done.3) | copy-start | bytes 7077892
  52.4 8.8 %copy-start.6 = (f32[256,1152]{1,0:T(8,128)S(1)}, f32[256,1152]{1,0:T(8,128)}, u32[]{:S(2)}) copy-start(f32[256,1152]{1,0:T(8,128)} %copy-done.5) | copy-start | bytes 3538948
  52.4 8.8 %copy-start.8 = (f32[256,1152]{1,0:T(8,128)S(1)}, f32[256,1152]{1,0:T(8,128)}, u32[]{:S(2)}) copy-start(f32[256,1152]{1,0:T(8,128)} %copy-done.7) | copy-start | bytes 3538948
  57.0 10.2 %collective-permute-start.2 = (f32[8,4,1152]{2,1,0:T(4,128)S(1)}, f32[8,4,1152]{2,1,0:T(4,128)S(1)}, u32[]{:S(2)}, u32[]{:S(2)}) collective-permute-start(f32[8,4,1152]{2,1,0:T(4,128)S(1)} %get-tuple-element.33), channel_id=1, source_target_pairs={{0,16},{32,48},{64,80},{96,112},{16,0},{48,32},{80,64},{112,96},{1... | collective-permute-start | bytes 442376 | tf_op jit(solution)/shard_map/ppermute | solution.py:501
  58.4 8.9 %collective-permute-start.3 = (f32[8,4,1152]{2,1,0:T(4,128)S(1)}, f32[8,4,1152]{2,1,0:T(4,128)S(1)}, u32[]{:S(2)}, u32[]{:S(2)}) collective-permute-start(f32[8,4,1152]{2,1,0:T(4,128)S(1)} %get-tuple-element.34), channel_id=1, source_target_pairs={{16,32},{48,64},{80,96},{32,16},{64,48},{96,80},{17,33},{49,65},{8... | collective-permute-start | bytes 442376 | tf_op jit(solution)/shard_map/ppermute | solution.py:501
  67.3 17.6 %copy-start = (f32[8,512]{1,0:T(8,128)S(1)}, f32[8,512]{1,0:T(8,128)}, u32[]{:S(2)}) copy-start(f32[8,512]{1,0:T(8,128)} %get-tuple-element.36.rank) | copy-start | bytes 49156
  67.3 17.6 %copy-start.1 = (s32[512,1]{0,1:T(1,128)S(1)}, s32[512,1]{0,1:T(1,128)}, u32[]{:S(2)}) copy-start(s32[512,1]{0,1:T(1,128)} %param.8) | copy-start | bytes 6148

commit v8 on v7

--- a/solution.py
+++ b/solution.py
@@ -363,17 +363,17 @@
         first = {}
 
         def store(r, q, i, value):
-            if i == 0:
+            if i % 2 == 0:
                 first[r, q] = value
                 return
             both = jnp.concatenate([first.pop((r, q)), value], axis=0)
-            at = pl.ds(pl.multiple_of(pair * 2 * CHUNKS, 2 * CHUNKS), 2 * CHUNKS)
+            at = pl.ds(pl.multiple_of((4 * pair + i - 1) * CHUNKS, 2 * CHUNKS), 2 * CHUNKS)
             smooth[r, at, q * 128:(q + 1) * 128] = jnp.where(inside(q), both, 0.0).astype(BF)
 
-        some_levels(one, PASSES + 1 + 2 * pair, final, store, 2)
+        some_levels(one, PASSES + 1 + 4 * pair, final, store, 4)
         return 0
 
-    lax.fori_loop(0, MIDDLE // (2 * CHUNKS), rounded, 0, unroll=2)
+    lax.fori_loop(0, MIDDLE // (4 * CHUNKS), rounded, 0)
 
 
 def diffuse(field, coef, over, root):

time: 86 us -> 85.9 us (level)
  no operation moved by 1% of the time
where the time goes in v8:
time: 85.9 us; the launch traced here: 85.7 us
  Pallas kernels  25 us (29%)
  waiting for transfers between devices  24.5 us (29%)
  starting transfers between devices  18.4 us (21%)
  blocking collectives  14.2 us (17%)
  local copies, waits for them, and re-layouts  3.5 us (4%)
    all_to_all x1, waiting for transfers between devices, body(): lax.all_to_all(packed, ('lat', 'lon'), split_axis=0, concat_axis=0, tiled...  24.5 us
    all_to_all x1, blocking collectives, body(): lax.all_to_all(values, ('lat', 'lon'), split_axis=0, concat_axis=0, tiled...  14.2 us
    ppermute x4, starting transfers between devices, swap(): return lax.ppermute(x, axis, pairs + [(j, i) for i, j in pairs])  11.2 us
    all_to_all x1, starting transfers between devices, body(): lax.all_to_all(packed, ('lat', 'lon'), split_axis=0, concat_axis=0, tiled...  7.15 us
    pallas_call x1, Pallas kernels, diffuse(): pl.pallas_call(diffuse_kernel, out_shape=(jax.ShapeDtypeStruct((RHS, MIDD...  6.09 us
    pallas_call x1, Pallas kernels, pack(): pl.pallas_call(pack_kernel, in_specs=[hbm] * 5, out_specs=(hbm, pl.BlockS...  5.88 us
    pallas_call x1, Pallas kernels, adjoint(): pl.pallas_call(adjoint_kernel, out_shape=(jax.ShapeDtypeStruct((RHS, ROWS...  4.67 us
    pallas_call x1, Pallas kernels, faces(): pl.pallas_call(faces_kernel, out_shape=(jax.ShapeDtypeStruct((2, ROWS, WI...  4.12 us
  transfers between devices with their start and end apart: 5, of which 1 were waited for; matrix products, arithmetic and copies ran while one was open for 0% of the time, Pallas kernels for 19%

profile of v8, /device:TPU:1, one launch (start us, length us, event | category | flops | bytes accessed | tf_op | source)
XLA Modules:
  0.0 85.7 jit_solution(3135619686111053758)
XLA Ops:
  0.0 2.5 %collective-permute-start = (f32[256,128]{1,0:T(8,128)}, f32[256,128]{1,0:T(8,128)S(1)}, u32[]{:S(2)}, u32[]{:S(2)}) collective-permute-start(f32[256,128]{1,0:T(8,128)} %own.1), channel_id=1, source_target_pairs={{0,1},{2,3},{4,5},{6,7},{8,9},{10,11},{12,13},{14,15},{1,0},{3,2},... | collective-permute-start | bytes 393224 | tf_op jit(solution)/shard_map/ppermute | solution.py:501
  2.5 4.7 %collective-permute-start.1 = (f32[256,128]{1,0:T(8,128)}, f32[256,128]{1,0:T(8,128)S(1)}, u32[]{:S(2)}, u32[]{:S(2)}) collective-permute-start(f32[256,128]{1,0:T(8,128)} %own.1), channel_id=1, source_target_pairs={{1,2},{3,4},{5,6},{7,8},{9,10},{11,12},{13,14},{15,0},{2,1},{4,3},... | collective-permute-start | bytes 393224 | tf_op jit(solution)/shard_map/ppermute | solution.py:501
  7.2 5.9 %pack.1 = (bf16[1024,1152]{1,0:T(8,128)(2,1)}, f32[8,512]{1,0:T(8,128)}) custom-call(bf16[512,1024]{1,0:T(8,128)(2,1)} %prints_hbm.1, bf16[4,512]{1,0:T(4,128)(2,1)} %bitcast.18, s32[1,512]{1,0:T(1,128)} %bitcast.15, s32[1,512]{1,0:T(1,128)} %bitcast.19, s32[1,512]{1,0:T(1,128)} %bitcast.20), custom_call_target="tpu_custom_call" | custom-call | flops 1073741824 | bytes 3145728 | tf_op jit(solution)/shard_map/pack/pallas_call | solution.py:139
  13.0 0.0 collective-permute-done.first
  13.1 0.0 collective-permute-done.1.second
  13.1 0.0 copy-start.2
  13.1 7.1 %all-to-all-start = ((bf16[128,8,1152]{2,1,0:T(8,128)(2,1)}), bf16[128,8,1152]{2,1,0:T(8,128)(2,1)S(1)}, u32[]{:S(2)}, u32[]{:S(2)}) async-start(bf16[128,8,1152]{2,1,0:T(8,128)(2,1)} %bitcast.17), calls=%async_computation | async-start | bytes 4718592 | tf_op jit(solution)/shard_map/all_to_all | solution.py:511
  20.2 0.0 copy-done.2
  20.2 4.1 %faces.1 = (f32[2,256,1152]{2,1,0:T(8,128)S(1)}, f32[256,1152]{1,0:T(8,128)S(1)}, f32[256,1152]{1,0:T(8,128)S(1)}, f32[8,8,1152]{2,1,0:T(8,128)S(1)}) custom-call(f32[256,128]{1,0:T(8,128)S(1)} %copy-done.2, f32[256,128]{1,0:T(8,128)S(1)} %collective-permute-done.first, f32[256,128]{1,0:T(8,128)S(1)} %collective-permute-done.1.second), custom_call_target="tpu_custom_call" | custom-call | flops 1073741824 | bytes 6291456 | tf_op jit(solution)/shard_map/faces/pallas_call | solution.py:208
  24.4 0.0 copy-start.3
  24.4 1.4 %copy-done.3 = f32[2,256,1152]{2,1,0:T(8,128)} copy-done((f32[2,256,1152]{2,1,0:T(8,128)}, f32[2,256,1152]{2,1,0:T(8,128)S(1)}, u32[]{:S(2)}) %copy-start.3) | copy-done | bytes 2359320
  25.8 1.0 %copy-done.5 = f32[256,1152]{1,0:T(8,128)} copy-done((f32[256,1152]{1,0:T(8,128)}, f32[256,1152]{1,0:T(8,128)S(1)}, u32[]{:S(2)}) %copy-start.5) | copy-done | bytes 1179672
  26.8 1.0 %copy-done.7 = f32[256,1152]{1,0:T(8,128)} copy-done((f32[256,1152]{1,0:T(8,128)}, f32[256,1152]{1,0:T(8,128)S(1)}, u32[]{:S(2)}) %copy-start.7) | copy-done | bytes 1179672
  27.9 24.5 %all-to-all-done = bf16[128,8,1152]{2,1,0:T(8,128)(2,1)S(1)} async-done(((bf16[128,8,1152]{2,1,0:T(8,128)(2,1)}), bf16[128,8,1152]{2,1,0:T(8,128)(2,1)S(1)}, u32[]{:S(2)}, u32[]{:S(2)}) %all-to-all-start) | async-done | bytes 2359328 | tf_op jit(solution)/shard_map/all_to_all | solution.py:511
  52.4 4.7 %adjoint.1 = (f32[4,256,1152]{2,1,0:T(8,128)S(1)}, f32[8,8,1152]{2,1,0:T(8,128)S(1)}, f32[8,4,1152]{2,1,0:T(4,128)S(1)}, f32[8,4,1152]{2,1,0:T(4,128)S(1)}, f32[16,1024]{1,0:T(8,128)S(1)}) custom-call(bf16[1024,1152]{1,0:T(8,128)(2,1)S(1)} %bitcast.11, f32[8,8,1152]{2,1,0:T(8,128)S(1)} %get-tuple-element.25.roots), custom_call_target="tpu_custom_call" | custom-call | flops 5368709120 | bytes 8388608 | tf_op jit(solution)/shard_map/adjoint/pallas_call | solution.py:274
  57.0 1.3 %collective-permute-start.2 = (f32[8,4,1152]{2,1,0:T(4,128)S(1)}, f32[8,4,1152]{2,1,0:T(4,128)S(1)}, u32[]{:S(2)}, u32[]{:S(2)}) collective-permute-start(f32[8,4,1152]{2,1,0:T(4,128)S(1)} %get-tuple-element.33), channel_id=1, source_target_pairs={{0,16},{32,48},{64,80},{96,112},{16,0},{48,32},{80,64},{112,96},{1... | collective-permute-start | bytes 442376 | tf_op jit(solution)/shard_map/ppermute | solution.py:501
  58.4 2.7 %collective-permute-start.3 = (f32[8,4,1152]{2,1,0:T(4,128)S(1)}, f32[8,4,1152]{2,1,0:T(4,128)S(1)}, u32[]{:S(2)}, u32[]{:S(2)}) collective-permute-start(f32[8,4,1152]{2,1,0:T(4,128)S(1)} %get-tuple-element.34), channel_id=1, source_target_pairs={{16,32},{48,64},{80,96},{32,16},{64,48},{96,80},{17,33},{49,65},{8... | collective-permute-start | bytes 442376 | tf_op jit(solution)/shard_map/ppermute | solution.py:501
  61.2 6.1 %diffuse.1 = (bf16[4,192,1152]{2,1,0:T(8,128)(2,1)S(1)}, f32[4,64,1152]{2,1,0:T(8,128)S(1)}) custom-call(f32[4,256,1152]{2,1,0:T(8,128)S(1)} %get-tuple-element.26.field, f32[2,256,1152]{2,1,0:T(8,128)S(1)} %copy-done.4, f32[256,1152]{1,0:T(8,128)S(1)} %copy-done.6, f32[256,1152]{1,0:T(8,128)S(1)} %copy-done.8), custom_call_target="tpu_custom_call" | custom-call | flops 6442450944 | bytes 8388608 | tf_op jit(solution)/shard_map/diffuse/pallas_call | solution.py:380
  67.2 0.0 collective-permute-done.2.inner
  67.3 0.0 collective-permute-done.3.beyond
  67.3 0.0 copy-start.1
  67.3 3.4 %finish.1 = f32[128,128]{1,0:T(8,128)S(1)} custom-call(bf16[4,192,1152]{2,1,0:T(8,128)(2,1)S(1)} %get-tuple-element.30.smooth, f32[4,64,1152]{2,1,0:T(8,128)S(1)} %get-tuple-element.31.outer, f32[8,8,1152]{2,1,0:T(8,128)S(1)} %get-tuple-element.32.rim, f32[8,8,1152]{2,1,0:T(8,128)S(1)} %get-tuple-element.25.roots, ...), custom_call_target="tpu_custom_call" | custom-call | flops 3221225472 | bytes 10485760 | tf_op jit(solution)/shard_map/finish/pallas_call | solution.py:466
  70.7 14.2 %all_to_all.22 = f32[128,1,128]{2,1,0:T(1,128)S(1)} all-to-all(f32[128,1,128]{2,1,0:T(1,128)S(1)} %bitcast.14), channel_id=1, replica_groups=mesh['lat'=8,'lon'=16] {'lat','lon'}, dimensions={0} | all-to-all | bytes 131072 | tf_op jit(solution)/shard_map/all_to_all | solution.py:517
  84.9 0.8 unpack.1
  (11 shorter events, 0.0 us)
Async XLA Ops:
  0.0 13.1 %collective-permute-start = (f32[256,128]{1,0:T(8,128)}, f32[256,128]{1,0:T(8,128)S(1)}, u32[]{:S(2)}, u32[]{:S(2)}) collective-permute-start(f32[256,128]{1,0:T(8,128)} %own.1), channel_id=1, source_target_pairs={{0,1},{2,3},{4,5},{6,7},{8,9},{10,11},{12,13},{14,15},{1,0},{3,2},... | collective-permute-start | bytes 393224 | tf_op jit(solution)/shard_map/ppermute | solution.py:501
  2.5 10.6 %collective-permute-start.1 = (f32[256,128]{1,0:T(8,128)}, f32[256,128]{1,0:T(8,128)S(1)}, u32[]{:S(2)}, u32[]{:S(2)}) collective-permute-start(f32[256,128]{1,0:T(8,128)} %own.1), channel_id=1, source_target_pairs={{1,2},{3,4},{5,6},{7,8},{9,10},{11,12},{13,14},{15,0},{2,1},{4,3},... | collective-permute-start | bytes 393224 | tf_op jit(solution)/shard_map/ppermute | solution.py:501
  13.1 7.2 %copy-start.2 = (f32[256,128]{1,0:T(8,128)S(1)}, f32[256,128]{1,0:T(8,128)}, u32[]{:S(2)}) copy-start(f32[256,128]{1,0:T(8,128)} %own.1) | copy-start | bytes 393220
  13.1 39.3 %all-to-all-start = ((bf16[128,8,1152]{2,1,0:T(8,128)(2,1)}), bf16[128,8,1152]{2,1,0:T(8,128)(2,1)S(1)}, u32[]{:S(2)}, u32[]{:S(2)}) async-start(bf16[128,8,1152]{2,1,0:T(8,128)(2,1)} %bitcast.17), calls=%async_computation | async-start | bytes 4718592 | tf_op jit(solution)/shard_map/all_to_all | solution.py:511
  24.4 1.4 %copy-start.3 = (f32[2,256,1152]{2,1,0:T(8,128)}, f32[2,256,1152]{2,1,0:T(8,128)S(1)}, u32[]{:S(2)}) copy-start(f32[2,256,1152]{2,1,0:T(8,128)S(1)} %get-tuple-element.27.coef) | copy-start | bytes 7077892
  25.8 1.0 %copy-start.5 = (f32[256,1152]{1,0:T(8,128)}, f32[256,1152]{1,0:T(8,128)S(1)}, u32[]{:S(2)}) copy-start(f32[256,1152]{1,0:T(8,128)S(1)} %get-tuple-element.28.over) | copy-start | bytes 3538948
  26.8 1.0 %copy-start.7 = (f32[256,1152]{1,0:T(8,128)}, f32[256,1152]{1,0:T(8,128)S(1)}, u32[]{:S(2)}) copy-start(f32[256,1152]{1,0:T(8,128)S(1)} %get-tuple-element.29.root) | copy-start | bytes 3538948
  52.4 8.8 %copy-start.4 = (f32[2,256,1152]{2,1,0:T(8,128)S(1)}, f32[2,256,1152]{2,1,0:T(8,128)}, u32[]{:S(2)}) copy-start(f32[2,256,1152]{2,1,0:T(8,128)} %copy-done.3) | copy-start | bytes 7077892
  52.4 8.8 %copy-start.6 = (f32[256,1152]{1,0:T(8,128)S(1)}, f32[256,1152]{1,0:T(8,128)}, u32[]{:S(2)}) copy-start(f32[256,1152]{1,0:T(8,128)} %copy-done.5) | copy-start | bytes 3538948
  52.4 8.8 %copy-start.8 = (f32[256,1152]{1,0:T(8,128)S(1)}, f32[256,1152]{1,0:T(8,128)}, u32[]{:S(2)}) copy-start(f32[256,1152]{1,0:T(8,128)} %copy-done.7) | copy-start | bytes 3538948
  57.0 10.2 %collective-permute-start.2 = (f32[8,4,1152]{2,1,0:T(4,128)S(1)}, f32[8,4,1152]{2,1,0:T(4,128)S(1)}, u32[]{:S(2)}, u32[]{:S(2)}) collective-permute-start(f32[8,4,1152]{2,1,0:T(4,128)S(1)} %get-tuple-element.33), channel_id=1, source_target_pairs={{0,16},{32,48},{64,80},{96,112},{16,0},{48,32},{80,64},{112,96},{1... | collective-permute-start | bytes 442376 | tf_op jit(solution)/shard_map/ppermute | solution.py:501
  58.4 8.9 %collective-permute-start.3 = (f32[8,4,1152]{2,1,0:T(4,128)S(1)}, f32[8,4,1152]{2,1,0:T(4,128)S(1)}, u32[]{:S(2)}, u32[]{:S(2)}) collective-permute-start(f32[8,4,1152]{2,1,0:T(4,128)S(1)} %get-tuple-element.34), channel_id=1, source_target_pairs={{16,32},{48,64},{80,96},{32,16},{64,48},{96,80},{17,33},{49,65},{8... | collective-permute-start | bytes 442376 | tf_op jit(solution)/shard_map/ppermute | solution.py:501
  67.3 17.6 %copy-start = (f32[8,512]{1,0:T(8,128)S(1)}, f32[8,512]{1,0:T(8,128)}, u32[]{:S(2)}) copy-start(f32[8,512]{1,0:T(8,128)} %get-tuple-element.36.rank) | copy-start | bytes 49156
  67.3 17.6 %copy-start.1 = (s32[512,1]{0,1:T(1,128)S(1)}, s32[512,1]{0,1:T(1,128)}, u32[]{:S(2)}) copy-start(s32[512,1]{0,1:T(1,128)} %param.8) | copy-start | bytes 6148
